TPU v7x, 256 devices: a whole 4x4x8 slice. The times are simulated.
256 devices in a mesh: res: 64 (over y, z, x_hi), seq: 4 (over x_lo, core).
Axes of the slice: x: 4 (x_hi: 2, x_lo: 2; x = x_hi * 2 + x_lo), y: 4, z: 8, core: 2. Of those that a mesh axis runs over, the one named last changes fastest.
Arguments:
- alignment_token_classes: int32 [256, 512], P('seq', 'res'), may hold values from 0 to 22
- deletions: int32 [256, 512], P('seq', 'res'), may hold values from 0 to 31
- alignment_mask: int32 [256, 512], P('seq', 'res'), may hold values from 0 to 1, as said below
- homolog_stack_values: bfloat16 [256, 512, 256], P('seq', 'res'), may hold values from -6 to 6
- letter_lookup_coefficients: float32 [23, 256], replicated, may hold values from -6 to 6
- gap_lookup_coefficients: float32 [2, 256], replicated, may hold values from -6 to 6
- standardize_gain: float32 [256], replicated, may hold values from 0.1 to 1.9
- standardize_offset: float32 [256], replicated, may hold values from -3 to 3
- first_factor_map: bfloat16 [256, 32], replicated, may hold values from -0.375 to 0.375
- left_bias_vector: float32 [32], replicated, may hold values from -4 to 4
- second_factor_map: bfloat16 [256, 32], replicated, may hold values from -0.375 to 0.375
- right_bias_vector: float32 [32], replicated, may hold values from -4 to 4
- output_weight_matrix: bfloat16 [1024, 128], replicated, may hold values from -1.5 to 1.5
- cotangent: bfloat16 [512, 512, 128], P('res'), may hold values from -0.08984375 to 0.08984375
Outputs:
- pair_update: bfloat16 [512, 512, 128], P('res', 'seq')
- grad_out_weight: float32 [1024, 128], replicated
- embedding_gradient: float32 [23, 256], replicated
Inputs may be any that keep to these rules, and one draw needn't show every extreme that they name: Row 0 of alignment_mask is 1 at every residue; the other entries are 0 or 1.
All inputs are finite; a program needn't handle non-finite values.
Results may differ from a plain program's by a relative error of at most 0.0057.
Values may be sent and summed in bfloat16 or wider, within the bound.
A program may use at most 128 MiB of HBM per device.

v0:
```python
import math

import jax
import jax.numpy as jnp
from jax import lax
from jax.sharding import PartitionSpec as P

EPSILON = 1e-05
TOP_PRECISION = lax.Precision.HIGHEST


def fold_outer(lead_rows, other_rows, channels, col_count):
    product = lax.dot_general(
        lead_rows, other_rows, (((0,), (0,)), ((), ())), preferred_element_type=jnp.float32
    )
    row_count = lead_rows.shape[1] // channels
    return (
        product.reshape(row_count, channels, col_count, channels)
        .transpose(0, 2, 1, 3)
        .reshape(row_count * col_count, channels * channels)
    )


def body(
    alignment_token_classes,
    deletions,
    alignment_mask,
    homolog_stack_values,
    letter_lookup_coefficients,
    gap_lookup_coefficients,
    standardize_gain,
    standardize_offset,
    first_factor_map,
    left_bias_vector,
    second_factor_map,
    right_bias_vector,
    output_weight_matrix,
    cotangent,
):
    sequence_block_rows, residue_block_rows = alignment_token_classes.shape
    token_vocabulary, input_features = letter_lookup_coefficients.shape
    channels = first_factor_map.shape[1]
    pair_width = output_weight_matrix.shape[1]
    residues = cotangent.shape[1]
    groups = lax.axis_size("seq")
    quarter = residues // groups
    token_indicator = (
        alignment_token_classes.reshape(-1, 1)
        == jnp.arange(token_vocabulary, dtype=jnp.int32)[None, :]
    ).astype(jnp.float32)
    counted = deletions.reshape(-1, 1).astype(jnp.float32)
    marked_deletion = (counted > 0).astype(jnp.float32)
    attenuated = 2.0 / math.pi * jnp.arctan(counted / 3.0)
    hidden_activations = (
        homolog_stack_values.reshape(-1, input_features).astype(jnp.float32)
        + jnp.dot(token_indicator, letter_lookup_coefficients, precision=TOP_PRECISION)
        + marked_deletion * gap_lookup_coefficients[0]
        + attenuated * gap_lookup_coefficients[1]
    )
    average = jnp.mean(hidden_activations, axis=-1, keepdims=True)
    mean_removed = hidden_activations - average
    variance = jnp.mean(mean_removed * mean_removed, axis=-1, keepdims=True)
    reciprocal_spread = lax.rsqrt(variance + EPSILON)
    standardized_values = mean_removed * reciprocal_spread
    normed = (standardized_values * standardize_gain + standardize_offset).astype(jnp.bfloat16)
    mask_decimal = alignment_mask.astype(jnp.float32)
    mask_column = mask_decimal.reshape(-1, 1)
    left_rows = (
        (
            mask_column
            * (
                jnp.dot(normed, first_factor_map, preferred_element_type=jnp.float32)
                + left_bias_vector
            )
        )
        .astype(jnp.bfloat16)
        .reshape(sequence_block_rows, residue_block_rows * channels)
    )
    right_rows = (
        (
            mask_column
            * (
                jnp.dot(normed, second_factor_map, preferred_element_type=jnp.float32)
                + right_bias_vector
            )
        )
        .astype(jnp.bfloat16)
        .reshape(sequence_block_rows, residue_block_rows * channels)
    )
    right_all, mask_all = (
        lax.all_gather(right_rows, "res", axis=1, tiled=True),
        lax.all_gather(alignment_mask.astype(jnp.bfloat16), "res", axis=1, tiled=True),
    )
    counts = lax.psum(
        jnp.dot(mask_decimal.T, mask_all.astype(jnp.float32), precision=TOP_PRECISION), "seq"
    )
    scaled = (cotangent.astype(jnp.float32) / counts[:, :, None]).astype(jnp.bfloat16)
    counts_quarter = lax.dynamic_slice_in_dim(counts, lax.axis_index("seq") * quarter, quarter, 1)
    wide_weight = output_weight_matrix.astype(jnp.float32)
    col_span = math.gcd(residues, 128)

    def backward_cols(position, carried):
        pair_acc, grad_weight, left_grad, grad_right = carried
        first_col = position * col_span
        right_part = lax.dynamic_slice_in_dim(
            right_all, first_col * channels, col_span * channels, 1
        )
        folded = fold_outer(left_rows, right_part, channels, col_span)
        pair_part = jnp.dot(folded, wide_weight, precision=TOP_PRECISION).reshape(
            residue_block_rows, col_span, pair_width
        )
        pair_acc = lax.dynamic_update_slice_in_dim(pair_acc, pair_part, first_col, 1)
        grad_part = lax.dynamic_slice_in_dim(scaled, first_col, col_span, 1).reshape(
            residue_block_rows * col_span, pair_width
        )
        grad_weight = grad_weight + lax.dot_general(
            folded, grad_part.astype(jnp.float32), (((0,), (0,)), ((), ())), precision=TOP_PRECISION
        )
        grad_outer = jnp.dot(
            grad_part, output_weight_matrix.T, preferred_element_type=jnp.float32
        ).astype(jnp.bfloat16)
        grad_outer = (
            grad_outer.reshape(residue_block_rows, col_span, channels, channels)
            .transpose(0, 2, 1, 3)
            .reshape(residue_block_rows * channels, col_span * channels)
        )
        left_grad = left_grad + lax.dot_general(
            grad_outer, right_part, (((1,), (1,)), ((), ())), preferred_element_type=jnp.float32
        )
        right_part_grad = jnp.dot(left_rows, grad_outer, preferred_element_type=jnp.float32)
        grad_right = lax.dynamic_update_slice_in_dim(
            grad_right, right_part_grad, first_col * channels, 1
        )
        return (pair_acc, grad_weight, left_grad, grad_right)

    pair_start = jnp.zeros((residue_block_rows, residues, pair_width), jnp.float32)
    initial = (
        pair_start,
        jnp.zeros((channels * channels, pair_width), jnp.float32),
        jnp.zeros((residue_block_rows * channels, sequence_block_rows), jnp.float32),
        jnp.zeros((sequence_block_rows, residues * channels), jnp.float32),
    )
    pair_acc, grad_weight, left_grad, grad_right = lax.fori_loop(
        0, residues // col_span, backward_cols, initial
    )
    pair_sum = lax.psum_scatter(pair_acc, "seq", scatter_dimension=1, tiled=True)
    pair_update = (pair_sum / counts_quarter[:, :, None]).astype(jnp.bfloat16)
    right_sum = lax.psum_scatter(grad_right, "res", scatter_dimension=1, tiled=True)
    mask_cube = mask_decimal[:, :, None]
    grad_left = (
        (mask_cube * left_grad.T.reshape(sequence_block_rows, residue_block_rows, channels))
        .astype(jnp.bfloat16)
        .reshape(-1, channels)
    )
    grad_rhs = (
        (mask_cube * right_sum.reshape(sequence_block_rows, residue_block_rows, channels))
        .astype(jnp.bfloat16)
        .reshape(-1, channels)
    )
    grad_normed = jnp.dot(
        grad_left, first_factor_map.T, preferred_element_type=jnp.float32
    ) + jnp.dot(grad_rhs, second_factor_map.T, preferred_element_type=jnp.float32)
    gained = grad_normed * standardize_gain
    gradient_activations = reciprocal_spread * (
        gained
        - jnp.mean(gained, axis=-1, keepdims=True)
        - standardized_values * jnp.mean(gained * standardized_values, axis=-1, keepdims=True)
    )
    table_part = lax.dot_general(
        token_indicator, gradient_activations, (((0,), (0,)), ((), ())), precision=TOP_PRECISION
    )
    weight_sum, table_sum = lax.psum((grad_weight, table_part), ("res", "seq"))
    return (pair_update, weight_sum, table_sum)


def solution(mesh):
    in_specs = (
        P("seq", "res"),
        P("seq", "res"),
        P("seq", "res"),
        P("seq", "res", None),
        P(),
        P(),
        P(),
        P(),
        P(),
        P(),
        P(),
        P(),
        P(),
        P("res", None, None),
    )
    out_specs = (P("res", "seq", None), P(), P())
    return jax.shard_map(body, mesh=mesh, in_specs=in_specs, out_specs=out_specs, check_vma=False)
```

profile of v0, /device:TPU:1, one launch (start us, length us, event | category | flops | bytes accessed | tf_op | source)
XLA Modules:
  0.0 1210.8 jit_solution(4777056734356300582)
XLA Ops:
  15.7 158.3 %all_gather.7 = bf16[64,512]{0,1:T(8,128)(2,1)S(1)} all-gather(bf16[64,8]{0,1:T(8,128)(2,1)S(1)} %get-tuple-element.307), channel_id=1, replica_groups=mesh['res'=64,'seq'=4] {'res'}, dimensions={1}, use_global_device_ids=true | all-gather | bytes 66560 | tf_op jit(solution)/shard_map/all_gather | solution.py:92
  174.1 36.7 %psum.21 = f32[8,512]{1,0:T(8,128)S(1)} all-reduce(f32[8,512]{1,0:T(8,128)S(1)} %fusion.36), channel_id=1, replica_groups=mesh['res'=64,'seq'=4] {'seq'}, use_global_device_ids=true, to_apply=%region_2.0 | all-reduce | flops 4096 | bytes 32768 | tf_op jit(solution)/shard_map/psum | solution.py:94
  216.3 339.8 %while.22 = (s32[]{:T(128)}, f32[8,512,128]{2,1,0:T(8,128)}, f32[1024,128]{1,0:T(8,128)S(1)}, f32[256,64]{0,1:T(8,128)S(1)}, f32[64,16384]{1,0:T(8,128)}, /*inde...) while((s32[]{:T(128)}, f32[8,512,128]{2,1,0:T(8,128)}, ...), condition=%wide.region_4.0_spmd.clone, body=%wide.region_3.0_spmd.clone.sunk | while | flops 3893657600 | bytes 74907928 | solution.py:143
  225.6 10.8 reshape.165
  236.4 11.4 copy.52
  258.5 11.5 copy.53
  287.2 10.7 reshape.166
  310.6 10.8 reshape.165
  321.3 11.4 copy.52
  343.4 11.5 copy.53
  372.2 10.7 reshape.166
  395.5 10.8 reshape.165
  406.3 11.4 copy.52
  417.7 9.7 convolution_dynamic-update-slice_fusion.2
  428.4 11.5 copy.53
  457.2 10.7 reshape.166
  480.5 10.8 reshape.165
  491.3 11.4 copy.52
  513.4 11.5 copy.53
  542.1 10.7 reshape.166
  558.2 21.7 %reduce-scatter.3.cloned.1.call-done = f32[8,128,128]{2,1,0:T(8,128)} async-done(((f32[8,512,128]{2,1,0:T(8,128)}), f32[8,128,128]{2,1,0:T(8,128)}) %reduce-scatter.3.cloned.1.call-update) | async-done | bytes 524304 | tf_op jit(solution)/shard_map/reduce_scatter | solution.py:146
  581.9 320.9 %reduce-scatter.5.cloned.1.call-done = f32[64,256]{1,0:T(8,128)} async-done(((f32[64,16384]{1,0:T(8,128)}), f32[64,256]{1,0:T(8,128)}) %reduce-scatter.5.cloned.1.call-update) | async-done | bytes 65552 | tf_op jit(solution)/shard_map/reduce_scatter | solution.py:148
  904.7 123.0 %psum.23 = f32[23,256]{1,0:T(8,128)} all-reduce(f32[23,256]{1,0:T(8,128)S(1)} %fusion.19), channel_id=1, replica_groups=mesh['res'=64,'seq'=4] {'res','seq'}, use_global_device_ids=true, to_apply=%region_10.0 | all-reduce | flops 5888 | bytes 47104 | tf_op jit(solution)/shard_map/psum | solution.py:172
  1027.7 174.7 %all-reduce.2.cloned.1.call-done = f32[1024,128]{1,0:T(8,128)} async-done(((f32[1024,128]{1,0:T(8,128)}), f32[1024,128]{1,0:T(8,128)}) %all-reduce.2.cloned.1.call-update) | async-done | bytes 524304 | tf_op jit(solution)/shard_map/psum | solution.py:172
  (145 shorter events, 174.2 us)
Async XLA Ops:
  7.2 4.8 copy-start
  7.2 5.5 copy-start.19
  7.2 5.7 copy-start.22
  7.2 5.7 copy-start.20
  7.2 205.2 %all-gather.2.cloned.1.call-start = ((), (), s32[]{:S(2)}) async-start(), calls=%async_computation.2 | async-start | bytes 2129920 | tf_op jit(solution)/shard_map/all_gather | solution.py:91
  9.8 3.3 copy-start.7
  9.8 3.3 copy-start.23
  10.8 3.4 copy-start.9
  10.8 3.4 copy-start.24
  12.6 199.9 %copy-start.3 = (f32[512,256]{0,1:T(8,128)}, f32[512,256]{0,1:T(8,128)S(1)}, u32[]{:S(2)}) copy-start(f32[512,256]{0,1:T(8,128)S(1)} %get-tuple-element.312) | copy-start | bytes 1572868
  12.6 198.3 %copy-start.5 = (bf16[8,512,128]{2,1,0:T(8,128)(2,1)S(1)}, bf16[8,512,128]{2,1,0:T(8,128)(2,1)}, u32[]{:S(2)}) copy-start(bf16[8,512,128]{2,1,0:T(8,128)(2,1)} %param.29) | copy-start | bytes 3145732
  12.6 161.4 %copy-start.11 = (f32[512]{0:T(512)}, f32[512]{0:T(512)S(1)}, u32[]{:S(2)}) copy-start(f32[512]{0:T(512)S(1)} %broadcast_multiply_fusion.2) | copy-start | bytes 6148
  12.7 161.2 %copy-start.15 = (f32[512]{0:T(512)}, f32[512]{0:T(512)S(1)}, u32[]{:S(2)}) copy-start(f32[512]{0:T(512)S(1)} %add_rsqrt_fusion) | copy-start | bytes 6148
  12.9 161.0 %copy-start.13 = (f32[512]{0:T(512)}, f32[512]{0:T(512)S(1)}, u32[]{:S(2)}) copy-start(f32[512]{0:T(512)S(1)} %mul.140) | copy-start | bytes 6148
  14.2 565.8 %reduce-scatter.3.cloned.1.call-start = ((), (), s32[]{:S(2)}) async-start(), calls=%async_computation.3 | async-start | bytes 2621440 | tf_op jit(solution)/shard_map/reduce_scatter | solution.py:146
  556.1 346.7 %reduce-scatter.5.cloned.1.call-start = ((), (), s32[]{:S(2)}) async-start(), calls=%async_computation.5 | async-start | bytes 4259840 | tf_op jit(solution)/shard_map/reduce_scatter | solution.py:148
  556.9 347.0 %copy-start.4 = (f32[512,256]{0,1:T(8,128)S(1)}, f32[512,256]{0,1:T(8,128)}, u32[]{:S(2)}) copy-start(f32[512,256]{0,1:T(8,128)} %copy-done.3) | copy-start | bytes 1572868
  556.9 347.0 %copy-start.8 = (bf16[256,32]{0,1:T(8,128)(2,1)S(1)}, bf16[256,32]{0,1:T(8,128)(2,1)}, u32[]{:S(2)}) copy-start(bf16[256,32]{0,1:T(8,128)(2,1)} %param.26) | copy-start | bytes 49156
  556.9 347.0 %copy-start.12 = (f32[512]{0:T(512)S(1)}, f32[512]{0:T(512)}, u32[]{:S(2)}) copy-start(f32[512]{0:T(512)} %copy-done.11) | copy-start | bytes 6148
  556.9 347.0 %copy-start.16 = (f32[512]{0:T(512)S(1)}, f32[512]{0:T(512)}, u32[]{:S(2)}) copy-start(f32[512]{0:T(512)} %copy-done.15) | copy-start | bytes 6148
  556.9 347.0 %copy-start.21 = (f32[256]{0:T(256)S(1)}, f32[256]{0:T(256)}, u32[]{:S(2)}) copy-start(f32[256]{0:T(256)} %param.22) | copy-start | bytes 3076
  556.9 645.5 %all-reduce.2.cloned.1.call-start = ((), (), s32[]{:S(2)}) async-start(), calls=%async_computation.4 | async-start | bytes 1048576 | tf_op jit(solution)/shard_map/psum | solution.py:172
  557.9 346.3 %copy-start.18 = (s32[512]{0:T(512)S(1)}, s32[512]{0:T(512)}, u32[]{:S(2)}) copy-start(s32[512]{0:T(512)} %copy-done.17) | copy-start | bytes 6148
  902.8 301.5 %copy-start.1 = (f32[23,256]{1,0:T(8,128)S(1)}, f32[23,256]{1,0:T(8,128)}, u32[]{:S(2)}) copy-start(f32[23,256]{1,0:T(8,128)} %param.20) | copy-start | bytes 70660
  (5 other events, 8.6 us)
Sparse Core Ops, SparseCore 0:
  14.3 111.7 all-gather.1
  556.2 23.7 reduce-scatter.2
  582.6 320.0 reduce-scatter.4
  908.7 293.7 all-reduce.1
where the time goes:
time: 1220 us; the launch traced here: 1210 us
  waiting for transfers between devices  518 us (42%)
  blocking collectives  318 us (26%)
  local copies, waits for them, and re-layouts  258 us (21%)
  matrix products  95.1 us (8%)
  between operations  14.2 us (1%)
    reduce_scatter x1, waiting for transfers between devices, body(): lax.psum_scatter(grad_right, 'res', scatter_dimension=1, tiled=True)  321 us
    psum x1, waiting for transfers between devices, body(): weight_sum, table_sum = lax.psum((grad_weight, table_part), ('res', 'seq'))  175 us
    all_gather x1, blocking collectives, body(): lax.all_gather(alignment_mask.astype(jnp.bfloat16), 'res', axis=1, tiled=...  158 us
    psum x1, blocking collectives, body(): weight_sum, table_sum = lax.psum((grad_weight, table_part), ('res', 'seq'))  123 us
    transpose x8, local copies, waits for them, and re-layouts, fold_outer(): return product.reshape(row_count, channels, col_count, channels).transpos...  91.6 us
    reshape x4, local copies, waits for them, and re-layouts, fold_outer(): product.reshape(row_count, channels, col_count, channels)  43 us
    reshape x4, local copies, waits for them, and re-layouts, backward_cols(): grad_outer = grad_outer.reshape(residue_block_rows, col_span, channels, c...  42.6 us
    dot_general x4, matrix products, backward_cols(): jnp.dot(folded, wide_weight, precision=TOP_PRECISION)  38.7 us
  transfers between devices with their start and end apart: 4, of which 3 were waited for; matrix products, arithmetic and copies ran while one was open for 1% of the time, Pallas kernels for 0%

commit v1 on v0

v1 whole, which is shorter than its diff:
```python
import math

import jax
import jax.numpy as jnp
from jax import lax
from jax.experimental import pallas as pl
from jax.experimental.pallas import tpu as pltpu
from jax.sharding import PartitionSpec as P

EPSILON = 1e-05
TOP_PRECISION = lax.Precision.HIGHEST
MESH = pl.DeviceIdType.MESH
F32 = jnp.float32
BF16 = jnp.bfloat16

ROWS = 64
BLOCK = 80
WIDE = 256
TILES = 6


def place():
    res = lax.axis_index("res")
    q = lax.axis_index("seq")
    return lax.div(res, 16), lax.rem(lax.div(res, 2), 8), lax.rem(res, 2), q


def row_peer(spot, n):
    _, z, x, _ = spot
    return (lax.div(n, 4) * 16 + z * 2 + x, lax.rem(n, 4))


def depth_peer(spot, n):
    y, _, _, q = spot
    return (y * 16 + n, q)


def right_user(spot, n):
    y, z, _, _ = spot
    return (lax.div(z, 2) * 16 + n, y)


def right_owner(spot, n):
    y, _, _, q = spot
    return (q * 16 + y * 4 + lax.div(n, 4), lax.rem(n, 4))


def repeat(count, step):
    lax.fori_loop(0, count, lambda n, carried: (step(n), carried)[1], 0)


def signal(barrier, target):
    pl.semaphore_signal(barrier, inc=1, device_id=target, device_id_type=MESH)


def remote(src, dst, send, recv, target):
    return pltpu.make_async_remote_copy(
        src_ref=src, dst_ref=dst, send_sem=send, recv_sem=recv, device_id=target, device_id_type=MESH
    )


def lanes(shape):
    return lax.broadcasted_iota(jnp.int32, shape, len(shape) - 1)


def swap(parts, stride):
    lane = lanes(parts[0].shape)
    low = lax.rem(lax.div(lane, stride), 2) == 0
    high = lax.rem(lax.div(lane, 2 * stride), 2) == 0

    def pair(first, second, step, keep):
        return (
            jnp.where(keep, first, pltpu.roll(second, step, 1)),
            jnp.where(keep, pltpu.roll(first, 128 - step, 1), second),
        )

    a, b = pair(parts[0], parts[1], stride, low)
    c, d = pair(parts[2], parts[3], stride, low)
    a, c = pair(a, c, 2 * stride, high)
    b, d = pair(b, d, 2 * stride, high)
    return [a, b, c, d]


def dot(first, second):
    return jnp.dot(first, second, preferred_element_type=F32)


def dot_nt(first, second):
    return lax.dot_general(first, second, (((1,), (1,)), ((), ())), preferred_element_type=F32)


def gather_kernel(
    token, deletion, mask, mask_rows, stack, table, gain, offset, maps, bias, cotangent,
    left_all, right_all, cot_all, white, spread,
    left_own, right_own, left_send, left_recv, right_send, right_recv, cot_send, cot_recv,
):
    spot = place()
    y, z, x, q = spot
    mine = y * 4 + q
    self_user = jnp.logical_and(lax.div(z, 2) == y, q == y)
    slot = lax.rem(z, 2) * 2 + x
    my_res = y * 16 + z * 2 + x

    def is_me(target):
        return jnp.logical_and(target[0] == my_res, target[1] == q)

    barrier = pltpu.get_barrier_semaphore()

    def greet(n):
        @pl.when(n != mine)
        def _():
            signal(barrier, row_peer(spot, n))

        owner = right_owner(spot, n)

        @pl.when(jnp.logical_not(is_me(owner)))
        def _():
            signal(barrier, owner)

    repeat(16, greet)

    lane = lanes((ROWS, 128))
    wide_lane = lanes((ROWS, WIDE))
    left_tiles = [jnp.zeros((ROWS, 128), F32), jnp.zeros((ROWS, 128), F32)]
    right_part = jnp.zeros((ROWS, WIDE), F32)
    for i in range(8):
        hot = jnp.logical_or(lane == token[:, i : i + 1], lane == deletion[:, i : i + 1] + 32).astype(F32)
        hidden = stack[i].astype(F32) + jnp.dot(
            hot, table[...], precision=TOP_PRECISION, preferred_element_type=F32
        )
        centered = hidden - jnp.mean(hidden, axis=-1, keepdims=True)
        variance = jnp.mean(centered * centered, axis=-1, keepdims=True)
        scale = lax.rsqrt(variance + EPSILON)
        whitened = centered * scale
        white[i] = whitened
        spread[i] = jnp.broadcast_to(scale, (ROWS, 128))
        normed = (whitened * gain[...] + offset[...]).astype(BF16)
        rows = mask[:, i : i + 1] * (dot(normed, maps[...]) + bias[...])
        left_tiles[i // 4] = jnp.where(lax.div(lane, 32) == i % 4, rows[:, :128], left_tiles[i // 4])
        right_part = jnp.where(lax.rem(wide_lane, 8) == i, rows[:, 128:], right_part)
    left_own[:ROWS, :128] = left_tiles[0].astype(BF16)
    left_own[:ROWS, 128:] = left_tiles[1].astype(BF16)
    left_own[ROWS:, :] = mask_rows[...]
    right_own[:ROWS, :] = right_part.astype(BF16)
    right_own[ROWS:, :] = mask_rows[...]

    pl.semaphore_wait(barrier, jnp.where(self_user, 30, 31))

    def left_slot(at_y, at_q):
        return left_all.at[at_q, :, pl.ds(pl.multiple_of(at_y * WIDE, WIDE), WIDE)]

    def left_copy(n):
        return remote(left_own, left_slot(y, q), left_send.at[n], left_recv.at[mine], row_peer(spot, n))

    def right_copy(n):
        return remote(
            right_own, right_all.at[slot, q], right_send.at[n], right_recv.at[slot * 4 + q], right_user(spot, n)
        )

    def cot_part(n):
        return cotangent.at[:, pl.ds(pl.multiple_of(q * 128 + n * 32, 32), 32), :]

    def cot_copy(n):
        return remote(cot_part(n), cot_all.at[y], cot_send.at[n], cot_recv.at[y], row_peer(spot, n * 4 + q))

    def start_main(n):
        @pl.when(jnp.logical_not(is_me(right_user(spot, n))))
        def _():
            right_copy(n).start()

        @pl.when(n != mine)
        def _():
            left_copy(n).start()

    def start_cot(n):
        @pl.when(n != y)
        def _():
            cot_copy(n).start()

    repeat(4, start_cot)
    repeat(16, start_main)
    pltpu.make_async_copy(left_own, left_slot(y, q), left_recv.at[mine]).start()

    @pl.when(self_user)
    def _():
        pltpu.make_async_copy(right_own, right_all.at[slot, q], right_recv.at[slot * 4 + q]).start()

    pltpu.make_async_copy(cot_part(y), cot_all.at[y], cot_recv.at[y]).start()

    def finish_main(n):
        at_y, at_q = lax.div(n, 4), lax.rem(n, 4)
        pltpu.make_async_copy(left_own, left_slot(at_y, at_q), left_recv.at[n]).wait()
        pltpu.make_async_copy(right_own, right_all.at[at_y, at_q], right_recv.at[n]).wait()

        @pl.when(n != mine)
        def _():
            left_copy(n).wait_send()

        @pl.when(jnp.logical_not(is_me(right_user(spot, n))))
        def _():
            right_copy(n).wait_send()

    def finish_cot(n):
        pltpu.make_async_copy(cot_part(n), cot_all.at[n], cot_recv.at[n]).wait()

        @pl.when(n != y)
        def _():
            cot_copy(n).wait_send()

    repeat(16, finish_main)
    repeat(4, finish_cot)


def pair_kernel(
    left_all, right_all, cot_all, weight, weight_turned,
    pair, weight_grad, left_grad, right_grad,
    left_mat, right_mat, product, counts, scaled, folded, grad_outer,
):
    row_mask = [
        jnp.concatenate(
            [
                left_all[2 * h, ROWS : ROWS + 8, y * WIDE : y * WIDE + 128].astype(F32)
                + left_all[2 * h + 1, ROWS : ROWS + 8, y * WIDE : y * WIDE + 128].astype(F32)
                for h in range(2)
            ],
            axis=1,
        )
        for y in range(4)
    ]
    column_mask = jnp.concatenate(
        [
            jnp.concatenate(
                [
                    right_all[b, 2 * h, ROWS : ROWS + 8, :128].astype(F32)
                    + right_all[b, 2 * h + 1, ROWS : ROWS + 8, :128].astype(F32)
                    for h in range(2)
                ],
                axis=1,
            )
            for b in range(4)
        ],
        axis=0,
    )
    for i in range(32):
        row = row_mask[i // 8][i % 8 : i % 8 + 1, :]
        product[i * 32 : (i + 1) * 32, :] = (row * column_mask).astype(BF16)
    counts[...] = dot(product[...], jnp.ones((256, 128), BF16))
    for y in range(4):
        cot = cot_all[y].astype(F32).reshape(256, 128)
        scaled[y * 256 : (y + 1) * 256, :] = (cot / counts[y * 256 : (y + 1) * 256, :]).astype(BF16)

    for q in range(4):
        rows = slice(q * ROWS, (q + 1) * ROWS)
        left_mat[rows, :] = left_all[q, :ROWS, :]
        for t in range(2):
            parts = [right_all[b, q, :ROWS, t * 128 : (t + 1) * 128].astype(F32) for b in range(4)]
            for b, part in enumerate(swap(parts, 8)):
                right_mat[rows, (t * 4 + b) * 128 : (t * 4 + b + 1) * 128] = part.astype(BF16)

    def forward(g):
        span = pl.ds(pl.multiple_of(g * 128, 128), 128)
        turned = left_mat[:, span].astype(F32).T.astype(BF16)
        for t in range(8):
            outer = dot(turned, right_mat[:, t * 128 : (t + 1) * 128])
            parts = swap([outer[i * 32 : (i + 1) * 32, :] for i in range(4)], 32)
            for a, part in enumerate(parts):
                folded[(t * 4 + a) * 32 : (t * 4 + a + 1) * 32, span] = part.astype(BF16)

    def backward(g):
        span = pl.ds(pl.multiple_of(g * 128, 128), 128)
        scaled_part = scaled[span, :]
        for t in range(8):
            grad = dot_nt(weight[t * 128 : (t + 1) * 128, :], scaled_part)
            parts = swap([grad[a * 32 : (a + 1) * 32, :] for a in range(4)], 32)
            for i, part in enumerate(parts):
                at = pl.ds(pl.multiple_of(g * 128 + i * 32, 32), 32)
                grad_outer[at, t * 128 : (t + 1) * 128] = part.astype(BF16)

    def project(g):
        span = pl.ds(pl.multiple_of(g * 128, 128), 128)
        turned = dot(weight_turned[...], folded[:, span])
        update = (turned.T / counts[span, :]).astype(BF16)
        pair[pl.ds(pl.multiple_of(g * 4, 4), 4)] = update.reshape(4, 32, 128)

    def weigh(g):
        span = pl.ds(pl.multiple_of(g * 128, 128), 128)
        weight_grad[span, :] = dot(folded[span, :], scaled[...]).astype(BF16)

    def left_part(g):
        span = pl.ds(pl.multiple_of(g * 128, 128), 128)
        part = dot_nt(right_mat[...], grad_outer[span, :]).astype(BF16)
        for q in range(4):
            left_grad[q, :, span] = part[q * ROWS : (q + 1) * ROWS, :]

    repeat(8, backward)
    repeat(8, left_part)
    for t in range(2):
        for q in range(4):
            part = [
                dot(left_mat[q * ROWS : (q + 1) * ROWS, :], grad_outer[:, (t * 4 + b) * 128 : (t * 4 + b + 1) * 128])
                for b in range(4)
            ]
            for b, block in enumerate(swap(part, 8)):
                right_grad[b, q, :, t * 128 : (t + 1) * 128] = block.astype(BF16)
    repeat(8, forward)
    repeat(8, weigh)
    repeat(8, project)


def scatter_kernel(
    left_grad, right_grad, weight_grad, pair, token_turned, mask, white, spread, gain, maps,
    pair_out, weight_out, table_out,
    left_in, right_in, weight_in, weight_sum, weight_far, weight_total,
    table_part, table_in, table_sum, table_far, table_total,
    left_send, left_recv, right_send, right_recv, pair_send, pair_recv,
    wa_send, wa_recv, wb_send, wb_recv, wc_send, wc_recv,
    ta_send, ta_recv, tb_send, tb_recv, tc_send, tc_recv,
):
    spot = place()
    y, z, x, q = spot
    mine = y * 4 + q
    deep = z * 2 + x
    my_res = y * 16 + deep
    self_user = jnp.logical_and(lax.div(z, 2) == y, q == y)

    def is_me(target):
        return jnp.logical_and(target[0] == my_res, target[1] == q)

    barrier = pltpu.get_barrier_semaphore()

    def greet(n):
        @pl.when(n != mine)
        def _():
            signal(barrier, row_peer(spot, n))

        @pl.when(n != deep)
        def _():
            signal(barrier, depth_peer(spot, n))

        user = right_user(spot, n)

        @pl.when(jnp.logical_not(is_me(user)))
        def _():
            signal(barrier, user)

    repeat(16, greet)
    pl.semaphore_wait(barrier, jnp.where(self_user, 45, 46))

    def left_piece(n):
        return left_grad.at[lax.rem(n, 4), :, pl.ds(pl.multiple_of(lax.div(n, 4) * WIDE, WIDE), WIDE)]

    def left_copy(n):
        return remote(left_piece(n), left_in.at[mine], left_send.at[n], left_recv.at[mine], row_peer(spot, n))

    def right_piece(n):
        return right_grad.at[lax.div(n, 4), lax.rem(n, 4)]

    def right_copy(n):
        return remote(right_piece(n), right_in.at[deep], right_send.at[n], right_recv.at[deep], right_owner(spot, n))

    def pair_piece(n):
        return pair.at[pl.ds(pl.multiple_of(n * 8, 8), 8)]

    def pair_slot(n):
        return pair_out.at[:, pl.ds(pl.multiple_of(n * 32, 32), 32), :]

    def pair_copy(n):
        return remote(pair_piece(n), pair_slot(y), pair_send.at[n], pair_recv.at[y], row_peer(spot, n * 4 + q))

    def weight_piece(n):
        return weight_grad.at[pl.ds(pl.multiple_of(n * 64, 64), 64), :]

    def wa_copy(n):
        return remote(weight_piece(n), weight_in.at[mine], wa_send.at[n], wa_recv.at[mine], row_peer(spot, n))

    def wb_copy(n):
        return remote(weight_sum, weight_far.at[deep], wb_send.at[n], wb_recv.at[deep], depth_peer(spot, n))

    def wc_slot(n):
        return weight_out.at[pl.ds(pl.multiple_of(n * 64, 64), 64), :]

    def wc_copy(n):
        return remote(weight_total, wc_slot(mine), wc_send.at[n], wc_recv.at[mine], row_peer(spot, n))

    def ta_copy(n):
        return remote(table_part.at[n], table_in.at[mine], ta_send.at[n], ta_recv.at[mine], row_peer(spot, n))

    def tb_copy(n):
        return remote(table_sum, table_far.at[deep], tb_send.at[n], tb_recv.at[deep], depth_peer(spot, n))

    def tc_copy(n):
        return remote(table_total, table_out.at[mine], tc_send.at[n], tc_recv.at[mine], row_peer(spot, n))

    def wait(src, dst, sem):
        pltpu.make_async_copy(src, dst, sem).wait()

    def start_main(n):
        @pl.when(jnp.logical_not(is_me(right_owner(spot, n))))
        def _():
            right_copy(n).start()

        @pl.when(n != mine)
        def _():
            left_copy(n).start()

    def start_rest(n):
        @pl.when(n != mine)
        def _():
            wa_copy(n).start()

    def start_pair(n):
        @pl.when(n != y)
        def _():
            pair_copy(n).start()

    repeat(16, start_main)
    pltpu.make_async_copy(left_piece(mine), left_in.at[mine], left_recv.at[mine]).start()

    @pl.when(self_user)
    def _():
        n = (lax.rem(z, 2) * 2 + x) * 4 + q
        pltpu.make_async_copy(right_piece(n), right_in.at[deep], right_recv.at[deep]).start()

    repeat(16, start_rest)
    pltpu.make_async_copy(weight_piece(mine), weight_in.at[mine], wa_recv.at[mine]).start()
    repeat(4, start_pair)
    pltpu.make_async_copy(pair_piece(y), pair_slot(y), pair_recv.at[y]).start()

    def arrive_main(n):
        wait(left_piece(n), left_in.at[n], left_recv.at[n])
        wait(right_piece(n), right_in.at[n], right_recv.at[n])

    repeat(16, arrive_main)

    repeat(16, lambda n: wait(weight_piece(n), weight_in.at[n], wa_recv.at[n]))
    total = weight_in[0].astype(F32)
    for n in range(1, 16):
        total = total + weight_in[n].astype(F32)
    weight_sum[...] = total.astype(BF16)

    def start_wb(n):
        @pl.when(n != deep)
        def _():
            wb_copy(n).start()

    repeat(16, start_wb)
    pltpu.make_async_copy(weight_sum, weight_far.at[deep], wb_recv.at[deep]).start()

    left_total = left_in[0].astype(F32)
    right_total = right_in[0].astype(F32)
    for n in range(1, 16):
        left_total = left_total + left_in[n].astype(F32)
        right_total = right_total + right_in[n].astype(F32)
    left_total = left_total.astype(BF16).astype(F32)
    right_total = right_total.astype(BF16).astype(F32)
    lane = lanes((ROWS, 128))
    wide_lane = lanes((ROWS, WIDE))
    kind = lax.broadcasted_iota(jnp.int32, (32, ROWS), 0)
    table = jnp.zeros((32, WIDE), F32)
    for i in range(8):
        tile = left_total[:, (i // 4) * 128 : (i // 4 + 1) * 128]
        picked = jnp.concatenate(
            [
                jnp.where(lax.div(lane, 32) == i % 4, tile, 0.0),
                jnp.where(lax.rem(wide_lane, 8) == i, right_total, 0.0),
            ],
            axis=1,
        ).astype(BF16)
        gained = mask[:, i : i + 1] * dot_nt(picked, maps[...]) * gain[...]
        whitened = white[i]
        stream_grad = spread[i][:, :1] * (
            gained
            - jnp.mean(gained, axis=-1, keepdims=True)
            - whitened * jnp.mean(gained * whitened, axis=-1, keepdims=True)
        )
        hot = (kind == token_turned[i : i + 1, :]).astype(F32)
        table = table + jnp.dot(hot, stream_grad, precision=TOP_PRECISION, preferred_element_type=F32)
    for n in range(TILES):
        table_part[n] = table[(n // 2) * 8 : (n // 2 + 1) * 8, (n % 2) * 128 : (n % 2 + 1) * 128]

    def start_ta(n):
        @pl.when(n != mine)
        def _():
            ta_copy(n).start()

        @pl.when(n == mine)
        def _():
            pltpu.make_async_copy(table_part.at[n], table_in.at[mine], ta_recv.at[mine]).start()

    repeat(TILES, start_ta)
    holder = mine < TILES

    @pl.when(holder)
    def _():
        repeat(16, lambda n: wait(table_sum, table_in.at[n], ta_recv.at[n]))
        partial = table_in[0]
        for n in range(1, 16):
            partial = partial + table_in[n]
        table_sum[...] = partial

        def start_tb(n):
            @pl.when(n != deep)
            def _():
                tb_copy(n).start()

        repeat(16, start_tb)
        pltpu.make_async_copy(table_sum, table_far.at[deep], tb_recv.at[deep]).start()

    repeat(16, lambda n: wait(weight_sum, weight_far.at[n], wb_recv.at[n]))
    total = weight_far[0].astype(F32)
    for n in range(1, 16):
        total = total + weight_far[n].astype(F32)
    weight_total[...] = total.astype(BF16)

    def start_wc(n):
        @pl.when(n != mine)
        def _():
            wc_copy(n).start()

    repeat(16, start_wc)
    pltpu.make_async_copy(weight_total, wc_slot(mine), wc_recv.at[mine]).start()

    @pl.when(holder)
    def _():
        repeat(16, lambda n: wait(table_sum, table_far.at[n], tb_recv.at[n]))
        partial = table_far[0]
        for n in range(1, 16):
            partial = partial + table_far[n]
        table_total[...] = partial

        def start_tc(n):
            @pl.when(n != mine)
            def _():
                tc_copy(n).start()

        repeat(16, start_tc)
        pltpu.make_async_copy(table_total, table_out.at[mine], tc_recv.at[mine]).start()

    repeat(4, lambda n: wait(pair_piece(n), pair_slot(n), pair_recv.at[n]))
    repeat(16, lambda n: wait(weight_total, wc_slot(n), wc_recv.at[n]))
    repeat(TILES, lambda n: wait(table_total, table_out.at[n], tc_recv.at[n]))

    def sent(n):
        @pl.when(n != mine)
        def _():
            left_copy(n).wait_send()
            wa_copy(n).wait_send()
            wc_copy(n).wait_send()

        @pl.when(jnp.logical_not(is_me(right_owner(spot, n))))
        def _():
            right_copy(n).wait_send()

        @pl.when(n != deep)
        def _():
            wb_copy(n).wait_send()

        @pl.when(jnp.logical_and(holder, n != deep))
        def _():
            tb_copy(n).wait_send()

        @pl.when(jnp.logical_and(holder, n != mine))
        def _():
            tc_copy(n).wait_send()

    def sent_table(n):
        @pl.when(n != mine)
        def _():
            ta_copy(n).wait_send()

    def sent_pair(n):
        @pl.when(n != y)
        def _():
            pair_copy(n).wait_send()

    repeat(16, sent)
    repeat(TILES, sent_table)
    repeat(4, sent_pair)


def vmem(count):
    return [pl.BlockSpec(memory_space=pltpu.VMEM)] * count


def sems(*sizes):
    return [pltpu.SemaphoreType.DMA((size,)) for size in sizes]


def shape(dims, dtype=BF16):
    return jax.ShapeDtypeStruct(dims, dtype)


def body(
    alignment_token_classes, deletions, alignment_mask, homolog_stack_values,
    letter_lookup_coefficients, gap_lookup_coefficients, standardize_gain, standardize_offset,
    first_factor_map, left_bias_vector, second_factor_map, right_bias_vector,
    output_weight_matrix, cotangent,
):
    q = lax.axis_index("seq")
    stack = homolog_stack_values.transpose(1, 0, 2)
    mask = alignment_mask.astype(F32)
    mask_turned = jnp.pad(mask.T, ((0, 8), (0, 0)))
    empty = jnp.zeros_like(mask_turned)
    odd = (q % 2) == 1
    mask_rows = jnp.concatenate(
        [jnp.where(odd, empty, mask_turned), jnp.where(odd, mask_turned, empty), empty, empty], axis=1
    ).astype(BF16)
    steps = jnp.arange(32, dtype=jnp.int32).astype(F32)[:, None]
    gaps = (steps > 0).astype(F32) * gap_lookup_coefficients[0] + (
        2.0 / math.pi * jnp.arctan(steps / 3.0)
    ) * gap_lookup_coefficients[1]
    letters = jnp.pad(letter_lookup_coefficients, ((0, 32 - letter_lookup_coefficients.shape[0]), (0, 0)))
    table = jnp.concatenate([letters, gaps, jnp.zeros((64, 256), F32)], axis=0)
    gain = standardize_gain[None, :]
    offset = standardize_offset[None, :]
    maps = jnp.concatenate([jnp.tile(first_factor_map, (1, 4)), jnp.repeat(second_factor_map, 8, axis=1)], axis=1)
    bias = jnp.concatenate([jnp.tile(left_bias_vector, 4), jnp.repeat(right_bias_vector, 8)])[None, :]
    weight = output_weight_matrix.reshape(32, 2, 4, 4, 128).transpose(1, 3, 2, 0, 4).reshape(1024, 128)

    left_all, right_all, cot_all, white, spread = pl.pallas_call(
        gather_kernel,
        out_shape=[
            shape((4, BLOCK, 1024)),
            shape((4, 4, BLOCK, WIDE)),
            shape((4, 8, 32, 128)),
            shape((8, ROWS, 256), F32),
            shape((8, ROWS, 128), F32),
        ],
        in_specs=vmem(10) + [pl.BlockSpec(memory_space=pl.ANY)],
        out_specs=vmem(5),
        scratch_shapes=[pltpu.VMEM((BLOCK, WIDE), BF16), pltpu.VMEM((BLOCK, WIDE), BF16)]
        + sems(16, 16, 16, 16, 4, 4),
        compiler_params=pltpu.CompilerParams(
            collective_id=0, has_side_effects=True, vmem_limit_bytes=32 * 1024 * 1024
        ),
        name="gather",
    )(
        alignment_token_classes, deletions, mask, mask_rows, stack, table, gain, offset, maps, bias, cotangent
    )

    pair, weight_grad, left_grad, right_grad = pl.pallas_call(
        pair_kernel,
        out_shape=[
            shape((32, 32, 128)),
            shape((1024, 128)),
            shape((4, ROWS, 1024)),
            shape((4, 4, ROWS, WIDE)),
        ],
        in_specs=vmem(5),
        out_specs=vmem(4),
        scratch_shapes=[
            pltpu.VMEM((256, 1024), BF16),
            pltpu.VMEM((256, 1024), BF16),
            pltpu.VMEM((1024, 256), BF16),
            pltpu.VMEM((1024, 128), F32),
            pltpu.VMEM((1024, 128), BF16),
            pltpu.VMEM((1024, 1024), BF16),
            pltpu.VMEM((1024, 1024), BF16),
        ],
        compiler_params=pltpu.CompilerParams(vmem_limit_bytes=40 * 1024 * 1024),
        name="pairs",
    )(left_all, right_all, cot_all, weight, weight.T)

    tile = pltpu.VMEM((8, 128), F32)
    pair_update, weight_out, table_out = pl.pallas_call(
        scatter_kernel,
        out_shape=[shape((8, 128, 128)), shape((1024, 128)), shape((TILES, 8, 128), F32)],
        in_specs=vmem(10),
        out_specs=vmem(3),
        scratch_shapes=[
            pltpu.VMEM((16, ROWS, WIDE), BF16),
            pltpu.VMEM((16, ROWS, WIDE), BF16),
            pltpu.VMEM((16, 64, 128), BF16),
            pltpu.VMEM((64, 128), BF16),
            pltpu.VMEM((16, 64, 128), BF16),
            pltpu.VMEM((64, 128), BF16),
            pltpu.VMEM((TILES, 8, 128), F32),
            pltpu.VMEM((16, 8, 128), F32),
            tile,
            pltpu.VMEM((16, 8, 128), F32),
            tile,
        ]
        + sems(16, 16, 16, 16, 4, 4, 16, 16, 16, 16, 16, 16, 16, 16, 16, 16, 16, 16),
        compiler_params=pltpu.CompilerParams(
            collective_id=1, has_side_effects=True, vmem_limit_bytes=32 * 1024 * 1024
        ),
        name="scatter",
    )(
        left_grad, right_grad, weight_grad, pair, alignment_token_classes.T, mask, white, spread, gain, maps
    )
    grad_weight = (
        weight_out.astype(F32).reshape(2, 4, 4, 32, 128).transpose(3, 0, 2, 1, 4).reshape(1024, 128)
    )
    grad_table = (
        table_out.reshape(TILES // 2, 2, 8, 128).transpose(0, 2, 1, 3).reshape(TILES * 4, 256)
    )[: letter_lookup_coefficients.shape[0]]
    return (pair_update, grad_weight, grad_table)


def solution(mesh):
    in_specs = (
        P("seq", "res"), P("seq", "res"), P("seq", "res"), P("seq", "res", None),
        P(), P(), P(), P(), P(), P(), P(), P(), P(),
        P("res", None, None),
    )
    out_specs = (P("res", "seq", None), P(), P())
    return jax.shard_map(body, mesh=mesh, in_specs=in_specs, out_specs=out_specs, check_vma=False)
```

time: 1220 us -> 141 us (0.12)
  waiting for transfers between devices: 518 us -> 0 us
  blocking collectives: 318 us -> 0 us
  local copies, waits for them, and re-layouts: 258 us -> 10.2 us
  Pallas kernels: 0 us -> 129 us
  matrix products: 95.1 us -> 0 us
  between operations: 14.2 us -> 0.85 us
    reduce_scatter x2 -> x0, waiting for transfers between devices: 343 us -> none  [the longest x1 321 us: body(): lax.psum_scatter(grad_right, 'res', scatter_dimension=1, tiled=True)]
    psum x1 -> x0, waiting for transfers between devices: 175 us -> none  [body(): weight_sum, table_sum = lax.psum((grad_weight, table_part), ('res', 'seq'))]
    psum x2 -> x0, blocking collectives: 160 us -> none  [the longest x1 123 us: body(): weight_sum, table_sum = lax.psum((grad_weight, table_part), ('res', 'seq'))]
    all_gather x1 -> x0, blocking collectives: 158 us -> none  [body(): lax.all_gather(alignment_mask.astype(jnp.bfloat16), 'res', axis=1, tiled=...]
    pallas_call x0 -> x3, Pallas kernels: none -> 129 us  [the longest x1 74.2 us: body(): pl.pallas_call(scatter_kernel, out_shape=[shape((8, 128, 128)), shape((10...]
    transpose x12 -> x1, local copies, waits for them, and re-layouts: 115 us -> 0.1 us  [body(): output_weight_matrix.reshape(32, 2, 4, 4, 128).transpose(1, 3, 2, 0, 4)]
    dot_general x31 -> x0, matrix products: 95.1 us -> none  [the longest x4 38.7 us: backward_cols(): jnp.dot(folded, wide_weight, precision=TOP_PRECISION)]
    reshape x14 -> x5, local copies, waits for them, and re-layouts: 87.8 us -> 1.48 us  [the longest x1 1.14 us: body(): weight_out.astype(F32).reshape(2, 4, 4, 32, 128).transpose(3, 0, 2, 1, 4)]
  transfers between devices with their start and end apart: 4 -> 0, of which waited for: 3 -> 0; matrix products, arithmetic and copies ran while one was open for 1% -> 0% of each run, Pallas kernels for 0% -> 0%
where the time goes in v1:
time: 141 us; the launch traced here: 140 us
  Pallas kernels  129 us (91%)
  local copies, waits for them, and re-layouts  10.2 us (7%)
    pallas_call x1, Pallas kernels, body(): pl.pallas_call(scatter_kernel, out_shape=[shape((8, 128, 128)), shape((10...  74.2 us
    pallas_call x1, Pallas kernels, body(): pl.pallas_call(gather_kernel, out_shape=[shape((4, BLOCK, 1024)), shape((...  36.5 us
    pallas_call x1, Pallas kernels, body(): pl.pallas_call(pair_kernel, out_shape=[shape((32, 32, 128)), shape((1024,...  18.1 us
    unnamed x34, local copies, waits for them, and re-layouts  8.1 us

profile of v1, /device:TPU:1, one launch (start us, length us, event | category | flops | bytes accessed | tf_op | source)
XLA Modules:
  0.0 140.3 jit_solution(1487824002074533050)
XLA Ops:
  0.8 0.6 copy-done.12
  1.5 0.6 copy-done.11
  2.1 0.7 copy-done.13
  2.9 0.1 reshape.56
  3.1 0.6 copy-done.9
  3.8 0.6 copy-done.10
  4.6 0.1 maximum_maximum_fusion.mask_rows
  4.7 0.6 copy-done.2
  5.4 0.6 copy-done.8
  6.1 0.1 copy.53
  6.2 0.6 copy-done.7
  6.9 0.1 copy.54
  7.1 0.8 copy-done.5
  7.9 0.1 copy.57
  8.1 0.1 copy.58
  8.2 0.1 copy-done.1
  8.3 0.5 copy-done.4
  8.8 0.1 copy-done.3
  8.9 36.5 %gather.1 = (bf16[4,80,1024]{2,1,0:T(8,128)(2,1)S(1)}, bf16[4,4,80,256]{3,2,1,0:T(8,128)(2,1)S(1)}, bf16[4,8,32,128]{3,2,1,0:T(8,128)(2,1)S(1)}, f32[8,64,256]{2,1,0:T(8,128)S(1)}, f32[8,64,128]{2,1,0:T(8,128)S(1)}) custom-call(s32[64,8]{1,0:T(8,128)S(1)} %copy.55.token, s32[64,8]{1,0:T(8,128)S(1)} %copy.56.deletion, f32[64,8]{1,0:T(8,128)S(1)} %get-tuple-element.28.mask, ...), custom_call_target="tpu_custom_call" | custom-call | tf_op jit(solution)/shard_map/gather/pallas_call | solution.py:620
  45.4 18.1 %pairs.1 = (bf16[32,32,128]{2,1,0:T(8,128)(2,1)S(1)}, bf16[1024,128]{1,0:T(8,128)(2,1)S(1)}, bf16[4,64,1024]{2,1,0:T(8,128)(2,1)S(1)}, bf16[4,4,64,256]{3,2,1,0:T(8,128)(2,1)S(1)}) custom-call(bf16[4,80,1024]{2,1,0:T(8,128)(2,1)S(1)} %get-tuple-element.15.left_all, bf16[4,4,80,256]{3,2,1,0:T(8,128)(2,1)S(1)} %get-tuple-element.16.right_all, ...), custom_call_target="tpu_custom_call" | custom-call | tf_op jit(solution)/shard_map/pairs/pallas_call | solution.py:641
  63.5 74.2 %scatter.1 = (bf16[8,128,128]{2,1,0:T(8,128)(2,1)S(1)}, bf16[1024,128]{1,0:T(8,128)(2,1)S(1)}, f32[6,8,128]{2,1,0:T(8,128)S(1)}) custom-call(bf16[4,64,1024]{2,1,0:T(8,128)(2,1)S(1)} %get-tuple-element.18.left_grad, bf16[4,4,64,256]{3,2,1,0:T(8,128)(2,1)S(1)} %get-tuple-element.19.right_grad, bf16[1024,128]{1,0:T(8,128)(2,1)S(1)} %get-tuple-element.20.weight_grad, ...), custom_call_target="tpu_custom_call" | custom-call | tf_op jit(solution)/shard_map/scatter/pallas_call | solution.py:665
  137.8 1.1 copy.59
  138.9 0.7 copy.64
  139.6 0.6 copy.65
  (42 shorter events, 1.1 us)
Async XLA Ops:
  0.6 6.2 %copy-start = (bf16[256,32]{0,1:T(8,128)(2,1)S(1)}, bf16[256,32]{0,1:T(8,128)(2,1)}, u32[]{:S(2)}) copy-start(bf16[256,32]{0,1:T(8,128)(2,1)} %param.24) | copy-start | bytes 49156
  0.8 0.7 copy-start.12
  1.5 0.7 copy-start.11
  2.1 0.7 copy-start.13
  3.0 0.7 copy-start.9
  3.7 0.7 copy-start.10
  4.6 0.7 copy-start.2
  5.3 0.7 copy-start.8
  6.1 0.7 copy-start.7
  6.9 1.0 copy-start.5
  6.9 1.0 copy-start.6
  7.0 1.3 copy-start.1
  8.1 0.8 copy-start.4
  8.2 0.7 copy-start.3

commit v2 on v0

v2 whole, which is shorter than its diff:
```python
import math

import jax
import jax.numpy as jnp
from jax import lax
from jax.experimental import pallas as pl
from jax.experimental.pallas import tpu as pltpu
from jax.sharding import PartitionSpec as P

EPSILON = 1e-05
MESH = pl.DeviceIdType.MESH
F32 = jnp.float32
BF16 = jnp.bfloat16

ROWS = 64
WIDE = 256
TILES = 6


def device(y, z, xh, xl, c):
    return (y * 16 + z * 2 + xh, xl * 2 + c)


def repeat(count, step):
    lax.fori_loop(0, count, lambda n, carried: (step(n), carried)[1], 0)


def remote(src, dst, send, recv, target):
    return pltpu.make_async_remote_copy(
        src_ref=src, dst_ref=dst, send_sem=send, recv_sem=recv, device_id=target, device_id_type=MESH
    )


def start_all(count, copy, own):
    def step(n):
        @pl.when(n != own)
        def _():
            copy(n).start()

    repeat(count, step)


def sent_all(count, copy, own):
    def step(n):
        @pl.when(n != own)
        def _():
            copy(n).wait_send()

    repeat(count, step)


def local(src, dst, sem):
    return pltpu.make_async_copy(src, dst, sem)


def lanes(dims):
    return lax.broadcasted_iota(jnp.int32, dims, len(dims) - 1)


def block(n, size):
    return pl.ds(pl.multiple_of(n * size, size), size)


def swap(parts, stride):
    lane = lanes(parts[0].shape)
    low = lax.rem(lax.div(lane, stride), 2) == 0
    high = lax.rem(lax.div(lane, 2 * stride), 2) == 0

    def pair(first, second, step, keep):
        return (
            jnp.where(keep, first, pltpu.roll(second, step, 1)),
            jnp.where(keep, pltpu.roll(first, 128 - step, 1), second),
        )

    a, b = pair(parts[0], parts[1], stride, low)
    c, d = pair(parts[2], parts[3], stride, low)
    a, c = pair(a, c, 2 * stride, high)
    b, d = pair(b, d, 2 * stride, high)
    return [a, b, c, d]


def dot(first, second):
    return jnp.dot(first, second, preferred_element_type=F32)


def dot_nt(first, second):
    return lax.dot_general(first, second, (((1,), (1,)), ((), ())), preferred_element_type=F32)


def split(value, count):
    pieces = []
    for _ in range(count):
        piece = value.astype(BF16)
        pieces.append(piece)
        value = value - piece.astype(F32)
    return pieces


def total(ref, count):
    value = ref[0].astype(F32)
    for n in range(1, count):
        value = value + ref[n].astype(F32)
    return value


def kernel(
    token_h, deletion_h, mask_h, mask_rows_h, token_row_h, stack_h, table_h, gain_h, offset_h, maps_h, bias_h,
    weight_h, turned_h, cotangent,
    pair_out, weight_out, table_out,
    token, deletion, mask, mask_rows, token_row, stack, table, gain, offset, maps, bias, weight, weight_turned,
    white, spread, left_own, right_own, row_masks, column_masks, cot_all, left_all, right_all,
    right_mat, product, counts, scaled, folded, grad_outer, pair,
    left_grad, left_core, left_sum, left_in, left_last, left_send, right_grad, right_part, right_in,
    weight_grad, weight_in, weight_sum, weight_far, weight_total, weight_all,
    table_part, table_core, table_x, table_y, table_z, table_half, table_all,
    in_sem, rm_send, rm_recv, cm_send, cm_recv, cot_send, cot_recv,
    l1_send, l1_recv, l2_send, l2_recv, l3_send, l3_recv, r_send, r_recv,
    gx_send, gx_recv, gz_send, gz_recv, gl_send, gl_recv, gr_send, gr_recv, pair_send, pair_recv,
    wa_send, wa_recv, wb_send, wb_recv, wc_send, wc_recv,
    t_send, t_recv, tx_send, tx_recv, ty_send, ty_recv, tz_send, tz_recv,
):
    res = lax.axis_index("res")
    q = lax.axis_index("seq")
    y, z, xh = lax.div(res, 16), lax.rem(lax.div(res, 2), 8), lax.rem(res, 2)
    xl, c = lax.div(q, 2), lax.rem(q, 2)
    zi, parity = lax.div(z, 2), lax.rem(z, 2)
    active = parity == xl
    other_q = (1 - xl) * 2 + c
    plane = y * 4 + xh * 2 + xl
    deep = z * 2 + c
    column = lax.rem(y, 2) * 2 + xh
    own_row = jnp.where(active, deep, -1)
    own_column = jnp.where(lax.div(y, 2) == c, plane, -1)
    other_core = device(y, z, xh, xl, 1 - c)
    partner = device(y, z, xh, 1 - xl, c)

    def wait(src, dst, sem):
        local(src, dst, sem).wait()

    loads = [
        local(src, dst, in_sem.at[n])
        for n, (src, dst) in enumerate(
            [
                (token_h, token), (deletion_h, deletion), (mask_h, mask), (mask_rows_h, mask_rows),
                (token_row_h, token_row), (stack_h, stack), (table_h, table), (gain_h, gain), (offset_h, offset),
                (maps_h, maps), (bias_h, bias), (weight_h, weight), (turned_h, weight_turned),
            ]
        )
    ]
    for load in loads:
        load.start()

    barrier = pltpu.get_barrier_semaphore()

    def signal(target):
        pl.semaphore_signal(barrier, inc=1, device_id=target, device_id_type=MESH)

    def greet(n):
        @pl.when(n != z * 4 + q)
        def _():
            signal((y * 16 + lax.div(n, 4) * 2 + xh, lax.rem(n, 4)))

        @pl.when(n != (y * 2 + xh) * 4 + q)
        def _():
            signal((lax.div(n, 8) * 16 + z * 2 + lax.rem(lax.div(n, 4), 2), lax.rem(n, 4)))

    repeat(32, greet)

    def line_user(n):
        return device(y, lax.div(n, 2), xh, parity, lax.rem(n, 2))

    def plane_user(n):
        return device(lax.div(n, 4), z, lax.div(lax.rem(n, 4), 2), lax.rem(n, 2), lax.div(y, 2))

    def rm_copy(n):
        return remote(mask_rows, row_masks.at[zi, q], rm_send.at[n], rm_recv.at[zi * 4 + q], line_user(n))

    def cm_copy(n):
        return remote(mask_rows, column_masks.at[column, q], cm_send.at[n], cm_recv.at[column * 4 + q], plane_user(n))

    def cot_part(n):
        return cotangent.at[:, pl.ds(c * 2, 2), block(n, 16), :]

    def cot_copy(n):
        return remote(cot_part(n), cot_all.at[zi], cot_send.at[n], cot_recv.at[zi], device(y, n, xh, xl, c))

    def left_slot(at_q, at_z):
        return left_all.at[at_q, :, block(at_z, WIDE)]

    def l1_copy():
        return remote(left_own, left_slot(q, zi), l1_send.at[0], l1_recv.at[0], partner)

    def l2_copy(n):
        return remote(
            left_own, left_slot(q, zi), l2_send.at[n], l2_recv.at[zi * 2 + xl], device(y, n, xh, xl, c)
        )

    def l2_forward(n):
        return remote(
            left_slot(other_q, zi), left_slot(other_q, zi), l2_send.at[8 + n], l2_recv.at[zi * 2 + 1 - xl],
            device(y, n, xh, xl, c),
        )

    def l3_copy(n):
        at_q = n * 2 + c
        return remote(left_all.at[at_q], left_all.at[at_q], l3_send.at[n], l3_recv.at[n], other_core)

    def r_copy(n):
        return remote(right_own, right_all.at[column, q], r_send.at[n], r_recv.at[column * 4 + q], plane_user(n))

    for load in loads[:11]:
        load.wait()
    lane = lanes((ROWS, 128))
    wide_lane = lanes((ROWS, WIDE))
    pieces = split(table[...], 3)
    right_value = jnp.zeros((ROWS, WIDE), F32)
    for h in range(2):
        hot = jnp.concatenate(
            [
                jnp.logical_or(lane == token[:, i : i + 1], lane == deletion[:, i : i + 1] + 32).astype(F32)
                for i in range(h * 4, h * 4 + 4)
            ],
            axis=0,
        ).astype(BF16)
        hidden = stack[h * 4 : h * 4 + 4].reshape(256, 256).astype(F32) + (
            dot(hot, pieces[0]) + dot(hot, pieces[1]) + dot(hot, pieces[2])
        )
        centered = hidden - jnp.mean(hidden, axis=-1, keepdims=True)
        variance = jnp.mean(centered * centered, axis=-1, keepdims=True)
        scale = lax.rsqrt(variance + EPSILON)
        whitened = centered * scale
        white[h * 256 : (h + 1) * 256, :] = whitened
        spread[h * 256 : (h + 1) * 256, :] = jnp.broadcast_to(scale, (256, 128))
        normed = (whitened * gain[...] + offset[...]).astype(BF16)
        rows = dot(normed, maps[...]) + bias[...]
        left_value = jnp.zeros((ROWS, 128), F32)
        for i in range(4):
            part = mask[:, h * 4 + i : h * 4 + i + 1].astype(F32) * rows[i * ROWS : (i + 1) * ROWS, :]
            left_value = jnp.where(lax.div(lane, 32) == i, part[:, :128], left_value)
            right_value = jnp.where(lax.rem(wide_lane, 8) == h * 4 + i, part[:, 128:], right_value)
        left_own[:, h * 128 : (h + 1) * 128] = left_value.astype(BF16)
        if h == 0:
            pl.semaphore_wait(barrier, 62)
            start_all(16, rm_copy, own_row)
            start_all(16, cm_copy, own_column)

            @pl.when(active)
            def _():
                local(mask_rows, row_masks.at[zi, q], rm_recv.at[zi * 4 + q]).start()
                start_all(8, cot_copy, z)
                local(cot_part(z), cot_all.at[zi], cot_recv.at[zi]).start()

            @pl.when(lax.div(y, 2) == c)
            def _():
                local(mask_rows, column_masks.at[column, q], cm_recv.at[column * 4 + q]).start()

    right_own[...] = right_value.astype(BF16)

    @pl.when(jnp.logical_not(active))
    def _():
        l1_copy().start()

    @pl.when(active)
    def _():
        start_all(8, l2_copy, z)
        local(left_own, left_slot(q, zi), l2_recv.at[zi * 2 + xl]).start()

    start_all(16, r_copy, own_column)

    @pl.when(lax.div(y, 2) == c)
    def _():
        local(right_own, right_all.at[column, q], r_recv.at[column * 4 + q]).start()

    @pl.when(active)
    def _():
        wait(left_own, left_slot(other_q, zi), l1_recv.at[0])
        start_all(8, l2_forward, z)

    def arrive_masks(n):
        wait(mask_rows, row_masks.at[lax.div(n, 4), lax.rem(n, 4)], rm_recv.at[n])
        wait(mask_rows, column_masks.at[lax.div(n, 4), lax.rem(n, 4)], cm_recv.at[n])

    repeat(16, arrive_masks)
    column_mask = jnp.concatenate(
        [
            jnp.concatenate([column_masks[b, 2 * h] + column_masks[b, 2 * h + 1] for h in range(2)], axis=1)
            for b in range(4)
        ],
        axis=0,
    )
    for i in range(32):
        row = jnp.concatenate(
            [
                row_masks[i // 8, 2 * h, i % 8 : i % 8 + 1, :] + row_masks[i // 8, 2 * h + 1, i % 8 : i % 8 + 1, :]
                for h in range(2)
            ],
            axis=1,
        )
        product[i * 32 : (i + 1) * 32, :] = (row * column_mask).astype(BF16)
    counts[...] = dot(product[...], jnp.ones((256, 128), BF16))
    for load in loads[11:]:
        load.wait()
    repeat(4, lambda n: wait(cot_part(n), cot_all.at[n], cot_recv.at[n]))
    for n in range(4):
        cot = cot_all[n].astype(F32).reshape(256, 128)
        scaled[n * 256 : (n + 1) * 256, :] = (cot / counts[n * 256 : (n + 1) * 256, :]).astype(BF16)

    def backward(g):
        span = block(g, 256)
        scaled_part = scaled[span, :]
        for t in range(8):
            grad = dot_nt(weight[t * 128 : (t + 1) * 128, :], scaled_part)
            for half in range(2):
                lane_part = grad[:, half * 128 : (half + 1) * 128]
                parts = swap([lane_part[a * 32 : (a + 1) * 32, :] for a in range(4)], 32)
                for i, part in enumerate(parts):
                    at = pl.ds(pl.multiple_of(g * 256 + half * 128 + i * 32, 32), 32)
                    grad_outer[at, t * 128 : (t + 1) * 128] = part.astype(BF16)

    repeat(4, backward)

    forwarded = jnp.where(active, zi * 2 + 1 - xl, -1)

    def arrive_left(n):
        @pl.when(n != forwarded)
        def _():
            wait(left_own, left_slot(lax.rem(n, 2) * 2 + c, lax.div(n, 2)), l2_recv.at[n])

    repeat(8, arrive_left)
    start_all(2, l3_copy, -1)
    repeat(16, lambda n: wait(right_own, right_all.at[lax.div(n, 4), lax.rem(n, 4)], r_recv.at[n]))
    for at_q in range(4):
        rows = slice(at_q * ROWS, (at_q + 1) * ROWS)
        for t in range(2):
            parts = [right_all[b, at_q, :, t * 128 : (t + 1) * 128].astype(F32) for b in range(4)]
            for b, part in enumerate(swap(parts, 8)):
                right_mat[rows, (t * 4 + b) * 128 : (t * 4 + b + 1) * 128] = part.astype(BF16)

    def left_step(g):
        span = block(g, 256)
        part = dot_nt(right_mat[...], grad_outer[span, :]).astype(BF16)
        for at_q in range(4):
            left_grad[at_q, :, span] = part[at_q * ROWS : (at_q + 1) * ROWS, :]

    repeat(4, left_step)

    def gx_copy(n):
        return remote(left_grad.at[n * 2 + 1 - c], left_core.at[n], gx_send.at[n], gx_recv.at[n], other_core)

    start_all(2, gx_copy, -1)
    repeat(2, lambda n: wait(left_all.at[n * 2 + 1 - c], left_all.at[n * 2 + 1 - c], l3_recv.at[n]))

    def right_step(t):
        for b in range(2):
            right_part[:, b * 256 : (b + 1) * 256] = dot(
                left_all[...].reshape(256, 1024), grad_outer[:, t * 512 + b * 256 : t * 512 + (b + 1) * 256]
            )
        for at_q in range(4):
            rows = slice(at_q * ROWS, (at_q + 1) * ROWS)
            parts = swap([right_part[rows, b * 128 : (b + 1) * 128] for b in range(4)], 8)
            for b, part in enumerate(parts):
                right_grad[b, at_q, :, t * 128 : (t + 1) * 128] = part.astype(BF16)

    right_step(0)

    def gz_part(n):
        return left_sum.at[:, :, block(n, WIDE)]

    def gz_copy(n):
        return remote(
            gz_part(n), left_in.at[z], gz_send.at[n], gz_recv.at[z], device(y, n * 2 + xl, xh, xl, c)
        )

    own_gz = jnp.where(active, zi, -1)
    for n in range(2):
        wait(left_core.at[n], left_core.at[n], gx_recv.at[n])
        left_sum[n] = (left_grad[n * 2 + c].astype(F32) + left_core[n].astype(F32)).astype(BF16)
    start_all(4, gz_copy, own_gz)

    @pl.when(active)
    def _():
        local(gz_part(zi), left_in.at[z], gz_recv.at[z]).start()

    right_step(1)

    def gr_part(n):
        return right_grad.at[lax.div(n, 4), lax.rem(n, 4)]

    def gr_copy(n):
        target = device(c * 2 + lax.div(n, 8), z, lax.rem(lax.div(n, 4), 2), lax.div(lax.rem(n, 4), 2), lax.rem(n, 2))
        return remote(gr_part(n), right_in.at[plane], gr_send.at[n], gr_recv.at[plane], target)

    own_gr = jnp.where(lax.div(y, 2) == c, column * 4 + q, -1)
    start_all(16, gr_copy, own_gr)

    @pl.when(lax.div(y, 2) == c)
    def _():
        local(gr_part(column * 4 + q), right_in.at[plane], gr_recv.at[plane]).start()

    def forward(g):
        span = block(g, 128)
        turned = left_all[:, :, span].reshape(256, 128).astype(F32).T.astype(BF16)
        for t in range(8):
            outer = dot(turned, right_mat[:, t * 128 : (t + 1) * 128])
            parts = swap([outer[i * 32 : (i + 1) * 32, :] for i in range(4)], 32)
            for a, part in enumerate(parts):
                folded[(t * 4 + a) * 32 : (t * 4 + a + 1) * 32, span] = part.astype(BF16)

    def weigh(g):
        span = block(g, 128)
        weight_grad[span, :] = dot(folded[span, :], scaled[...]).astype(BF16)

    def project(g):
        span = block(g, 128)
        value = dot(weight_turned[...], folded[:, span])
        update = (value.T / counts[span, :]).astype(BF16)
        pair[block(g, 4)] = update.reshape(4, 32, 128)

    repeat(8, forward)
    repeat(8, weigh)

    def plane_peer(n):
        return device(lax.div(n, 4), z, lax.div(lax.rem(n, 4), 2), lax.rem(n, 2), c)

    def deep_peer(n):
        return device(y, lax.div(n, 2), xh, xl, lax.rem(n, 2))

    def wa_part(n):
        return weight_grad.at[block(n, 64), :]

    def wa_copy(n):
        return remote(wa_part(n), weight_in.at[plane], wa_send.at[n], wa_recv.at[plane], plane_peer(n))

    def wb_copy(n):
        return remote(weight_sum, weight_far.at[deep], wb_send.at[n], wb_recv.at[deep], deep_peer(n))

    def wc_slot(n):
        return weight_all.at[block(n, 64), :]

    def wc_copy(n):
        return remote(weight_total, wc_slot(plane), wc_send.at[n], wc_recv.at[plane], plane_peer(n))

    start_all(16, wa_copy, plane)
    local(wa_part(plane), weight_in.at[plane], wa_recv.at[plane]).start()
    repeat(8, project)

    def pair_part(n):
        return pair.at[block(lax.div(n, 2), 8), block(lax.rem(n, 2), 16), :]

    def pair_slot(n):
        return pair_out.at[:, block(n, 16), :]

    def pair_copy(n):
        target = device(y, lax.div(n, 2) * 2 + xl, xh, c, lax.rem(n, 2))
        return remote(pair_part(n), pair_slot(z), pair_send.at[n], pair_recv.at[z], target)

    keeps_pair = jnp.logical_and(active, xl == c)
    own_pair = jnp.where(keeps_pair, zi * 2 + c, -1)
    start_all(8, pair_copy, own_pair)

    @pl.when(keeps_pair)
    def _():
        local(pair_part(zi * 2 + c), pair_slot(z), pair_recv.at[z]).start()

    def gl_copy():
        return remote(left_send, left_last, gl_send.at[0], gl_recv.at[0], partner)

    @pl.when(active)
    def _():
        repeat(8, lambda n: wait(gz_part(0), left_in.at[n], gz_recv.at[n]))
        away = left_in[0, 1 - xl].astype(F32)
        for n in range(1, 8):
            away = away + left_in[n, 1 - xl].astype(F32)
        left_send[...] = away.astype(BF16)
        gl_copy().start()
        here = left_in[0, xl].astype(F32)
        for n in range(1, 8):
            here = here + left_in[n, xl].astype(F32)
        left_last[...] = here.astype(BF16)

    repeat(16, lambda n: wait(right_in.at[n], right_in.at[n], gr_recv.at[n]))
    right_total = total(right_in, 16).astype(BF16).astype(F32)

    @pl.when(jnp.logical_not(active))
    def _():
        wait(left_last, left_last, gl_recv.at[0])

    left_total = left_last[...].astype(F32)

    sums = jnp.zeros((32, WIDE), F32)
    for h in range(2):
        picked = []
        for i in range(4):
            keep = mask[:, h * 4 + i : h * 4 + i + 1].astype(F32)
            tile = left_total[:, h * 128 : (h + 1) * 128]
            picked.append(
                jnp.concatenate(
                    [
                        jnp.where(lax.div(lane, 32) == i, tile, 0.0) * keep,
                        jnp.where(lax.rem(wide_lane, 8) == h * 4 + i, right_total, 0.0) * keep,
                    ],
                    axis=1,
                )
            )
        picked = jnp.concatenate(picked, axis=0).astype(BF16)
        gained = dot_nt(picked, maps[...]) * gain[...]
        whitened = white[h * 256 : (h + 1) * 256, :]
        stream_grad = spread[h * 256 : (h + 1) * 256, :1] * (
            gained
            - jnp.mean(gained, axis=-1, keepdims=True)
            - whitened * jnp.mean(gained * whitened, axis=-1, keepdims=True)
        )
        kind = lax.broadcasted_iota(jnp.int32, (32, 256), 0)
        hot = (kind == token_row[:, h * 256 : (h + 1) * 256]).astype(F32).astype(BF16)
        for piece in split(stream_grad, 2):
            sums = sums + dot(hot, piece)
    for n in range(TILES):
        table_part[n] = sums[(n // 2) * 8 : (n // 2 + 1) * 8, (n % 2) * 128 : (n % 2 + 1) * 128]

    def t_copy():
        return remote(table_part.at[pl.ds((1 - c) * 3, 3)], table_core, t_send.at[0], t_recv.at[0], other_core)

    at_x = xh * 2 + xl

    def tx_copy(n):
        return remote(
            table_x.at[at_x], table_x.at[at_x], tx_send.at[n], tx_recv.at[at_x],
            device(y, z, lax.div(n, 2), lax.rem(n, 2), c),
        )

    def ty_copy(n):
        return remote(table_y.at[y], table_y.at[y], ty_send.at[n], ty_recv.at[y], device(n, z, xh, xl, c))

    def tz_copy(n):
        return remote(table_z.at[z], table_z.at[z], tz_send.at[n], tz_recv.at[z], device(y, n, xh, xl, c))

    def half(at_c):
        return table_all.at[pl.ds(at_c * 3, 3)]

    def t_last():
        return remote(table_half, half(c), t_send.at[1], t_recv.at[1], other_core)

    def arrive(count, ref, sem, own):
        def step(n):
            @pl.when(n != own)
            def _():
                wait(ref.at[n], ref.at[n], sem.at[n])

        repeat(count, step)

    t_copy().start()
    wait(table_core, table_core, t_recv.at[0])
    table_x[at_x] = table_part[pl.ds(c * 3, 3)] + table_core[...]
    start_all(4, tx_copy, at_x)

    repeat(16, lambda n: wait(weight_in.at[n], weight_in.at[n], wa_recv.at[n]))
    weight_sum[...] = total(weight_in, 16).astype(BF16)
    start_all(16, wb_copy, deep)
    local(weight_sum, weight_far.at[deep], wb_recv.at[deep]).start()

    arrive(4, table_x, tx_recv, at_x)
    table_y[y] = total(table_x, 4)
    start_all(4, ty_copy, y)
    arrive(4, table_y, ty_recv, y)
    table_z[z] = total(table_y, 4)
    start_all(8, tz_copy, z)

    repeat(16, lambda n: wait(weight_far.at[n], weight_far.at[n], wb_recv.at[n]))
    weight_total[...] = total(weight_far, 16).astype(BF16)
    start_all(16, wc_copy, plane)
    local(weight_total, wc_slot(plane), wc_recv.at[plane]).start()

    arrive(8, table_z, tz_recv, z)
    summed = total(table_z, 8)
    table_half[...] = summed
    t_last().start()
    table_all[pl.ds(c * 3, 3)] = summed
    repeat(8, lambda n: wait(pair_slot(n), pair_slot(n), pair_recv.at[n]))
    wait(table_half, half(1 - c), t_recv.at[1])
    for n in range(TILES):
        high = min(8, table_out.shape[0] - (n // 2) * 8)
        table_out[(n // 2) * 8 : (n // 2) * 8 + high, (n % 2) * 128 : (n % 2 + 1) * 128] = table_all[n][:high]
    repeat(16, lambda n: wait(weight_total, wc_slot(n), wc_recv.at[n]))
    for t in range(2):
        for b in range(4):
            for a in range(4):
                at = ((t * 4 + b) * 4 + a) * 32
                weight_out[pl.ds(t * 16 + a * 4 + b, 32, stride=32), :] = weight_all[at : at + 32, :].astype(F32)

    sent_all(16, rm_copy, own_row)
    sent_all(16, cm_copy, own_column)
    sent_all(16, r_copy, own_column)
    sent_all(16, gr_copy, own_gr)
    sent_all(2, l3_copy, -1)
    sent_all(2, gx_copy, -1)
    sent_all(4, gz_copy, own_gz)
    sent_all(16, wa_copy, plane)
    sent_all(16, wb_copy, deep)
    sent_all(16, wc_copy, plane)
    sent_all(8, pair_copy, own_pair)
    sent_all(4, tx_copy, at_x)
    sent_all(4, ty_copy, y)
    sent_all(8, tz_copy, z)
    t_copy().wait_send()
    t_last().wait_send()

    @pl.when(active)
    def _():
        sent_all(8, cot_copy, z)
        sent_all(8, l2_copy, z)
        sent_all(8, l2_forward, z)
        gl_copy().wait_send()

    @pl.when(jnp.logical_not(active))
    def _():
        l1_copy().wait_send()


def shape(dims, dtype=BF16):
    return jax.ShapeDtypeStruct(dims, dtype)


def body(
    alignment_token_classes, deletions, alignment_mask, homolog_stack_values,
    letter_lookup_coefficients, gap_lookup_coefficients, standardize_gain, standardize_offset,
    first_factor_map, left_bias_vector, second_factor_map, right_bias_vector,
    output_weight_matrix, cotangent,
):
    core = lax.rem(lax.axis_index("seq"), 2)
    mask_turned = alignment_mask.astype(F32).T
    empty = jnp.zeros_like(mask_turned)
    mask_rows = jnp.concatenate(
        [jnp.where(core == 0, mask_turned, empty), jnp.where(core == 1, mask_turned, empty)], axis=1
    )
    steps = jnp.arange(32, dtype=jnp.int32).astype(F32)[:, None]
    gaps = (steps > 0).astype(F32) * gap_lookup_coefficients[0] + (
        2.0 / math.pi * jnp.arctan(steps / 3.0)
    ) * gap_lookup_coefficients[1]
    kinds = letter_lookup_coefficients.shape[0]
    letters = jnp.pad(letter_lookup_coefficients, ((0, 32 - kinds), (0, 0)))
    table = jnp.concatenate([letters, gaps, jnp.zeros((64, 256), F32)], axis=0)
    maps = jnp.concatenate([jnp.tile(first_factor_map, (1, 4)), jnp.repeat(second_factor_map, 8, axis=1)], axis=1)
    bias = jnp.concatenate([jnp.tile(left_bias_vector, 4), jnp.repeat(right_bias_vector, 8)])[None, :]
    weight = output_weight_matrix.reshape(32, 2, 4, 4, 128).transpose(1, 3, 2, 0, 4).reshape(1024, 128)
    inputs = [
        alignment_token_classes, deletions, alignment_mask, mask_rows, alignment_token_classes.T.reshape(1, 512),
        homolog_stack_values.transpose(1, 0, 2), table, standardize_gain[None, :], standardize_offset[None, :],
        maps, bias, weight, weight.T,
    ]
    vmem = pltpu.VMEM
    scratch = [vmem(value.shape, value.dtype) for value in inputs] + [
        vmem((512, 256), F32), vmem((512, 128), F32),
        vmem((ROWS, WIDE), BF16), vmem((ROWS, WIDE), BF16),
        vmem((4, 4, 8, 128), F32), vmem((4, 4, 8, 128), F32),
        vmem((4, 8, 2, 16, 128), BF16),
        vmem((4, ROWS, 1024), BF16), vmem((4, 4, ROWS, WIDE), BF16),
        vmem((256, 1024), BF16), vmem((1024, 256), BF16),
        vmem((1024, 128), F32), vmem((1024, 128), BF16),
        vmem((1024, 1024), BF16), vmem((1024, 1024), BF16),
        vmem((32, 32, 128), BF16),
        vmem((4, ROWS, 1024), BF16), vmem((2, ROWS, 1024), BF16), vmem((2, ROWS, 1024), BF16),
        vmem((8, 2, ROWS, WIDE), BF16), vmem((ROWS, WIDE), BF16), vmem((ROWS, WIDE), BF16),
        vmem((4, 4, ROWS, WIDE), BF16), vmem((256, 512), F32), vmem((16, ROWS, WIDE), BF16),
        vmem((1024, 128), BF16), vmem((16, 64, 128), BF16), vmem((64, 128), BF16),
        vmem((16, 64, 128), BF16), vmem((64, 128), BF16), vmem((1024, 128), BF16),
        vmem((TILES, 8, 128), F32), vmem((3, 8, 128), F32),
        vmem((4, 3, 8, 128), F32), vmem((4, 3, 8, 128), F32), vmem((8, 3, 8, 128), F32),
        vmem((3, 8, 128), F32), vmem((TILES, 8, 128), F32),
    ]
    sizes = [len(inputs), 16, 16, 16, 16, 8, 4, 1, 1, 16, 8, 2, 2, 16, 16]
    sizes += [2, 2, 4, 8, 1, 1, 16, 16, 8, 8, 16, 16, 16, 16, 16, 16, 2, 2, 4, 4, 4, 4, 8, 8]
    return pl.pallas_call(
        kernel,
        out_shape=[shape((8, 128, 128)), shape((1024, 128), F32), shape((kinds, 256), F32)],
        in_specs=[pl.BlockSpec(memory_space=pl.ANY)] * (len(inputs) + 1),
        out_specs=[pl.BlockSpec(memory_space=pltpu.VMEM)] * 3,
        scratch_shapes=scratch + [pltpu.SemaphoreType.DMA((size,)) for size in sizes],
        compiler_params=pltpu.CompilerParams(
            collective_id=0, has_side_effects=True, vmem_limit_bytes=48 * 1024 * 1024
        ),
        name="outer_product_mean",
    )(*inputs, cotangent.reshape(8, 4, 128, 128))


def solution(mesh):
    in_specs = (
        P("seq", "res"), P("seq", "res"), P("seq", "res"), P("seq", "res", None),
        P(), P(), P(), P(), P(), P(), P(), P(), P(),
        P("res", None, None),
    )
    out_specs = (P("res", "seq", None), P(), P())
    return jax.shard_map(body, mesh=mesh, in_specs=in_specs, out_specs=out_specs, check_vma=False)
```

time: 1220 us -> 84.7 us (0.07)
  waiting for transfers between devices: 518 us -> 0 us
  blocking collectives: 318 us -> 0 us
  local copies, waits for them, and re-layouts: 258 us -> 9.11 us
  matrix products: 95.1 us -> 0 us
  Pallas kernels: 0 us -> 74 us
  between operations: 14.2 us -> 0.81 us
    reduce_scatter x2 -> x0, waiting for transfers between devices: 343 us -> none  [the longest x1 321 us: body(): lax.psum_scatter(grad_right, 'res', scatter_dimension=1, tiled=True)]
    psum x1 -> x0, waiting for transfers between devices: 175 us -> none  [body(): weight_sum, table_sum = lax.psum((grad_weight, table_part), ('res', 'seq'))]
    psum x2 -> x0, blocking collectives: 160 us -> none  [the longest x1 123 us: body(): weight_sum, table_sum = lax.psum((grad_weight, table_part), ('res', 'seq'))]
    all_gather x1 -> x0, blocking collectives: 158 us -> none  [body(): lax.all_gather(alignment_mask.astype(jnp.bfloat16), 'res', axis=1, tiled=...]
    transpose x12 -> x1, local copies, waits for them, and re-layouts: 115 us -> 0.1 us  [body(): output_weight_matrix.reshape(32, 2, 4, 4, 128).transpose(1, 3, 2, 0, 4)]
    dot_general x31 -> x0, matrix products: 95.1 us -> none  [the longest x4 38.7 us: backward_cols(): jnp.dot(folded, wide_weight, precision=TOP_PRECISION)]
    reshape x14 -> x5, local copies, waits for them, and re-layouts: 87.8 us -> 0.42 us  [the longest x1 0.14 us: body(): output_weight_matrix.reshape(32, 2, 4, 4, 128).transpose(1, 3, 2, 0, 4)]
    pallas_call x0 -> x1, Pallas kernels: none -> 74 us  [body(): pl.pallas_call(kernel, out_shape=[shape((8, 128, 128)), shape((1024, 128)...]
  transfers between devices with their start and end apart: 4 -> 0, of which waited for: 3 -> 0; matrix products, arithmetic and copies ran while one was open for 1% -> 0% of each run, Pallas kernels for 0% -> 0%
where the time goes in v2:
time: 84.7 us; the launch traced here: 84.3 us
  Pallas kernels  74 us (87%)
  local copies, waits for them, and re-layouts  9.11 us (11%)
    pallas_call x1, Pallas kernels, body(): pl.pallas_call(kernel, out_shape=[shape((8, 128, 128)), shape((1024, 128)...  74 us
    unnamed x35, local copies, waits for them, and re-layouts  8.22 us

profile of v2, /device:TPU:1, one launch (start us, length us, event | category | flops | bytes accessed | tf_op | source)
XLA Modules:
  0.0 84.3 jit_solution(2100124037791820885)
XLA Ops:
  0.8 0.5 copy-done.12
  1.3 0.1 tile.21
  1.5 0.6 copy-done.11
  2.1 0.7 copy-done.9
  2.9 0.6 copy-done.13
  3.5 0.1 reshape.47
  3.7 0.6 copy-done.10
  4.3 0.1 copy.38.deletion_h
  4.4 0.1 copy.37.token_h
  4.5 0.1 copy.39.mask_h
  4.6 0.6 copy-done.7
  5.2 0.1 copy.33
  5.4 0.6 copy-done.6
  6.1 0.1 copy.34
  6.3 0.8 copy-done.4
  7.1 0.1 copy.35
  7.3 0.1 copy.36
  7.4 0.1 copy-done.1
  7.5 0.5 copy-done.3
  8.0 0.1 copy-done.2
  8.1 74.0 %outer_product_mean.1 = (bf16[8,128,128]{2,1,0:T(8,128)(2,1)S(1)}, f32[1024,128]{1,0:T(8,128)S(1)}, f32[23,256]{1,0:T(8,128)S(1)}) custom-call(s32[64,8]{1,0:T(8,128)S(1)} %copy.37.token_h, s32[64,8]{1,0:T(8,128)S(1)} %copy.38.deletion_h, s32[64,8]{1,0:T(8,128)S(1)} %copy.39.mask_h, f32[8,128]{1,0:T(8,128)S(1)} %pad_maximum_fusion.1.mask_rows_h, ...), custom_call_target="tpu_custom_call" | custom-call | tf_op jit(solution)/shard_map/outer_product_mean/pallas_call | solution.py:672
  82.2 0.7 copy.45
  82.9 0.8 copy.46
  83.7 0.6 copy.47
  (35 shorter events, 0.7 us)
Async XLA Ops:
  0.6 5.4 %copy-start = (bf16[256,32]{0,1:T(8,128)(2,1)S(1)}, bf16[256,32]{0,1:T(8,128)(2,1)}, u32[]{:S(2)}) copy-start(bf16[256,32]{0,1:T(8,128)(2,1)} %param.24) | copy-start | bytes 49156
  0.7 0.7 copy-start.12
  0.7 0.7 copy-start.8
  1.4 0.7 copy-start.11
  2.1 0.7 copy-start.9
  2.8 0.7 copy-start.13
  3.7 0.7 copy-start.10
  4.5 0.7 copy-start.7
  5.2 0.7 copy-start.6
  6.1 1.0 %copy-start.4 = (bf16[64,8,256]{2,1,0:T(8,128)(2,1)S(1)}, bf16[64,8,256]{2,1,0:T(8,128)(2,1)}, u32[]{:S(2)}) copy-start(bf16[64,8,256]{2,1,0:T(8,128)(2,1)} %param.17) | copy-start | bytes 786436
  6.1 1.0 %copy-start.5 = (bf16[1024,128]{1,0:T(8,128)(2,1)S(1)}, bf16[1024,128]{1,0:T(8,128)(2,1)}, u32[]{:S(2)}) copy-start(bf16[1024,128]{1,0:T(8,128)(2,1)} %param.26) | copy-start | bytes 786436
  6.2 1.3 %copy-start.1 = (bf16[8,512,128]{2,1,0:T(8,128)(2,1)S(1)}, bf16[8,512,128]{2,1,0:T(8,128)(2,1)}, u32[]{:S(2)}) copy-start(bf16[8,512,128]{2,1,0:T(8,128)(2,1)} %param.27) | copy-start | bytes 3145732
  7.2 0.8 copy-start.3
  7.4 0.7 copy-start.2

commit v3 on v2

--- a/solution.py
+++ b/solution.py
@@ -2,6 +2,7 @@
 
 import jax
 import jax.numpy as jnp
+import numpy as np
 from jax import lax
 from jax.experimental import pallas as pl
 from jax.experimental.pallas import tpu as pltpu
@@ -104,19 +105,21 @@
 
 
 def kernel(
-    token_h, deletion_h, mask_h, mask_rows_h, token_row_h, stack_h, table_h, gain_h, offset_h, maps_h, bias_h,
-    weight_h, turned_h, cotangent,
+    token_h, deletion_h, mask_h, stack_h, letters_h, gaps_h, steps_h, gain_h, offset_h,
+    left_map_h, left_bias_h, right_map_h, right_bias_h, weight_h, cotangent,
     pair_out, weight_out, table_out,
-    token, deletion, mask, mask_rows, token_row, stack, table, gain, offset, maps, bias, weight, weight_turned,
+    token, deletion, mask, stack_raw, letters, gaps, steps, gain, offset,
+    left_map, left_bias, right_map, right_bias, weight_raw,
+    square, turned, mask_rows, stack, table, maps, bias, weight_wide, weight, weight_turned, hot_turned,
     white, spread, left_own, right_own, row_masks, column_masks, cot_all, left_all, right_all,
     right_mat, product, counts, scaled, folded, grad_outer, pair,
     left_grad, left_core, left_sum, left_in, left_last, left_send, right_grad, right_part, right_in,
-    weight_grad, weight_in, weight_sum, weight_far, weight_total, weight_all,
+    weight_grad, weight_core, weight_half, weight_in, weight_sum, weight_far, weight_total, weight_all,
     table_part, table_core, table_x, table_y, table_z, table_half, table_all,
     in_sem, rm_send, rm_recv, cm_send, cm_recv, cot_send, cot_recv,
     l1_send, l1_recv, l2_send, l2_recv, l3_send, l3_recv, r_send, r_recv,
     gx_send, gx_recv, gz_send, gz_recv, gl_send, gl_recv, gr_send, gr_recv, pair_send, pair_recv,
-    wa_send, wa_recv, wb_send, wb_recv, wc_send, wc_recv,
+    wh_send, wh_recv, wa_send, wa_recv, wb_send, wb_recv, wc_send, wc_recv,
     t_send, t_recv, tx_send, tx_recv, ty_send, ty_recv, tz_send, tz_recv,
 ):
     res = lax.axis_index("res")
@@ -141,9 +144,10 @@
         local(src, dst, in_sem.at[n])
         for n, (src, dst) in enumerate(
             [
-                (token_h, token), (deletion_h, deletion), (mask_h, mask), (mask_rows_h, mask_rows),
-                (token_row_h, token_row), (stack_h, stack), (table_h, table), (gain_h, gain), (offset_h, offset),
-                (maps_h, maps), (bias_h, bias), (weight_h, weight), (turned_h, weight_turned),
+                (token_h, token), (deletion_h, deletion), (mask_h, mask), (stack_h, stack_raw),
+                (letters_h, letters), (gaps_h, gaps), (steps_h, steps), (gain_h, gain), (offset_h, offset),
+                (left_map_h, left_map), (left_bias_h, left_bias), (right_map_h, right_map),
+                (right_bias_h, right_bias), (weight_h, weight_raw),
             ]
         )
     ]
@@ -208,23 +212,60 @@
     def r_copy(n):
         return remote(right_own, right_all.at[column, q], r_send.at[n], r_recv.at[column * 4 + q], plane_user(n))
 
-    for load in loads[:11]:
+    for load in loads[:13]:
         load.wait()
+    mask_value = mask[...].astype(F32)
+    empty = jnp.zeros((8, ROWS), F32)
+    mask_rows[...] = jnp.where(
+        c == 0, jnp.concatenate([mask_value, empty], axis=1), jnp.concatenate([empty, mask_value], axis=1)
+    )
+    square[...] = jnp.zeros((128, 128), F32)
+    square[0:8, 0:ROWS] = token[...].astype(F32)
+    square[8:16, 0:ROWS] = deletion[...].astype(F32)
+    square[16:24, 0:ROWS] = mask_value
+    turned[...] = square[...].T[:ROWS]
+    for n in range(2):
+        stack[n] = stack_raw[:, :, n * 128 : (n + 1) * 128].astype(F32).reshape(512, 128)
+    table[...] = jnp.zeros((128, WIDE), F32)
+    table[: letters.shape[0], :] = letters[...]
+    table[32:64, :] = steps[:, 0:1] * gaps[0:1, :] + steps[:, 1:2] * gaps[1:2, :]
+    spread_left = (
+        lax.rem(lax.broadcasted_iota(jnp.int32, (128, 32), 0), 32) == lanes((128, 32))
+    ).astype(F32).astype(BF16)
+    spread_right = (
+        lax.div(lax.broadcasted_iota(jnp.int32, (WIDE, 32), 0), 8) == lanes((WIDE, 32))
+    ).astype(F32).astype(BF16)
+    maps[:128, :] = dot(spread_left, left_map[...]).astype(BF16)
+    maps[128:, :] = dot(spread_right, right_map[...]).astype(BF16)
+    bias[...] = jnp.concatenate(
+        [
+            sum(dot_nt(piece, spread_left) for piece in split(jnp.broadcast_to(left_bias[...], (8, 32)), 3)),
+            sum(dot_nt(piece, spread_right) for piece in split(jnp.broadcast_to(right_bias[...], (8, 32)), 3)),
+        ],
+        axis=1,
+    )
     lane = lanes((ROWS, 128))
+    fine = lane.astype(F32)
     wide_lane = lanes((ROWS, WIDE))
     pieces = split(table[...], 3)
     right_value = jnp.zeros((ROWS, WIDE), F32)
     for h in range(2):
         hot = jnp.concatenate(
             [
-                jnp.logical_or(lane == token[:, i : i + 1], lane == deletion[:, i : i + 1] + 32).astype(F32)
+                jnp.logical_or(fine == turned[:, i : i + 1], fine == turned[:, 8 + i : 9 + i] + 32.0).astype(F32)
                 for i in range(h * 4, h * 4 + 4)
             ],
             axis=0,
-        ).astype(BF16)
-        hidden = stack[h * 4 : h * 4 + 4].reshape(256, 256).astype(F32) + (
-            dot(hot, pieces[0]) + dot(hot, pieces[1]) + dot(hot, pieces[2])
-        )
+        )
+        hot_turned[h] = hot.T[:32].astype(BF16)
+        hot = hot.astype(BF16)
+        hidden = jnp.concatenate(
+            [
+                jnp.concatenate([stack[n, pl.ds(i, ROWS, stride=8), :] for i in range(h * 4, h * 4 + 4)], axis=0)
+                for n in range(2)
+            ],
+            axis=1,
+        ) + (dot(hot, pieces[0]) + dot(hot, pieces[1]) + dot(hot, pieces[2]))
         centered = hidden - jnp.mean(hidden, axis=-1, keepdims=True)
         variance = jnp.mean(centered * centered, axis=-1, keepdims=True)
         scale = lax.rsqrt(variance + EPSILON)
@@ -232,10 +273,10 @@
         white[h * 256 : (h + 1) * 256, :] = whitened
         spread[h * 256 : (h + 1) * 256, :] = jnp.broadcast_to(scale, (256, 128))
         normed = (whitened * gain[...] + offset[...]).astype(BF16)
-        rows = dot(normed, maps[...]) + bias[...]
+        rows = dot_nt(normed, maps[...]) + bias[:1, :]
         left_value = jnp.zeros((ROWS, 128), F32)
         for i in range(4):
-            part = mask[:, h * 4 + i : h * 4 + i + 1].astype(F32) * rows[i * ROWS : (i + 1) * ROWS, :]
+            part = turned[:, 16 + h * 4 + i : 17 + h * 4 + i] * rows[i * ROWS : (i + 1) * ROWS, :]
             left_value = jnp.where(lax.div(lane, 32) == i, part[:, :128], left_value)
             right_value = jnp.where(lax.rem(wide_lane, 8) == h * 4 + i, part[:, 128:], right_value)
         left_own[:, h * 128 : (h + 1) * 128] = left_value.astype(BF16)
@@ -275,6 +316,16 @@
     def _():
         wait(left_own, left_slot(other_q, zi), l1_recv.at[0])
         start_all(8, l2_forward, z)
+
+    loads[13].wait()
+    weight_wide[...] = weight_raw[...].astype(F32)
+    for t in range(2):
+        for b in range(4):
+            for a in range(4):
+                at = ((t * 4 + b) * 4 + a) * 32
+                weight[at : at + 32, :] = weight_wide[pl.ds(t * 16 + a * 4 + b, 32, stride=32), :].astype(BF16)
+    for t in range(8):
+        weight_turned[:, t * 128 : (t + 1) * 128] = weight[t * 128 : (t + 1) * 128, :].astype(F32).T.astype(BF16)
 
     def arrive_masks(n):
         wait(mask_rows, row_masks.at[lax.div(n, 4), lax.rem(n, 4)], rm_recv.at[n])
@@ -298,8 +349,6 @@
         )
         product[i * 32 : (i + 1) * 32, :] = (row * column_mask).astype(BF16)
     counts[...] = dot(product[...], jnp.ones((256, 128), BF16))
-    for load in loads[11:]:
-        load.wait()
     repeat(4, lambda n: wait(cot_part(n), cot_all.at[n], cot_recv.at[n]))
     for n in range(4):
         cot = cot_all[n].astype(F32).reshape(256, 128)
@@ -399,16 +448,16 @@
 
     def forward(g):
         span = block(g, 128)
-        turned = left_all[:, :, span].reshape(256, 128).astype(F32).T.astype(BF16)
+        lead = left_all[:, :, span].reshape(256, 128).astype(F32).T.astype(BF16)
         for t in range(8):
-            outer = dot(turned, right_mat[:, t * 128 : (t + 1) * 128])
+            outer = dot(lead, right_mat[:, t * 128 : (t + 1) * 128])
             parts = swap([outer[i * 32 : (i + 1) * 32, :] for i in range(4)], 32)
             for a, part in enumerate(parts):
                 folded[(t * 4 + a) * 32 : (t * 4 + a + 1) * 32, span] = part.astype(BF16)
 
     def weigh(g):
         span = block(g, 128)
-        weight_grad[span, :] = dot(folded[span, :], scaled[...]).astype(BF16)
+        weight_grad[span, :] = dot(folded[span, :], scaled[...])
 
     def project(g):
         span = block(g, 128)
@@ -422,27 +471,36 @@
     def plane_peer(n):
         return device(lax.div(n, 4), z, lax.div(lax.rem(n, 4), 2), lax.rem(n, 2), c)
 
-    def deep_peer(n):
-        return device(y, lax.div(n, 2), xh, xl, lax.rem(n, 2))
+    def line_peer(n):
+        return device(y, n, xh, xl, c)
+
+    def wh_copy():
+        return remote(weight_grad.at[block(1 - c, 512), :], weight_core, wh_send.at[0], wh_recv.at[0], other_core)
 
     def wa_part(n):
-        return weight_grad.at[block(n, 64), :]
+        return weight_half.at[block(n, 32), :]
 
     def wa_copy(n):
         return remote(wa_part(n), weight_in.at[plane], wa_send.at[n], wa_recv.at[plane], plane_peer(n))
 
     def wb_copy(n):
-        return remote(weight_sum, weight_far.at[deep], wb_send.at[n], wb_recv.at[deep], deep_peer(n))
+        return remote(weight_sum, weight_far.at[z], wb_send.at[n], wb_recv.at[z], line_peer(n))
 
     def wc_slot(n):
-        return weight_all.at[block(n, 64), :]
+        return weight_all.at[c, block(n, 32), :]
 
     def wc_copy(n):
         return remote(weight_total, wc_slot(plane), wc_send.at[n], wc_recv.at[plane], plane_peer(n))
 
+    def wd_copy():
+        return remote(weight_all.at[c], weight_all.at[c], wh_send.at[1], wh_recv.at[1], other_core)
+
+    wh_copy().start()
+    repeat(8, project)
+    wait(weight_core, weight_core, wh_recv.at[0])
+    weight_half[...] = (weight_grad[block(c, 512), :] + weight_core[...]).astype(BF16)
     start_all(16, wa_copy, plane)
     local(wa_part(plane), weight_in.at[plane], wa_recv.at[plane]).start()
-    repeat(8, project)
 
     def pair_part(n):
         return pair.at[block(lax.div(n, 2), 8), block(lax.rem(n, 2), 16), :]
@@ -487,11 +545,16 @@
 
     left_total = left_last[...].astype(F32)
 
+    repeat(16, lambda n: wait(weight_in.at[n], weight_in.at[n], wa_recv.at[n]))
+    weight_sum[...] = total(weight_in, 16).astype(BF16)
+    start_all(8, wb_copy, z)
+    local(weight_sum, weight_far.at[z], wb_recv.at[z]).start()
+
     sums = jnp.zeros((32, WIDE), F32)
     for h in range(2):
         picked = []
         for i in range(4):
-            keep = mask[:, h * 4 + i : h * 4 + i + 1].astype(F32)
+            keep = turned[:, 16 + h * 4 + i : 17 + h * 4 + i]
             tile = left_total[:, h * 128 : (h + 1) * 128]
             picked.append(
                 jnp.concatenate(
@@ -503,17 +566,15 @@
                 )
             )
         picked = jnp.concatenate(picked, axis=0).astype(BF16)
-        gained = dot_nt(picked, maps[...]) * gain[...]
+        gained = dot(picked, maps[...]) * gain[...]
         whitened = white[h * 256 : (h + 1) * 256, :]
         stream_grad = spread[h * 256 : (h + 1) * 256, :1] * (
             gained
             - jnp.mean(gained, axis=-1, keepdims=True)
             - whitened * jnp.mean(gained * whitened, axis=-1, keepdims=True)
         )
-        kind = lax.broadcasted_iota(jnp.int32, (32, 256), 0)
-        hot = (kind == token_row[:, h * 256 : (h + 1) * 256]).astype(F32).astype(BF16)
         for piece in split(stream_grad, 2):
-            sums = sums + dot(hot, piece)
+            sums = sums + dot(hot_turned[h], piece)
     for n in range(TILES):
         table_part[n] = sums[(n // 2) * 8 : (n // 2 + 1) * 8, (n % 2) * 128 : (n % 2 + 1) * 128]
 
@@ -553,10 +614,10 @@
     table_x[at_x] = table_part[pl.ds(c * 3, 3)] + table_core[...]
     start_all(4, tx_copy, at_x)
 
-    repeat(16, lambda n: wait(weight_in.at[n], weight_in.at[n], wa_recv.at[n]))
-    weight_sum[...] = total(weight_in, 16).astype(BF16)
-    start_all(16, wb_copy, deep)
-    local(weight_sum, weight_far.at[deep], wb_recv.at[deep]).start()
+    repeat(8, lambda n: wait(weight_far.at[n], weight_far.at[n], wb_recv.at[n]))
+    weight_total[...] = total(weight_far, 8).astype(BF16)
+    start_all(16, wc_copy, plane)
+    local(weight_total, wc_slot(plane), wc_recv.at[plane]).start()
 
     arrive(4, table_x, tx_recv, at_x)
     table_y[y] = total(table_x, 4)
@@ -565,10 +626,8 @@
     table_z[z] = total(table_y, 4)
     start_all(8, tz_copy, z)
 
-    repeat(16, lambda n: wait(weight_far.at[n], weight_far.at[n], wb_recv.at[n]))
-    weight_total[...] = total(weight_far, 16).astype(BF16)
-    start_all(16, wc_copy, plane)
-    local(weight_total, wc_slot(plane), wc_recv.at[plane]).start()
+    repeat(16, lambda n: wait(weight_total, wc_slot(n), wc_recv.at[n]))
+    wd_copy().start()
 
     arrive(8, table_z, tz_recv, z)
     summed = total(table_z, 8)
@@ -580,12 +639,12 @@
     for n in range(TILES):
         high = min(8, table_out.shape[0] - (n // 2) * 8)
         table_out[(n // 2) * 8 : (n // 2) * 8 + high, (n % 2) * 128 : (n % 2 + 1) * 128] = table_all[n][:high]
-    repeat(16, lambda n: wait(weight_total, wc_slot(n), wc_recv.at[n]))
+    wait(weight_all.at[1 - c], weight_all.at[1 - c], wh_recv.at[1])
     for t in range(2):
         for b in range(4):
             for a in range(4):
                 at = ((t * 4 + b) * 4 + a) * 32
-                weight_out[pl.ds(t * 16 + a * 4 + b, 32, stride=32), :] = weight_all[at : at + 32, :].astype(F32)
+                weight_out[pl.ds(t * 16 + a * 4 + b, 32, stride=32), :] = weight_all[at // 512, at % 512 : at % 512 + 32, :].astype(F32)
 
     sent_all(16, rm_copy, own_row)
     sent_all(16, cm_copy, own_column)
@@ -595,7 +654,9 @@
     sent_all(2, gx_copy, -1)
     sent_all(4, gz_copy, own_gz)
     sent_all(16, wa_copy, plane)
-    sent_all(16, wb_copy, deep)
+    sent_all(8, wb_copy, z)
+    wh_copy().wait_send()
+    wd_copy().wait_send()
     sent_all(16, wc_copy, plane)
     sent_all(8, pair_copy, own_pair)
     sent_all(4, tx_copy, at_x)
@@ -626,29 +687,25 @@
     first_factor_map, left_bias_vector, second_factor_map, right_bias_vector,
     output_weight_matrix, cotangent,
 ):
-    core = lax.rem(lax.axis_index("seq"), 2)
-    mask_turned = alignment_mask.astype(F32).T
-    empty = jnp.zeros_like(mask_turned)
-    mask_rows = jnp.concatenate(
-        [jnp.where(core == 0, mask_turned, empty), jnp.where(core == 1, mask_turned, empty)], axis=1
+    kinds = letter_lookup_coefficients.shape[0]
+    grades = np.arange(32, dtype=np.float32)
+    steps = jnp.asarray(
+        np.stack([(grades > 0).astype(np.float32), (2.0 / math.pi * np.arctan(grades / 3.0)).astype(np.float32)], 1)
     )
-    steps = jnp.arange(32, dtype=jnp.int32).astype(F32)[:, None]
-    gaps = (steps > 0).astype(F32) * gap_lookup_coefficients[0] + (
-        2.0 / math.pi * jnp.arctan(steps / 3.0)
-    ) * gap_lookup_coefficients[1]
-    kinds = letter_lookup_coefficients.shape[0]
-    letters = jnp.pad(letter_lookup_coefficients, ((0, 32 - kinds), (0, 0)))
-    table = jnp.concatenate([letters, gaps, jnp.zeros((64, 256), F32)], axis=0)
-    maps = jnp.concatenate([jnp.tile(first_factor_map, (1, 4)), jnp.repeat(second_factor_map, 8, axis=1)], axis=1)
-    bias = jnp.concatenate([jnp.tile(left_bias_vector, 4), jnp.repeat(right_bias_vector, 8)])[None, :]
-    weight = output_weight_matrix.reshape(32, 2, 4, 4, 128).transpose(1, 3, 2, 0, 4).reshape(1024, 128)
     inputs = [
-        alignment_token_classes, deletions, alignment_mask, mask_rows, alignment_token_classes.T.reshape(1, 512),
-        homolog_stack_values.transpose(1, 0, 2), table, standardize_gain[None, :], standardize_offset[None, :],
-        maps, bias, weight, weight.T,
+        alignment_token_classes.T, deletions.T, alignment_mask.T, homolog_stack_values,
+        letter_lookup_coefficients, gap_lookup_coefficients, steps,
+        standardize_gain.reshape(1, 256), standardize_offset.reshape(1, 256),
+        first_factor_map.T, left_bias_vector.reshape(1, 32), second_factor_map.T, right_bias_vector.reshape(1, 32),
+        output_weight_matrix,
     ]
     vmem = pltpu.VMEM
     scratch = [vmem(value.shape, value.dtype) for value in inputs] + [
+        vmem((128, 128), F32), vmem((ROWS, 128), F32), vmem((8, 128), F32),
+        vmem((2, 512, 128), F32),
+        vmem((128, WIDE), F32), vmem((384, 256), BF16), vmem((8, 384), F32),
+        vmem((1024, 128), F32), vmem((1024, 128), BF16), vmem((128, 1024), BF16),
+        vmem((2, 32, 256), BF16),
         vmem((512, 256), F32), vmem((512, 128), F32),
         vmem((ROWS, WIDE), BF16), vmem((ROWS, WIDE), BF16),
         vmem((4, 4, 8, 128), F32), vmem((4, 4, 8, 128), F32),
@@ -661,25 +718,47 @@
         vmem((4, ROWS, 1024), BF16), vmem((2, ROWS, 1024), BF16), vmem((2, ROWS, 1024), BF16),
         vmem((8, 2, ROWS, WIDE), BF16), vmem((ROWS, WIDE), BF16), vmem((ROWS, WIDE), BF16),
         vmem((4, 4, ROWS, WIDE), BF16), vmem((256, 512), F32), vmem((16, ROWS, WIDE), BF16),
-        vmem((1024, 128), BF16), vmem((16, 64, 128), BF16), vmem((64, 128), BF16),
-        vmem((16, 64, 128), BF16), vmem((64, 128), BF16), vmem((1024, 128), BF16),
+        vmem((1024, 128), F32), vmem((512, 128), F32), vmem((512, 128), BF16),
+        vmem((16, 32, 128), BF16), vmem((32, 128), BF16),
+        vmem((8, 32, 128), BF16), vmem((32, 128), BF16), vmem((2, 512, 128), BF16),
         vmem((TILES, 8, 128), F32), vmem((3, 8, 128), F32),
         vmem((4, 3, 8, 128), F32), vmem((4, 3, 8, 128), F32), vmem((8, 3, 8, 128), F32),
         vmem((3, 8, 128), F32), vmem((TILES, 8, 128), F32),
     ]
     sizes = [len(inputs), 16, 16, 16, 16, 8, 4, 1, 1, 16, 8, 2, 2, 16, 16]
-    sizes += [2, 2, 4, 8, 1, 1, 16, 16, 8, 8, 16, 16, 16, 16, 16, 16, 2, 2, 4, 4, 4, 4, 8, 8]
-    return pl.pallas_call(
+    sizes += [2, 2, 4, 8, 1, 1, 16, 16, 8, 8, 2, 2, 16, 16, 8, 8, 16, 16, 2, 2, 4, 4, 4, 4, 8, 8]
+    results = pl.pallas_call(
         kernel,
         out_shape=[shape((8, 128, 128)), shape((1024, 128), F32), shape((kinds, 256), F32)],
         in_specs=[pl.BlockSpec(memory_space=pl.ANY)] * (len(inputs) + 1),
         out_specs=[pl.BlockSpec(memory_space=pltpu.VMEM)] * 3,
         scratch_shapes=scratch + [pltpu.SemaphoreType.DMA((size,)) for size in sizes],
         compiler_params=pltpu.CompilerParams(
-            collective_id=0, has_side_effects=True, vmem_limit_bytes=48 * 1024 * 1024
+            collective_id=0, has_side_effects=True, vmem_limit_bytes=60 * 1024 * 1024
         ),
         name="outer_product_mean",
     )(*inputs, cotangent.reshape(8, 4, 128, 128))
+    return pl.pallas_call(
+        hand_over,
+        out_shape=[shape(value.shape, value.dtype) for value in results],
+        in_specs=[pl.BlockSpec(memory_space=pl.ANY)] * 3,
+        out_specs=[pl.BlockSpec(memory_space=pl.ANY)] * 3,
+        scratch_shapes=[vmem(value.shape, value.dtype) for value in results] + [pltpu.SemaphoreType.DMA((3,))],
+        name="hand_over",
+    )(*results)
+
+
+def hand_over(pair, weight, table, pair_out, weight_out, table_out, pair_here, weight_here, table_here, sem):
+    here = [pair_here, weight_here, table_here]
+    arrive = [local(src, dst, sem.at[n]) for n, (src, dst) in enumerate(zip([pair, weight, table], here))]
+    leave = [local(src, dst, sem.at[n]) for n, (src, dst) in enumerate(zip(here, [pair_out, weight_out, table_out]))]
+    for copy in arrive:
+        copy.start()
+    for first, second in zip(arrive, leave):
+        first.wait()
+        second.start()
+    for copy in leave:
+        copy.wait()
 
 
 def solution(mesh):

time: 84.7 us -> 79.5 us (0.939)
  local copies, waits for them, and re-layouts: 9.11 us -> 0 us
  Pallas kernels: 74 us -> 78.8 us
    unnamed x35 -> x0, local copies, waits for them, and re-layouts: 8.22 us -> none
    pallas_call x1, Pallas kernels: 74 us -> 76.8 us  [body(): pl.pallas_call(kernel, out_shape=[shape((8, 128, 128)), shape((1024, 128)...]
    pallas_call x0 -> x1, Pallas kernels: none -> 1.94 us  [body(): pl.pallas_call(hand_over, out_shape=[shape(value.shape, value.dtype) for...]
where the time goes in v3:
time: 79.5 us; the launch traced here: 79.4 us
  Pallas kernels  78.8 us (99%)
    pallas_call x1, Pallas kernels, body(): pl.pallas_call(kernel, out_shape=[shape((8, 128, 128)), shape((1024, 128)...  76.8 us
    pallas_call x1, Pallas kernels, body(): pl.pallas_call(hand_over, out_shape=[shape(value.shape, value.dtype) for...  1.94 us

profile of v3, /device:TPU:1, one launch (start us, length us, event | category | flops | bytes accessed | tf_op | source)
XLA Modules:
  0.0 79.4 jit_solution(7487743335962886635)
XLA Ops:
  0.6 76.8 %outer_product_mean.1 = (bf16[8,128,128]{2,1,0:T(8,128)(2,1)}, f32[1024,128]{1,0:T(8,128)}, f32[23,256]{1,0:T(8,128)}) custom-call(s32[8,64]{1,0:T(8,128)} %bitcast.13, s32[8,64]{1,0:T(8,128)} %bitcast.14, s32[8,64]{1,0:T(8,128)} %bitcast.15, bf16[64,8,256]{2,1,0:T(8,128)(2,1)} %stack_h.1, f32[23,256]{1,0:T(8,128)} %letters_h.1, f32[2,256]{1,0:T(2,128)} %gaps_h.1, ...), custom_call_target="tpu_custom_call" | custom-call | tf_op jit(solution)/shard_map/outer_product_mean/pallas_call | solution.py:730
  77.5 1.9 %hand_over.1 = (bf16[8,128,128]{2,1,0:T(8,128)(2,1)}, f32[1024,128]{1,0:T(8,128)}, f32[23,256]{1,0:T(8,128)}) custom-call(bf16[8,128,128]{2,1,0:T(8,128)(2,1)} %get-tuple-element.6.pair, f32[1024,128]{1,0:T(8,128)} %get-tuple-element.7.weight, f32[23,256]{1,0:T(8,128)} %get-tuple-element.8.table), custom_call_target="tpu_custom_call" | custom-call | tf_op jit(solution)/shard_map/hand_over/pallas_call | solution.py:741

commit v4 on v3

--- a/solution.py
+++ b/solution.py
@@ -109,18 +109,18 @@
     left_map_h, left_bias_h, right_map_h, right_bias_h, weight_h, cotangent,
     pair_out, weight_out, table_out,
     token, deletion, mask, stack_raw, letters, gaps, steps, gain, offset,
-    left_map, left_bias, right_map, right_bias, weight_raw,
+    left_map, left_bias, right_map, right_bias, weight_raw, cot_raw, cot_stage,
     square, turned, mask_rows, stack, table, maps, bias, weight_wide, weight, weight_turned, hot_turned,
     white, spread, left_own, right_own, row_masks, column_masks, cot_all, left_all, right_all,
-    right_mat, product, counts, scaled, folded, grad_outer, pair,
-    left_grad, left_core, left_sum, left_in, left_last, left_send, right_grad, right_part, right_in,
+    right_mat, product, counts, scaled, folded, grad_outer, pair, pair_in,
+    right_grad, right_part, right_core, right_sum, right_in, right_last, right_send, left_grad, left_in,
     weight_grad, weight_core, weight_half, weight_in, weight_sum, weight_far, weight_total, weight_all,
-    table_part, table_core, table_x, table_y, table_z, table_half, table_all,
+    table_part, table_core, table_p, table_z, table_half, table_all,
     in_sem, rm_send, rm_recv, cm_send, cm_recv, cot_send, cot_recv,
-    l1_send, l1_recv, l2_send, l2_recv, l3_send, l3_recv, r_send, r_recv,
-    gx_send, gx_recv, gz_send, gz_recv, gl_send, gl_recv, gr_send, gr_recv, pair_send, pair_recv,
+    r1_send, r1_recv, r2_send, r2_recv, r3_send, r3_recv, l_send, l_recv,
+    gx_send, gx_recv, gz_send, gz_recv, gf_send, gf_recv, gl_send, gl_recv, pair_send, pair_recv,
     wh_send, wh_recv, wa_send, wa_recv, wb_send, wb_recv, wc_send, wc_recv,
-    t_send, t_recv, tx_send, tx_recv, ty_send, ty_recv, tz_send, tz_recv,
+    t_send, t_recv, tp_send, tp_recv, tz_send, tz_recv,
 ):
     res = lax.axis_index("res")
     q = lax.axis_index("seq")
@@ -128,12 +128,12 @@
     xl, c = lax.div(q, 2), lax.rem(q, 2)
     zi, parity = lax.div(z, 2), lax.rem(z, 2)
     active = parity == xl
+    inside = lax.div(y, 2) == c
     other_q = (1 - xl) * 2 + c
     plane = y * 4 + xh * 2 + xl
-    deep = z * 2 + c
-    column = lax.rem(y, 2) * 2 + xh
-    own_row = jnp.where(active, deep, -1)
-    own_column = jnp.where(lax.div(y, 2) == c, plane, -1)
+    band = lax.rem(y, 2) * 2 + xh
+    own_column = jnp.where(active, z * 2 + c, -1)
+    own_row = jnp.where(inside, plane, -1)
     other_core = device(y, z, xh, xl, 1 - c)
     partner = device(y, z, xh, 1 - xl, c)
 
@@ -147,7 +147,7 @@
                 (token_h, token), (deletion_h, deletion), (mask_h, mask), (stack_h, stack_raw),
                 (letters_h, letters), (gaps_h, gaps), (steps_h, steps), (gain_h, gain), (offset_h, offset),
                 (left_map_h, left_map), (left_bias_h, left_bias), (right_map_h, right_map),
-                (right_bias_h, right_bias), (weight_h, weight_raw),
+                (right_bias_h, right_bias), (weight_h, weight_raw), (cotangent.at[:, :, xl], cot_raw),
             ]
         )
     ]
@@ -177,40 +177,39 @@
         return device(lax.div(n, 4), z, lax.div(lax.rem(n, 4), 2), lax.rem(n, 2), lax.div(y, 2))
 
     def rm_copy(n):
-        return remote(mask_rows, row_masks.at[zi, q], rm_send.at[n], rm_recv.at[zi * 4 + q], line_user(n))
+        return remote(mask_rows, row_masks.at[band, q], rm_send.at[n], rm_recv.at[band * 4 + q], plane_user(n))
 
     def cm_copy(n):
-        return remote(mask_rows, column_masks.at[column, q], cm_send.at[n], cm_recv.at[column * 4 + q], plane_user(n))
-
-    def cot_part(n):
-        return cotangent.at[:, pl.ds(c * 2, 2), block(n, 16), :]
+        return remote(mask_rows, column_masks.at[zi, q], cm_send.at[n], cm_recv.at[zi * 4 + q], line_user(n))
 
     def cot_copy(n):
-        return remote(cot_part(n), cot_all.at[zi], cot_send.at[n], cot_recv.at[zi], device(y, n, xh, xl, c))
-
-    def left_slot(at_q, at_z):
-        return left_all.at[at_q, :, block(at_z, WIDE)]
-
-    def l1_copy():
-        return remote(left_own, left_slot(q, zi), l1_send.at[0], l1_recv.at[0], partner)
-
-    def l2_copy(n):
+        return remote(cot_stage.at[n], cot_all.at[band], cot_send.at[n], cot_recv.at[band], device(n, z, c, xl, lax.div(y, 2)))
+
+    own_cot = jnp.where(jnp.logical_and(inside, xh == c), y, -1)
+
+    def left_slot(at_band, at_q):
+        return left_all.at[at_q, :, block(at_band, WIDE)]
+
+    def l_copy(n):
+        return remote(left_own, left_slot(band, q), l_send.at[n], l_recv.at[band * 4 + q], plane_user(n))
+
+    def r1_copy():
+        return remote(right_own, right_all.at[zi, q], r1_send.at[0], r1_recv.at[0], partner)
+
+    def r2_copy(n):
         return remote(
-            left_own, left_slot(q, zi), l2_send.at[n], l2_recv.at[zi * 2 + xl], device(y, n, xh, xl, c)
+            right_own, right_all.at[zi, q], r2_send.at[n], r2_recv.at[zi * 2 + xl], device(y, n, xh, xl, c)
         )
 
-    def l2_forward(n):
+    def r2_forward(n):
         return remote(
-            left_slot(other_q, zi), left_slot(other_q, zi), l2_send.at[8 + n], l2_recv.at[zi * 2 + 1 - xl],
+            right_all.at[zi, other_q], right_all.at[zi, other_q], r2_send.at[8 + n], r2_recv.at[zi * 2 + 1 - xl],
             device(y, n, xh, xl, c),
         )
 
-    def l3_copy(n):
+    def r3_copy(n):
         at_q = n * 2 + c
-        return remote(left_all.at[at_q], left_all.at[at_q], l3_send.at[n], l3_recv.at[n], other_core)
-
-    def r_copy(n):
-        return remote(right_own, right_all.at[column, q], r_send.at[n], r_recv.at[column * 4 + q], plane_user(n))
+        return remote(right_all.at[:, at_q], right_all.at[:, at_q], r3_send.at[n], r3_recv.at[n], other_core)
 
     for load in loads[:13]:
         load.wait()
@@ -244,6 +243,11 @@
         ],
         axis=1,
     )
+    loads[14].wait()
+    for n in range(4):
+        strip = cot_raw[:, n * 4 : n * 4 + 4].astype(F32)
+        strip = jnp.where(c == 0, strip[:, :, :8, :], strip[:, :, 8:, :])
+        cot_stage[n] = strip.reshape(8, 32, 128).astype(BF16)
     lane = lanes((ROWS, 128))
     fine = lane.astype(F32)
     wide_lane = lanes((ROWS, WIDE))
@@ -282,40 +286,43 @@
         left_own[:, h * 128 : (h + 1) * 128] = left_value.astype(BF16)
         if h == 0:
             pl.semaphore_wait(barrier, 62)
+            start_all(4, cot_copy, own_cot)
             start_all(16, rm_copy, own_row)
             start_all(16, cm_copy, own_column)
 
+            @pl.when(inside)
+            def _():
+                local(mask_rows, row_masks.at[band, q], rm_recv.at[band * 4 + q]).start()
+
+            @pl.when(jnp.logical_and(inside, xh == c))
+            def _():
+                local(cot_stage.at[y], cot_all.at[band], cot_recv.at[band]).start()
+
             @pl.when(active)
             def _():
-                local(mask_rows, row_masks.at[zi, q], rm_recv.at[zi * 4 + q]).start()
-                start_all(8, cot_copy, z)
-                local(cot_part(z), cot_all.at[zi], cot_recv.at[zi]).start()
-
-            @pl.when(lax.div(y, 2) == c)
-            def _():
-                local(mask_rows, column_masks.at[column, q], cm_recv.at[column * 4 + q]).start()
+                local(mask_rows, column_masks.at[zi, q], cm_recv.at[zi * 4 + q]).start()
 
     right_own[...] = right_value.astype(BF16)
 
     @pl.when(jnp.logical_not(active))
     def _():
-        l1_copy().start()
+        r1_copy().start()
 
     @pl.when(active)
     def _():
-        start_all(8, l2_copy, z)
-        local(left_own, left_slot(q, zi), l2_recv.at[zi * 2 + xl]).start()
-
-    start_all(16, r_copy, own_column)
-
-    @pl.when(lax.div(y, 2) == c)
-    def _():
-        local(right_own, right_all.at[column, q], r_recv.at[column * 4 + q]).start()
+        start_all(8, r2_copy, z)
+        local(right_own, right_all.at[zi, q], r2_recv.at[zi * 2 + xl]).start()
+
+    start_all(16, l_copy, own_row)
+
+    @pl.when(inside)
+    def _():
+        local(left_own, left_slot(band, q), l_recv.at[band * 4 + q]).start()
 
     @pl.when(active)
     def _():
-        wait(left_own, left_slot(other_q, zi), l1_recv.at[0])
-        start_all(8, l2_forward, z)
+        wait(right_own, right_all.at[zi, other_q], r1_recv.at[0])
+        start_all(8, r2_forward, z)
 
     loads[13].wait()
     weight_wide[...] = weight_raw[...].astype(F32)
@@ -349,7 +356,7 @@
         )
         product[i * 32 : (i + 1) * 32, :] = (row * column_mask).astype(BF16)
     counts[...] = dot(product[...], jnp.ones((256, 128), BF16))
-    repeat(4, lambda n: wait(cot_part(n), cot_all.at[n], cot_recv.at[n]))
+    repeat(4, lambda n: wait(cot_stage.at[n], cot_all.at[n], cot_recv.at[n]))
     for n in range(4):
         cot = cot_all[n].astype(F32).reshape(256, 128)
         scaled[n * 256 : (n + 1) * 256, :] = (cot / counts[n * 256 : (n + 1) * 256, :]).astype(BF16)
@@ -370,34 +377,21 @@
 
     forwarded = jnp.where(active, zi * 2 + 1 - xl, -1)
 
-    def arrive_left(n):
+    def arrive_right(n):
         @pl.when(n != forwarded)
         def _():
-            wait(left_own, left_slot(lax.rem(n, 2) * 2 + c, lax.div(n, 2)), l2_recv.at[n])
-
-    repeat(8, arrive_left)
-    start_all(2, l3_copy, -1)
-    repeat(16, lambda n: wait(right_own, right_all.at[lax.div(n, 4), lax.rem(n, 4)], r_recv.at[n]))
+            wait(right_own, right_all.at[lax.div(n, 2), lax.rem(n, 2) * 2 + c], r2_recv.at[n])
+
+    repeat(8, arrive_right)
+    start_all(2, r3_copy, -1)
+    repeat(16, lambda n: wait(left_own, left_slot(lax.div(n, 4), lax.rem(n, 4)), l_recv.at[n]))
+    repeat(2, lambda n: wait(right_all.at[:, n * 2 + 1 - c], right_all.at[:, n * 2 + 1 - c], r3_recv.at[n]))
     for at_q in range(4):
         rows = slice(at_q * ROWS, (at_q + 1) * ROWS)
         for t in range(2):
             parts = [right_all[b, at_q, :, t * 128 : (t + 1) * 128].astype(F32) for b in range(4)]
             for b, part in enumerate(swap(parts, 8)):
                 right_mat[rows, (t * 4 + b) * 128 : (t * 4 + b + 1) * 128] = part.astype(BF16)
-
-    def left_step(g):
-        span = block(g, 256)
-        part = dot_nt(right_mat[...], grad_outer[span, :]).astype(BF16)
-        for at_q in range(4):
-            left_grad[at_q, :, span] = part[at_q * ROWS : (at_q + 1) * ROWS, :]
-
-    repeat(4, left_step)
-
-    def gx_copy(n):
-        return remote(left_grad.at[n * 2 + 1 - c], left_core.at[n], gx_send.at[n], gx_recv.at[n], other_core)
-
-    start_all(2, gx_copy, -1)
-    repeat(2, lambda n: wait(left_all.at[n * 2 + 1 - c], left_all.at[n * 2 + 1 - c], l3_recv.at[n]))
 
     def right_step(t):
         for b in range(2):
@@ -410,41 +404,60 @@
             for b, part in enumerate(parts):
                 right_grad[b, at_q, :, t * 128 : (t + 1) * 128] = part.astype(BF16)
 
+    def gx_copy(n):
+        return remote(right_grad.at[:, n * 2 + 1 - c], right_core.at[n], gx_send.at[n], gx_recv.at[n], other_core)
+
     right_step(0)
-
-    def gz_part(n):
-        return left_sum.at[:, :, block(n, WIDE)]
+    right_step(1)
+    start_all(2, gx_copy, -1)
+
+    def gl_part(n):
+        return left_grad.at[lax.rem(n, 4), :, block(lax.div(n, 4), WIDE)]
+
+    def gl_copy(n):
+        target = device(c * 2 + lax.div(n, 8), z, lax.rem(lax.div(n, 4), 2), lax.div(lax.rem(n, 4), 2), lax.rem(n, 2))
+        return remote(gl_part(n), left_in.at[plane], gl_send.at[n], gl_recv.at[plane], target)
+
+    own_gl = jnp.where(inside, band * 4 + q, -1)
+
+    def left_step(g):
+        span = block(g, 256)
+        part = dot_nt(right_mat[...], grad_outer[span, :]).astype(BF16)
+        for at_q in range(4):
+            left_grad[at_q, :, span] = part[at_q * ROWS : (at_q + 1) * ROWS, :]
+
+    left_step(0)
 
     def gz_copy(n):
         return remote(
-            gz_part(n), left_in.at[z], gz_send.at[n], gz_recv.at[z], device(y, n * 2 + xl, xh, xl, c)
+            right_sum.at[n], right_in.at[z], gz_send.at[n], gz_recv.at[z], device(y, n * 2 + xl, xh, xl, c)
         )
 
     own_gz = jnp.where(active, zi, -1)
     for n in range(2):
-        wait(left_core.at[n], left_core.at[n], gx_recv.at[n])
-        left_sum[n] = (left_grad[n * 2 + c].astype(F32) + left_core[n].astype(F32)).astype(BF16)
+        wait(right_core.at[n], right_core.at[n], gx_recv.at[n])
+        for b in range(4):
+            right_sum[b, n] = (right_grad[b, n * 2 + c].astype(F32) + right_core[n, b].astype(F32)).astype(BF16)
     start_all(4, gz_copy, own_gz)
 
     @pl.when(active)
     def _():
-        local(gz_part(zi), left_in.at[z], gz_recv.at[z]).start()
-
-    right_step(1)
-
-    def gr_part(n):
-        return right_grad.at[lax.div(n, 4), lax.rem(n, 4)]
-
-    def gr_copy(n):
-        target = device(c * 2 + lax.div(n, 8), z, lax.rem(lax.div(n, 4), 2), lax.div(lax.rem(n, 4), 2), lax.rem(n, 2))
-        return remote(gr_part(n), right_in.at[plane], gr_send.at[n], gr_recv.at[plane], target)
-
-    own_gr = jnp.where(lax.div(y, 2) == c, column * 4 + q, -1)
-    start_all(16, gr_copy, own_gr)
-
-    @pl.when(lax.div(y, 2) == c)
-    def _():
-        local(gr_part(column * 4 + q), right_in.at[plane], gr_recv.at[plane]).start()
+        local(right_sum.at[zi], right_in.at[z], gz_recv.at[z]).start()
+
+    for g in range(4):
+        if g > 0:
+            left_step(g)
+
+        def start_left(n):
+            @pl.when(n + g * 4 != own_gl)
+            def _():
+                gl_copy(n + g * 4).start()
+
+        repeat(4, start_left)
+
+    @pl.when(inside)
+    def _():
+        local(gl_part(band * 4 + q), left_in.at[plane], gl_recv.at[plane]).start()
 
     def forward(g):
         span = block(g, 128)
@@ -503,47 +516,44 @@
     local(wa_part(plane), weight_in.at[plane], wa_recv.at[plane]).start()
 
     def pair_part(n):
-        return pair.at[block(lax.div(n, 2), 8), block(lax.rem(n, 2), 16), :]
-
-    def pair_slot(n):
-        return pair_out.at[:, block(n, 16), :]
+        return pair.at[block(n, 8)]
 
     def pair_copy(n):
-        target = device(y, lax.div(n, 2) * 2 + xl, xh, c, lax.rem(n, 2))
-        return remote(pair_part(n), pair_slot(z), pair_send.at[n], pair_recv.at[z], target)
-
-    keeps_pair = jnp.logical_and(active, xl == c)
-    own_pair = jnp.where(keeps_pair, zi * 2 + c, -1)
-    start_all(8, pair_copy, own_pair)
+        target = device(c * 2 + lax.div(n, 2), z, lax.rem(n, 2), lax.div(y, 2), lax.rem(y, 2))
+        return remote(pair_part(n), pair_in.at[xh * 2 + xl], pair_send.at[n], pair_recv.at[xh * 2 + xl], target)
+
+    keeps_pair = jnp.logical_and(inside, q == y)
+    own_pair = jnp.where(keeps_pair, band, -1)
+    start_all(4, pair_copy, own_pair)
 
     @pl.when(keeps_pair)
     def _():
-        local(pair_part(zi * 2 + c), pair_slot(z), pair_recv.at[z]).start()
-
-    def gl_copy():
-        return remote(left_send, left_last, gl_send.at[0], gl_recv.at[0], partner)
+        local(pair_part(band), pair_in.at[xh * 2 + xl], pair_recv.at[xh * 2 + xl]).start()
+
+    def gf_copy():
+        return remote(right_send, right_last, gf_send.at[0], gf_recv.at[0], partner)
 
     @pl.when(active)
     def _():
-        repeat(8, lambda n: wait(gz_part(0), left_in.at[n], gz_recv.at[n]))
-        away = left_in[0, 1 - xl].astype(F32)
+        repeat(8, lambda n: wait(right_in.at[n], right_in.at[n], gz_recv.at[n]))
+        away = right_in[0, 1 - xl].astype(F32)
         for n in range(1, 8):
-            away = away + left_in[n, 1 - xl].astype(F32)
-        left_send[...] = away.astype(BF16)
-        gl_copy().start()
-        here = left_in[0, xl].astype(F32)
+            away = away + right_in[n, 1 - xl].astype(F32)
+        right_send[...] = away.astype(BF16)
+        gf_copy().start()
+        here = right_in[0, xl].astype(F32)
         for n in range(1, 8):
-            here = here + left_in[n, xl].astype(F32)
-        left_last[...] = here.astype(BF16)
-
-    repeat(16, lambda n: wait(right_in.at[n], right_in.at[n], gr_recv.at[n]))
-    right_total = total(right_in, 16).astype(BF16).astype(F32)
+            here = here + right_in[n, xl].astype(F32)
+        right_last[...] = here.astype(BF16)
+
+    repeat(16, lambda n: wait(left_in.at[n], left_in.at[n], gl_recv.at[n]))
+    left_total = total(left_in, 16).astype(BF16).astype(F32)
 
     @pl.when(jnp.logical_not(active))
     def _():
-        wait(left_last, left_last, gl_recv.at[0])
-
-    left_total = left_last[...].astype(F32)
+        wait(right_last, right_last, gf_recv.at[0])
+
+    right_total = right_last[...].astype(F32)
 
     repeat(16, lambda n: wait(weight_in.at[n], weight_in.at[n], wa_recv.at[n]))
     weight_sum[...] = total(weight_in, 16).astype(BF16)
@@ -581,16 +591,8 @@
     def t_copy():
         return remote(table_part.at[pl.ds((1 - c) * 3, 3)], table_core, t_send.at[0], t_recv.at[0], other_core)
 
-    at_x = xh * 2 + xl
-
-    def tx_copy(n):
-        return remote(
-            table_x.at[at_x], table_x.at[at_x], tx_send.at[n], tx_recv.at[at_x],
-            device(y, z, lax.div(n, 2), lax.rem(n, 2), c),
-        )
-
-    def ty_copy(n):
-        return remote(table_y.at[y], table_y.at[y], ty_send.at[n], ty_recv.at[y], device(n, z, xh, xl, c))
+    def tp_copy(n):
+        return remote(table_p.at[plane], table_p.at[plane], tp_send.at[n], tp_recv.at[plane], plane_peer(n))
 
     def tz_copy(n):
         return remote(table_z.at[z], table_z.at[z], tz_send.at[n], tz_recv.at[z], device(y, n, xh, xl, c))
@@ -611,19 +613,23 @@
 
     t_copy().start()
     wait(table_core, table_core, t_recv.at[0])
-    table_x[at_x] = table_part[pl.ds(c * 3, 3)] + table_core[...]
-    start_all(4, tx_copy, at_x)
+    table_p[plane] = table_part[pl.ds(c * 3, 3)] + table_core[...]
+    start_all(16, tp_copy, plane)
 
     repeat(8, lambda n: wait(weight_far.at[n], weight_far.at[n], wb_recv.at[n]))
     weight_total[...] = total(weight_far, 8).astype(BF16)
     start_all(16, wc_copy, plane)
     local(weight_total, wc_slot(plane), wc_recv.at[plane]).start()
 
-    arrive(4, table_x, tx_recv, at_x)
-    table_y[y] = total(table_x, 4)
-    start_all(4, ty_copy, y)
-    arrive(4, table_y, ty_recv, y)
-    table_z[z] = total(table_y, 4)
+    repeat(4, lambda n: wait(pair_part(n), pair_in.at[n], pair_recv.at[n]))
+    for at_z in range(8):
+        run = [
+            pair_in[at_x * 2 + at_z % 2, :, (at_z // 2) * 8 : (at_z // 2 + 1) * 8, :].astype(F32) for at_x in range(2)
+        ]
+        pair_out[:, at_z * 16 : (at_z + 1) * 16, :] = jnp.concatenate(run, axis=1).astype(BF16)
+
+    arrive(16, table_p, tp_recv, plane)
+    table_z[z] = total(table_p, 16)
     start_all(8, tz_copy, z)
 
     repeat(16, lambda n: wait(weight_total, wc_slot(n), wc_recv.at[n]))
@@ -634,7 +640,6 @@
     table_half[...] = summed
     t_last().start()
     table_all[pl.ds(c * 3, 3)] = summed
-    repeat(8, lambda n: wait(pair_slot(n), pair_slot(n), pair_recv.at[n]))
     wait(table_half, half(1 - c), t_recv.at[1])
     for n in range(TILES):
         high = min(8, table_out.shape[0] - (n // 2) * 8)
@@ -648,33 +653,32 @@
 
     sent_all(16, rm_copy, own_row)
     sent_all(16, cm_copy, own_column)
-    sent_all(16, r_copy, own_column)
-    sent_all(16, gr_copy, own_gr)
-    sent_all(2, l3_copy, -1)
+    sent_all(4, cot_copy, own_cot)
+    sent_all(16, l_copy, own_row)
+    sent_all(2, r3_copy, -1)
     sent_all(2, gx_copy, -1)
     sent_all(4, gz_copy, own_gz)
+    sent_all(16, gl_copy, own_gl)
     sent_all(16, wa_copy, plane)
     sent_all(8, wb_copy, z)
+    sent_all(16, wc_copy, plane)
     wh_copy().wait_send()
     wd_copy().wait_send()
-    sent_all(16, wc_copy, plane)
-    sent_all(8, pair_copy, own_pair)
-    sent_all(4, tx_copy, at_x)
-    sent_all(4, ty_copy, y)
+    sent_all(4, pair_copy, own_pair)
+    sent_all(16, tp_copy, plane)
     sent_all(8, tz_copy, z)
     t_copy().wait_send()
     t_last().wait_send()
 
     @pl.when(active)
     def _():
-        sent_all(8, cot_copy, z)
-        sent_all(8, l2_copy, z)
-        sent_all(8, l2_forward, z)
-        gl_copy().wait_send()
+        sent_all(8, r2_copy, z)
+        sent_all(8, r2_forward, z)
+        gf_copy().wait_send()
 
     @pl.when(jnp.logical_not(active))
     def _():
-        l1_copy().wait_send()
+        r1_copy().wait_send()
 
 
 def shape(dims, dtype=BF16):
@@ -701,6 +705,7 @@
     ]
     vmem = pltpu.VMEM
     scratch = [vmem(value.shape, value.dtype) for value in inputs] + [
+        vmem((8, 16, 16, 128), BF16), vmem((4, 8, 32, 128), BF16),
         vmem((128, 128), F32), vmem((ROWS, 128), F32), vmem((8, 128), F32),
         vmem((2, 512, 128), F32),
         vmem((128, WIDE), F32), vmem((384, 256), BF16), vmem((8, 384), F32),
@@ -709,24 +714,25 @@
         vmem((512, 256), F32), vmem((512, 128), F32),
         vmem((ROWS, WIDE), BF16), vmem((ROWS, WIDE), BF16),
         vmem((4, 4, 8, 128), F32), vmem((4, 4, 8, 128), F32),
-        vmem((4, 8, 2, 16, 128), BF16),
+        vmem((4, 8, 32, 128), BF16),
         vmem((4, ROWS, 1024), BF16), vmem((4, 4, ROWS, WIDE), BF16),
         vmem((256, 1024), BF16), vmem((1024, 256), BF16),
         vmem((1024, 128), F32), vmem((1024, 128), BF16),
         vmem((1024, 1024), BF16), vmem((1024, 1024), BF16),
-        vmem((32, 32, 128), BF16),
-        vmem((4, ROWS, 1024), BF16), vmem((2, ROWS, 1024), BF16), vmem((2, ROWS, 1024), BF16),
-        vmem((8, 2, ROWS, WIDE), BF16), vmem((ROWS, WIDE), BF16), vmem((ROWS, WIDE), BF16),
-        vmem((4, 4, ROWS, WIDE), BF16), vmem((256, 512), F32), vmem((16, ROWS, WIDE), BF16),
+        vmem((32, 32, 128), BF16), vmem((4, 8, 32, 128), BF16),
+        vmem((4, 4, ROWS, WIDE), BF16), vmem((256, 512), F32), vmem((2, 4, ROWS, WIDE), BF16),
+        vmem((4, 2, ROWS, WIDE), BF16), vmem((8, 2, ROWS, WIDE), BF16),
+        vmem((ROWS, WIDE), BF16), vmem((ROWS, WIDE), BF16),
+        vmem((4, ROWS, 1024), BF16), vmem((16, ROWS, WIDE), BF16),
         vmem((1024, 128), F32), vmem((512, 128), F32), vmem((512, 128), BF16),
         vmem((16, 32, 128), BF16), vmem((32, 128), BF16),
         vmem((8, 32, 128), BF16), vmem((32, 128), BF16), vmem((2, 512, 128), BF16),
         vmem((TILES, 8, 128), F32), vmem((3, 8, 128), F32),
-        vmem((4, 3, 8, 128), F32), vmem((4, 3, 8, 128), F32), vmem((8, 3, 8, 128), F32),
+        vmem((16, 3, 8, 128), F32), vmem((8, 3, 8, 128), F32),
         vmem((3, 8, 128), F32), vmem((TILES, 8, 128), F32),
     ]
-    sizes = [len(inputs), 16, 16, 16, 16, 8, 4, 1, 1, 16, 8, 2, 2, 16, 16]
-    sizes += [2, 2, 4, 8, 1, 1, 16, 16, 8, 8, 2, 2, 16, 16, 8, 8, 16, 16, 2, 2, 4, 4, 4, 4, 8, 8]
+    sizes = [len(inputs) + 1, 16, 16, 16, 16, 4, 4, 1, 1, 16, 8, 2, 2, 16, 16]
+    sizes += [2, 2, 4, 8, 1, 1, 16, 16, 4, 4, 2, 2, 16, 16, 8, 8, 16, 16, 2, 2, 16, 16, 8, 8]
     results = pl.pallas_call(
         kernel,
         out_shape=[shape((8, 128, 128)), shape((1024, 128), F32), shape((kinds, 256), F32)],
@@ -737,7 +743,7 @@
             collective_id=0, has_side_effects=True, vmem_limit_bytes=60 * 1024 * 1024
         ),
         name="outer_product_mean",
-    )(*inputs, cotangent.reshape(8, 4, 128, 128))
+    )(*inputs, cotangent.reshape(8, 16, 2, 16, 128))
     return pl.pallas_call(
         hand_over,
         out_shape=[shape(value.shape, value.dtype) for value in results],

time: 79.5 us -> 69.2 us (0.87)
  Pallas kernels: 78.8 us -> 68.4 us
    pallas_call x1, Pallas kernels: 76.8 us -> 66.5 us  [body(): pl.pallas_call(kernel, out_shape=[shape((8, 128, 128)), shape((1024, 128)...]
where the time goes in v4:
time: 69.2 us; the launch traced here: 69.1 us
  Pallas kernels  68.4 us (99%)
    pallas_call x1, Pallas kernels, body(): pl.pallas_call(kernel, out_shape=[shape((8, 128, 128)), shape((1024, 128)...  66.5 us
    pallas_call x1, Pallas kernels, body(): pl.pallas_call(hand_over, out_shape=[shape(value.shape, value.dtype) for...  1.94 us

profile of v4, /device:TPU:1, one launch (start us, length us, event | category | flops | bytes accessed | tf_op | source)
XLA Modules:
  0.0 69.1 jit_solution(2241348788064745706)
XLA Ops:
  0.6 66.5 %outer_product_mean.1 = (bf16[8,128,128]{2,1,0:T(8,128)(2,1)}, f32[1024,128]{1,0:T(8,128)}, f32[23,256]{1,0:T(8,128)}) custom-call(s32[8,64]{1,0:T(8,128)} %bitcast.13, s32[8,64]{1,0:T(8,128)} %bitcast.14, s32[8,64]{1,0:T(8,128)} %bitcast.15, bf16[64,8,256]{2,1,0:T(8,128)(2,1)} %stack_h.1, f32[23,256]{1,0:T(8,128)} %letters_h.1, f32[2,256]{1,0:T(2,128)} %gaps_h.1, ...), custom_call_target="tpu_custom_call" | custom-call | tf_op jit(solution)/shard_map/outer_product_mean/pallas_call | solution.py:736
  67.1 1.9 %hand_over.1 = (bf16[8,128,128]{2,1,0:T(8,128)(2,1)}, f32[1024,128]{1,0:T(8,128)}, f32[23,256]{1,0:T(8,128)}) custom-call(bf16[8,128,128]{2,1,0:T(8,128)(2,1)} %get-tuple-element.6.pair, f32[1024,128]{1,0:T(8,128)} %get-tuple-element.7.weight, f32[23,256]{1,0:T(8,128)} %get-tuple-element.8.table), custom_call_target="tpu_custom_call" | custom-call | tf_op jit(solution)/shard_map/hand_over/pallas_call | solution.py:747

commit v5 on v4

--- a/solution.py
+++ b/solution.py
@@ -107,16 +107,16 @@
 def kernel(
     token_h, deletion_h, mask_h, stack_h, letters_h, gaps_h, steps_h, gain_h, offset_h,
     left_map_h, left_bias_h, right_map_h, right_bias_h, weight_h, cotangent,
-    pair_out, weight_out, table_out,
+    pair_h, weight_grad_h, table_out,
     token, deletion, mask, stack_raw, letters, gaps, steps, gain, offset,
     left_map, left_bias, right_map, right_bias, weight_raw, cot_raw, cot_stage,
     square, turned, mask_rows, stack, table, maps, bias, weight_wide, weight, weight_turned, hot_turned,
     white, spread, left_own, right_own, row_masks, column_masks, cot_all, left_all, right_all,
-    right_mat, product, counts, scaled, folded, grad_outer, pair, pair_in,
+    right_mat, wide_grad, wide_outer, product, counts, scaled, folded, grad_outer, pair, pair_in,
     right_grad, right_part, right_core, right_sum, right_in, right_last, right_send, left_grad, left_in,
     weight_grad, weight_core, weight_half, weight_in, weight_sum, weight_far, weight_total, weight_all,
-    table_part, table_core, table_p, table_z, table_half, table_all,
-    in_sem, rm_send, rm_recv, cm_send, cm_recv, cot_send, cot_recv,
+    table_part, table_core, table_p, table_z, table_half, table_all, pair_out, weight_out,
+    in_sem, out_sem, rm_send, rm_recv, cm_send, cm_recv, cot_send, cot_recv,
     r1_send, r1_recv, r2_send, r2_recv, r3_send, r3_recv, l_send, l_recv,
     gx_send, gx_recv, gz_send, gz_recv, gf_send, gf_recv, gl_send, gl_recv, pair_send, pair_recv,
     wh_send, wh_recv, wa_send, wa_recv, wb_send, wb_recv, wc_send, wc_recv,
@@ -363,35 +363,16 @@
 
     def backward(g):
         span = block(g, 256)
-        scaled_part = scaled[span, :]
+        wide_grad[...] = dot_nt(weight[...], scaled[span, :])
         for t in range(8):
-            grad = dot_nt(weight[t * 128 : (t + 1) * 128, :], scaled_part)
             for half in range(2):
-                lane_part = grad[:, half * 128 : (half + 1) * 128]
+                lane_part = wide_grad[t * 128 : (t + 1) * 128, half * 128 : (half + 1) * 128]
                 parts = swap([lane_part[a * 32 : (a + 1) * 32, :] for a in range(4)], 32)
                 for i, part in enumerate(parts):
                     at = pl.ds(pl.multiple_of(g * 256 + half * 128 + i * 32, 32), 32)
                     grad_outer[at, t * 128 : (t + 1) * 128] = part.astype(BF16)
 
     repeat(4, backward)
-
-    forwarded = jnp.where(active, zi * 2 + 1 - xl, -1)
-
-    def arrive_right(n):
-        @pl.when(n != forwarded)
-        def _():
-            wait(right_own, right_all.at[lax.div(n, 2), lax.rem(n, 2) * 2 + c], r2_recv.at[n])
-
-    repeat(8, arrive_right)
-    start_all(2, r3_copy, -1)
-    repeat(16, lambda n: wait(left_own, left_slot(lax.div(n, 4), lax.rem(n, 4)), l_recv.at[n]))
-    repeat(2, lambda n: wait(right_all.at[:, n * 2 + 1 - c], right_all.at[:, n * 2 + 1 - c], r3_recv.at[n]))
-    for at_q in range(4):
-        rows = slice(at_q * ROWS, (at_q + 1) * ROWS)
-        for t in range(2):
-            parts = [right_all[b, at_q, :, t * 128 : (t + 1) * 128].astype(F32) for b in range(4)]
-            for b, part in enumerate(swap(parts, 8)):
-                right_mat[rows, (t * 4 + b) * 128 : (t * 4 + b + 1) * 128] = part.astype(BF16)
 
     def right_step(t):
         for b in range(2):
@@ -407,27 +388,20 @@
     def gx_copy(n):
         return remote(right_grad.at[:, n * 2 + 1 - c], right_core.at[n], gx_send.at[n], gx_recv.at[n], other_core)
 
+    repeat(16, lambda n: wait(left_own, left_slot(lax.div(n, 4), lax.rem(n, 4)), l_recv.at[n]))
     right_step(0)
     right_step(1)
     start_all(2, gx_copy, -1)
 
-    def gl_part(n):
-        return left_grad.at[lax.rem(n, 4), :, block(lax.div(n, 4), WIDE)]
-
-    def gl_copy(n):
-        target = device(c * 2 + lax.div(n, 8), z, lax.rem(lax.div(n, 4), 2), lax.div(lax.rem(n, 4), 2), lax.rem(n, 2))
-        return remote(gl_part(n), left_in.at[plane], gl_send.at[n], gl_recv.at[plane], target)
-
-    own_gl = jnp.where(inside, band * 4 + q, -1)
-
-    def left_step(g):
-        span = block(g, 256)
-        part = dot_nt(right_mat[...], grad_outer[span, :]).astype(BF16)
-        for at_q in range(4):
-            left_grad[at_q, :, span] = part[at_q * ROWS : (at_q + 1) * ROWS, :]
-
-    left_step(0)
-
+    forwarded = jnp.where(active, zi * 2 + 1 - xl, -1)
+
+    def arrive_right(n):
+        @pl.when(n != forwarded)
+        def _():
+            wait(right_own, right_all.at[lax.div(n, 2), lax.rem(n, 2) * 2 + c], r2_recv.at[n])
+
+    repeat(8, arrive_right)
+    start_all(2, r3_copy, -1)
     def gz_copy(n):
         return remote(
             right_sum.at[n], right_in.at[z], gz_send.at[n], gz_recv.at[z], device(y, n * 2 + xl, xh, xl, c)
@@ -444,9 +418,32 @@
     def _():
         local(right_sum.at[zi], right_in.at[z], gz_recv.at[z]).start()
 
+    repeat(2, lambda n: wait(right_all.at[:, n * 2 + 1 - c], right_all.at[:, n * 2 + 1 - c], r3_recv.at[n]))
+    for at_q in range(4):
+        rows = slice(at_q * ROWS, (at_q + 1) * ROWS)
+        for t in range(2):
+            parts = [right_all[b, at_q, :, t * 128 : (t + 1) * 128].astype(F32) for b in range(4)]
+            for b, part in enumerate(swap(parts, 8)):
+                right_mat[rows, (t * 4 + b) * 128 : (t * 4 + b + 1) * 128] = part.astype(BF16)
+
+
+    def gl_part(n):
+        return left_grad.at[lax.rem(n, 4), :, block(lax.div(n, 4), WIDE)]
+
+    def gl_copy(n):
+        target = device(c * 2 + lax.div(n, 8), z, lax.rem(lax.div(n, 4), 2), lax.div(lax.rem(n, 4), 2), lax.rem(n, 2))
+        return remote(gl_part(n), left_in.at[plane], gl_send.at[n], gl_recv.at[plane], target)
+
+    own_gl = jnp.where(inside, band * 4 + q, -1)
+
+    def left_step(g):
+        span = block(g, 256)
+        part = dot_nt(right_mat[...], grad_outer[span, :]).astype(BF16)
+        for at_q in range(4):
+            left_grad[at_q, :, span] = part[at_q * ROWS : (at_q + 1) * ROWS, :]
+
     for g in range(4):
-        if g > 0:
-            left_step(g)
+        left_step(g)
 
         def start_left(n):
             @pl.when(n + g * 4 != own_gl)
@@ -460,26 +457,24 @@
         local(gl_part(band * 4 + q), left_in.at[plane], gl_recv.at[plane]).start()
 
     def forward(g):
-        span = block(g, 128)
-        lead = left_all[:, :, span].reshape(256, 128).astype(F32).T.astype(BF16)
-        for t in range(8):
-            outer = dot(lead, right_mat[:, t * 128 : (t + 1) * 128])
-            parts = swap([outer[i * 32 : (i + 1) * 32, :] for i in range(4)], 32)
-            for a, part in enumerate(parts):
-                folded[(t * 4 + a) * 32 : (t * 4 + a + 1) * 32, span] = part.astype(BF16)
-
-    def weigh(g):
-        span = block(g, 128)
-        weight_grad[span, :] = dot(folded[span, :], scaled[...])
+        lead = left_all[:, :, block(g, 256)].reshape(256, 256).astype(F32).T.astype(BF16)
+        wide_outer[...] = dot(lead, right_mat[...])
+        for half in range(2):
+            span = pl.ds(pl.multiple_of(g * 256 + half * 128, 128), 128)
+            for t in range(8):
+                tile = wide_outer[half * 128 : (half + 1) * 128, t * 128 : (t + 1) * 128]
+                parts = swap([tile[i * 32 : (i + 1) * 32, :] for i in range(4)], 32)
+                for a, part in enumerate(parts):
+                    folded[(t * 4 + a) * 32 : (t * 4 + a + 1) * 32, span] = part.astype(BF16)
 
     def project(g):
-        span = block(g, 128)
+        span = block(g, 256)
         value = dot(weight_turned[...], folded[:, span])
         update = (value.T / counts[span, :]).astype(BF16)
-        pair[block(g, 4)] = update.reshape(4, 32, 128)
-
-    repeat(8, forward)
-    repeat(8, weigh)
+        pair[block(g, 8)] = update.reshape(8, 32, 128)
+
+    repeat(4, forward)
+    weight_grad[...] = dot(folded[...], scaled[...])
 
     def plane_peer(n):
         return device(lax.div(n, 4), z, lax.div(lax.rem(n, 4), 2), lax.rem(n, 2), c)
@@ -509,7 +504,7 @@
         return remote(weight_all.at[c], weight_all.at[c], wh_send.at[1], wh_recv.at[1], other_core)
 
     wh_copy().start()
-    repeat(8, project)
+    repeat(4, project)
     wait(weight_core, weight_core, wh_recv.at[0])
     weight_half[...] = (weight_grad[block(c, 512), :] + weight_core[...]).astype(BF16)
     start_all(16, wa_copy, plane)
@@ -627,29 +622,19 @@
             pair_in[at_x * 2 + at_z % 2, :, (at_z // 2) * 8 : (at_z // 2 + 1) * 8, :].astype(F32) for at_x in range(2)
         ]
         pair_out[:, at_z * 16 : (at_z + 1) * 16, :] = jnp.concatenate(run, axis=1).astype(BF16)
+    local(pair_out, pair_h, out_sem.at[0]).start()
 
     arrive(16, table_p, tp_recv, plane)
     table_z[z] = total(table_p, 16)
     start_all(8, tz_copy, z)
 
+    def lay_out(at_c):
+        for n in range(16):
+            first = at_c * 16 + n % 4 * 4 + n // 4
+            weight_out[pl.ds(first, 32, stride=32), :] = weight_all[at_c, n * 32 : (n + 1) * 32, :].astype(F32)
+
     repeat(16, lambda n: wait(weight_total, wc_slot(n), wc_recv.at[n]))
     wd_copy().start()
-
-    arrive(8, table_z, tz_recv, z)
-    summed = total(table_z, 8)
-    table_half[...] = summed
-    t_last().start()
-    table_all[pl.ds(c * 3, 3)] = summed
-    wait(table_half, half(1 - c), t_recv.at[1])
-    for n in range(TILES):
-        high = min(8, table_out.shape[0] - (n // 2) * 8)
-        table_out[(n // 2) * 8 : (n // 2) * 8 + high, (n % 2) * 128 : (n % 2 + 1) * 128] = table_all[n][:high]
-    wait(weight_all.at[1 - c], weight_all.at[1 - c], wh_recv.at[1])
-    for t in range(2):
-        for b in range(4):
-            for a in range(4):
-                at = ((t * 4 + b) * 4 + a) * 32
-                weight_out[pl.ds(t * 16 + a * 4 + b, 32, stride=32), :] = weight_all[at // 512, at % 512 : at % 512 + 32, :].astype(F32)
 
     sent_all(16, rm_copy, own_row)
     sent_all(16, cm_copy, own_column)
@@ -661,14 +646,9 @@
     sent_all(16, gl_copy, own_gl)
     sent_all(16, wa_copy, plane)
     sent_all(8, wb_copy, z)
-    sent_all(16, wc_copy, plane)
+    sent_all(4, pair_copy, own_pair)
     wh_copy().wait_send()
-    wd_copy().wait_send()
-    sent_all(4, pair_copy, own_pair)
-    sent_all(16, tp_copy, plane)
-    sent_all(8, tz_copy, z)
     t_copy().wait_send()
-    t_last().wait_send()
 
     @pl.when(active)
     def _():
@@ -679,6 +659,28 @@
     @pl.when(jnp.logical_not(active))
     def _():
         r1_copy().wait_send()
+
+    wait(weight_all.at[1 - c], weight_all.at[1 - c], wh_recv.at[1])
+    for at_c in range(2):
+        lay_out(at_c)
+    local(weight_out, weight_grad_h, out_sem.at[1]).start()
+    sent_all(16, wc_copy, plane)
+    sent_all(16, tp_copy, plane)
+    wd_copy().wait_send()
+
+    arrive(8, table_z, tz_recv, z)
+    summed = total(table_z, 8)
+    table_half[...] = summed
+    t_last().start()
+    table_all[pl.ds(c * 3, 3)] = summed
+    sent_all(8, tz_copy, z)
+    wait(table_half, half(1 - c), t_recv.at[1])
+    for n in range(TILES):
+        high = min(8, table_out.shape[0] - (n // 2) * 8)
+        table_out[(n // 2) * 8 : (n // 2) * 8 + high, (n % 2) * 128 : (n % 2 + 1) * 128] = table_all[n][:high]
+    t_last().wait_send()
+    wait(pair_out, pair_h, out_sem.at[0])
+    wait(weight_out, weight_grad_h, out_sem.at[1])
 
 
 def shape(dims, dtype=BF16):
@@ -716,7 +718,8 @@
         vmem((4, 4, 8, 128), F32), vmem((4, 4, 8, 128), F32),
         vmem((4, 8, 32, 128), BF16),
         vmem((4, ROWS, 1024), BF16), vmem((4, 4, ROWS, WIDE), BF16),
-        vmem((256, 1024), BF16), vmem((1024, 256), BF16),
+        vmem((256, 1024), BF16), vmem((1024, 256), F32), vmem((256, 1024), F32),
+        vmem((1024, 256), BF16),
         vmem((1024, 128), F32), vmem((1024, 128), BF16),
         vmem((1024, 1024), BF16), vmem((1024, 1024), BF16),
         vmem((32, 32, 128), BF16), vmem((4, 8, 32, 128), BF16),
@@ -730,14 +733,15 @@
         vmem((TILES, 8, 128), F32), vmem((3, 8, 128), F32),
         vmem((16, 3, 8, 128), F32), vmem((8, 3, 8, 128), F32),
         vmem((3, 8, 128), F32), vmem((TILES, 8, 128), F32),
+        vmem((8, 128, 128), BF16), vmem((1024, 128), F32),
     ]
-    sizes = [len(inputs) + 1, 16, 16, 16, 16, 4, 4, 1, 1, 16, 8, 2, 2, 16, 16]
+    sizes = [len(inputs) + 1, 2, 16, 16, 16, 16, 4, 4, 1, 1, 16, 8, 2, 2, 16, 16]
     sizes += [2, 2, 4, 8, 1, 1, 16, 16, 4, 4, 2, 2, 16, 16, 8, 8, 16, 16, 2, 2, 16, 16, 8, 8]
     results = pl.pallas_call(
         kernel,
         out_shape=[shape((8, 128, 128)), shape((1024, 128), F32), shape((kinds, 256), F32)],
         in_specs=[pl.BlockSpec(memory_space=pl.ANY)] * (len(inputs) + 1),
-        out_specs=[pl.BlockSpec(memory_space=pltpu.VMEM)] * 3,
+        out_specs=[pl.BlockSpec(memory_space=pl.ANY)] * 2 + [pl.BlockSpec(memory_space=pltpu.VMEM)],
         scratch_shapes=scratch + [pltpu.SemaphoreType.DMA((size,)) for size in sizes],
         compiler_params=pltpu.CompilerParams(
             collective_id=0, has_side_effects=True, vmem_limit_bytes=60 * 1024 * 1024

time: 69.2 us -> 62.7 us (0.906)
  Pallas kernels: 68.4 us -> 62 us
    pallas_call x1, Pallas kernels: 66.5 us -> 60 us  [body(): pl.pallas_call(kernel, out_shape=[shape((8, 128, 128)), shape((1024, 128)...]
where the time goes in v5:
time: 62.7 us; the launch traced here: 62.6 us
  Pallas kernels  62 us (99%)
  between operations  0.64 us (1%)
    pallas_call x1, Pallas kernels, body(): pl.pallas_call(kernel, out_shape=[shape((8, 128, 128)), shape((1024, 128)...  60 us
    pallas_call x1, Pallas kernels, body(): pl.pallas_call(hand_over, out_shape=[shape(value.shape, value.dtype) for...  1.94 us

profile of v5, /device:TPU:1, one launch (start us, length us, event | category | flops | bytes accessed | tf_op | source)
XLA Modules:
  0.0 62.6 jit_solution(10992513665063422158)
XLA Ops:
  0.6 60.0 %outer_product_mean.1 = (bf16[8,128,128]{2,1,0:T(8,128)(2,1)}, f32[1024,128]{1,0:T(8,128)}, f32[23,256]{1,0:T(8,128)}) custom-call(s32[8,64]{1,0:T(8,128)} %bitcast.13, s32[8,64]{1,0:T(8,128)} %bitcast.14, s32[8,64]{1,0:T(8,128)} %bitcast.15, bf16[64,8,256]{2,1,0:T(8,128)(2,1)} %stack_h.1, f32[23,256]{1,0:T(8,128)} %letters_h.1, f32[2,256]{1,0:T(2,128)} %gaps_h.1, ...), custom_call_target="tpu_custom_call" | custom-call | tf_op jit(solution)/shard_map/outer_product_mean/pallas_call | solution.py:740
  60.7 1.9 %hand_over.1 = (bf16[8,128,128]{2,1,0:T(8,128)(2,1)}, f32[1024,128]{1,0:T(8,128)}, f32[23,256]{1,0:T(8,128)}) custom-call(bf16[8,128,128]{2,1,0:T(8,128)(2,1)} %get-tuple-element.6.pair, f32[1024,128]{1,0:T(8,128)} %get-tuple-element.7.weight, f32[23,256]{1,0:T(8,128)} %get-tuple-element.8.table), custom_call_target="tpu_custom_call" | custom-call | tf_op jit(solution)/shard_map/hand_over/pallas_call | solution.py:751

commit v6 on v5

--- a/solution.py
+++ b/solution.py
@@ -41,17 +41,23 @@
     repeat(count, step)
 
 
-def sent_all(count, copy, own):
-    def step(n):
-        @pl.when(n != own)
-        def _():
-            copy(n).wait_send()
-
-    repeat(count, step)
-
-
 def local(src, dst, sem):
     return pltpu.make_async_copy(src, dst, sem)
+
+
+def drain(sem, gauge, count):
+    part = gauge.at[pl.ds(0, count)]
+    local(part, part, sem).wait()
+
+
+def sent(sem, gauge, count, own, unit=1):
+    @pl.when(own >= 0)
+    def _():
+        drain(sem, gauge, count - unit)
+
+    @pl.when(own < 0)
+    def _():
+        drain(sem, gauge, count)
 
 
 def lanes(dims):
@@ -116,6 +122,7 @@
     right_grad, right_part, right_core, right_sum, right_in, right_last, right_send, left_grad, left_in,
     weight_grad, weight_core, weight_half, weight_in, weight_sum, weight_far, weight_total, weight_all,
     table_part, table_core, table_p, table_z, table_half, table_all, pair_out, weight_out,
+    gauge, gauge_m, gauge_w, gauge_t,
     in_sem, out_sem, rm_send, rm_recv, cm_send, cm_recv, cot_send, cot_recv,
     r1_send, r1_recv, r2_send, r2_recv, r3_send, r3_recv, l_send, l_recv,
     gx_send, gx_recv, gz_send, gz_recv, gf_send, gf_recv, gl_send, gl_recv, pair_send, pair_recv,
@@ -177,13 +184,13 @@
         return device(lax.div(n, 4), z, lax.div(lax.rem(n, 4), 2), lax.rem(n, 2), lax.div(y, 2))
 
     def rm_copy(n):
-        return remote(mask_rows, row_masks.at[band, q], rm_send.at[n], rm_recv.at[band * 4 + q], plane_user(n))
+        return remote(mask_rows, row_masks.at[band, q], rm_send, rm_recv, plane_user(n))
 
     def cm_copy(n):
-        return remote(mask_rows, column_masks.at[zi, q], cm_send.at[n], cm_recv.at[zi * 4 + q], line_user(n))
+        return remote(mask_rows, column_masks.at[zi, q], cm_send, cm_recv, line_user(n))
 
     def cot_copy(n):
-        return remote(cot_stage.at[n], cot_all.at[band], cot_send.at[n], cot_recv.at[band], device(n, z, c, xl, lax.div(y, 2)))
+        return remote(cot_stage.at[n], cot_all.at[band], cot_send, cot_recv, device(n, z, c, xl, lax.div(y, 2)))
 
     own_cot = jnp.where(jnp.logical_and(inside, xh == c), y, -1)
 
@@ -191,25 +198,25 @@
         return left_all.at[at_q, :, block(at_band, WIDE)]
 
     def l_copy(n):
-        return remote(left_own, left_slot(band, q), l_send.at[n], l_recv.at[band * 4 + q], plane_user(n))
+        return remote(left_own, left_slot(band, q), l_send, l_recv, plane_user(n))
 
     def r1_copy():
-        return remote(right_own, right_all.at[zi, q], r1_send.at[0], r1_recv.at[0], partner)
+        return remote(right_own, right_all.at[zi, q], r1_send, r1_recv, partner)
 
     def r2_copy(n):
         return remote(
-            right_own, right_all.at[zi, q], r2_send.at[n], r2_recv.at[zi * 2 + xl], device(y, n, xh, xl, c)
+            right_own, right_all.at[zi, q], r2_send, r2_recv, device(y, n, xh, xl, c)
         )
 
     def r2_forward(n):
         return remote(
-            right_all.at[zi, other_q], right_all.at[zi, other_q], r2_send.at[8 + n], r2_recv.at[zi * 2 + 1 - xl],
+            right_all.at[zi, other_q], right_all.at[zi, other_q], r2_send, r2_recv,
             device(y, n, xh, xl, c),
         )
 
     def r3_copy(n):
         at_q = n * 2 + c
-        return remote(right_all.at[:, at_q], right_all.at[:, at_q], r3_send.at[n], r3_recv.at[n], other_core)
+        return remote(right_all.at[:, at_q], right_all.at[:, at_q], r3_send, r3_recv, other_core)
 
     for load in loads[:13]:
         load.wait()
@@ -292,15 +299,15 @@
 
             @pl.when(inside)
             def _():
-                local(mask_rows, row_masks.at[band, q], rm_recv.at[band * 4 + q]).start()
+                local(mask_rows, row_masks.at[band, q], rm_recv).start()
 
             @pl.when(jnp.logical_and(inside, xh == c))
             def _():
-                local(cot_stage.at[y], cot_all.at[band], cot_recv.at[band]).start()
+                local(cot_stage.at[y], cot_all.at[band], cot_recv).start()
 
             @pl.when(active)
             def _():
-                local(mask_rows, column_masks.at[zi, q], cm_recv.at[zi * 4 + q]).start()
+                local(mask_rows, column_masks.at[zi, q], cm_recv).start()
 
     right_own[...] = right_value.astype(BF16)
 
@@ -311,17 +318,17 @@
     @pl.when(active)
     def _():
         start_all(8, r2_copy, z)
-        local(right_own, right_all.at[zi, q], r2_recv.at[zi * 2 + xl]).start()
+        local(right_own, right_all.at[zi, q], r2_recv).start()
 
     start_all(16, l_copy, own_row)
 
     @pl.when(inside)
     def _():
-        local(left_own, left_slot(band, q), l_recv.at[band * 4 + q]).start()
+        local(left_own, left_slot(band, q), l_recv).start()
 
     @pl.when(active)
     def _():
-        wait(right_own, right_all.at[zi, other_q], r1_recv.at[0])
+        wait(right_own, right_all.at[zi, other_q], r1_recv)
         start_all(8, r2_forward, z)
 
     loads[13].wait()
@@ -334,11 +341,8 @@
     for t in range(8):
         weight_turned[:, t * 128 : (t + 1) * 128] = weight[t * 128 : (t + 1) * 128, :].astype(F32).T.astype(BF16)
 
-    def arrive_masks(n):
-        wait(mask_rows, row_masks.at[lax.div(n, 4), lax.rem(n, 4)], rm_recv.at[n])
-        wait(mask_rows, column_masks.at[lax.div(n, 4), lax.rem(n, 4)], cm_recv.at[n])
-
-    repeat(16, arrive_masks)
+    wait(row_masks, row_masks, rm_recv)
+    wait(column_masks, column_masks, cm_recv)
     column_mask = jnp.concatenate(
         [
             jnp.concatenate([column_masks[b, 2 * h] + column_masks[b, 2 * h + 1] for h in range(2)], axis=1)
@@ -356,7 +360,7 @@
         )
         product[i * 32 : (i + 1) * 32, :] = (row * column_mask).astype(BF16)
     counts[...] = dot(product[...], jnp.ones((256, 128), BF16))
-    repeat(4, lambda n: wait(cot_stage.at[n], cot_all.at[n], cot_recv.at[n]))
+    wait(cot_all, cot_all, cot_recv)
     for n in range(4):
         cot = cot_all[n].astype(F32).reshape(256, 128)
         scaled[n * 256 : (n + 1) * 256, :] = (cot / counts[n * 256 : (n + 1) * 256, :]).astype(BF16)
@@ -386,39 +390,39 @@
                 right_grad[b, at_q, :, t * 128 : (t + 1) * 128] = part.astype(BF16)
 
     def gx_copy(n):
-        return remote(right_grad.at[:, n * 2 + 1 - c], right_core.at[n], gx_send.at[n], gx_recv.at[n], other_core)
-
-    repeat(16, lambda n: wait(left_own, left_slot(lax.div(n, 4), lax.rem(n, 4)), l_recv.at[n]))
+        return remote(right_grad.at[:, n * 2 + 1 - c], right_core.at[n], gx_send, gx_recv, other_core)
+
+    wait(left_all, left_all, l_recv)
     right_step(0)
     right_step(1)
     start_all(2, gx_copy, -1)
 
-    forwarded = jnp.where(active, zi * 2 + 1 - xl, -1)
-
-    def arrive_right(n):
-        @pl.when(n != forwarded)
-        def _():
-            wait(right_own, right_all.at[lax.div(n, 2), lax.rem(n, 2) * 2 + c], r2_recv.at[n])
-
-    repeat(8, arrive_right)
+    @pl.when(active)
+    def _():
+        drain(r2_recv, gauge, 7)
+
+    @pl.when(jnp.logical_not(active))
+    def _():
+        drain(r2_recv, gauge, 8)
+
     start_all(2, r3_copy, -1)
     def gz_copy(n):
         return remote(
-            right_sum.at[n], right_in.at[z], gz_send.at[n], gz_recv.at[z], device(y, n * 2 + xl, xh, xl, c)
+            right_sum.at[n], right_in.at[z], gz_send, gz_recv, device(y, n * 2 + xl, xh, xl, c)
         )
 
     own_gz = jnp.where(active, zi, -1)
+    wait(right_core, right_core, gx_recv)
     for n in range(2):
-        wait(right_core.at[n], right_core.at[n], gx_recv.at[n])
         for b in range(4):
             right_sum[b, n] = (right_grad[b, n * 2 + c].astype(F32) + right_core[n, b].astype(F32)).astype(BF16)
     start_all(4, gz_copy, own_gz)
 
     @pl.when(active)
     def _():
-        local(right_sum.at[zi], right_in.at[z], gz_recv.at[z]).start()
-
-    repeat(2, lambda n: wait(right_all.at[:, n * 2 + 1 - c], right_all.at[:, n * 2 + 1 - c], r3_recv.at[n]))
+        local(right_sum.at[zi], right_in.at[z], gz_recv).start()
+
+    drain(r3_recv, gauge, 8)
     for at_q in range(4):
         rows = slice(at_q * ROWS, (at_q + 1) * ROWS)
         for t in range(2):
@@ -432,7 +436,7 @@
 
     def gl_copy(n):
         target = device(c * 2 + lax.div(n, 8), z, lax.rem(lax.div(n, 4), 2), lax.div(lax.rem(n, 4), 2), lax.rem(n, 2))
-        return remote(gl_part(n), left_in.at[plane], gl_send.at[n], gl_recv.at[plane], target)
+        return remote(gl_part(n), left_in.at[plane], gl_send, gl_recv, target)
 
     own_gl = jnp.where(inside, band * 4 + q, -1)
 
@@ -454,7 +458,7 @@
 
     @pl.when(inside)
     def _():
-        local(gl_part(band * 4 + q), left_in.at[plane], gl_recv.at[plane]).start()
+        local(gl_part(band * 4 + q), left_in.at[plane], gl_recv).start()
 
     def forward(g):
         lead = left_all[:, :, block(g, 256)].reshape(256, 256).astype(F32).T.astype(BF16)
@@ -489,16 +493,16 @@
         return weight_half.at[block(n, 32), :]
 
     def wa_copy(n):
-        return remote(wa_part(n), weight_in.at[plane], wa_send.at[n], wa_recv.at[plane], plane_peer(n))
+        return remote(wa_part(n), weight_in.at[plane], wa_send, wa_recv, plane_peer(n))
 
     def wb_copy(n):
-        return remote(weight_sum, weight_far.at[z], wb_send.at[n], wb_recv.at[z], line_peer(n))
+        return remote(weight_sum, weight_far.at[z], wb_send, wb_recv, line_peer(n))
 
     def wc_slot(n):
         return weight_all.at[c, block(n, 32), :]
 
     def wc_copy(n):
-        return remote(weight_total, wc_slot(plane), wc_send.at[n], wc_recv.at[plane], plane_peer(n))
+        return remote(weight_total, wc_slot(plane), wc_send, wc_recv, plane_peer(n))
 
     def wd_copy():
         return remote(weight_all.at[c], weight_all.at[c], wh_send.at[1], wh_recv.at[1], other_core)
@@ -508,14 +512,14 @@
     wait(weight_core, weight_core, wh_recv.at[0])
     weight_half[...] = (weight_grad[block(c, 512), :] + weight_core[...]).astype(BF16)
     start_all(16, wa_copy, plane)
-    local(wa_part(plane), weight_in.at[plane], wa_recv.at[plane]).start()
+    local(wa_part(plane), weight_in.at[plane], wa_recv).start()
 
     def pair_part(n):
         return pair.at[block(n, 8)]
 
     def pair_copy(n):
         target = device(c * 2 + lax.div(n, 2), z, lax.rem(n, 2), lax.div(y, 2), lax.rem(y, 2))
-        return remote(pair_part(n), pair_in.at[xh * 2 + xl], pair_send.at[n], pair_recv.at[xh * 2 + xl], target)
+        return remote(pair_part(n), pair_in.at[xh * 2 + xl], pair_send, pair_recv, target)
 
     keeps_pair = jnp.logical_and(inside, q == y)
     own_pair = jnp.where(keeps_pair, band, -1)
@@ -523,14 +527,14 @@
 
     @pl.when(keeps_pair)
     def _():
-        local(pair_part(band), pair_in.at[xh * 2 + xl], pair_recv.at[xh * 2 + xl]).start()
+        local(pair_part(band), pair_in.at[xh * 2 + xl], pair_recv).start()
 
     def gf_copy():
-        return remote(right_send, right_last, gf_send.at[0], gf_recv.at[0], partner)
+        return remote(right_send, right_last, gf_send, gf_recv, partner)
 
     @pl.when(active)
     def _():
-        repeat(8, lambda n: wait(right_in.at[n], right_in.at[n], gz_recv.at[n]))
+        wait(right_in, right_in, gz_recv)
         away = right_in[0, 1 - xl].astype(F32)
         for n in range(1, 8):
             away = away + right_in[n, 1 - xl].astype(F32)
@@ -541,19 +545,19 @@
             here = here + right_in[n, xl].astype(F32)
         right_last[...] = here.astype(BF16)
 
-    repeat(16, lambda n: wait(left_in.at[n], left_in.at[n], gl_recv.at[n]))
+    wait(left_in, left_in, gl_recv)
     left_total = total(left_in, 16).astype(BF16).astype(F32)
 
     @pl.when(jnp.logical_not(active))
     def _():
-        wait(right_last, right_last, gf_recv.at[0])
+        wait(right_last, right_last, gf_recv)
 
     right_total = right_last[...].astype(F32)
 
-    repeat(16, lambda n: wait(weight_in.at[n], weight_in.at[n], wa_recv.at[n]))
+    wait(weight_in, weight_in, wa_recv)
     weight_sum[...] = total(weight_in, 16).astype(BF16)
     start_all(8, wb_copy, z)
-    local(weight_sum, weight_far.at[z], wb_recv.at[z]).start()
+    local(weight_sum, weight_far.at[z], wb_recv).start()
 
     sums = jnp.zeros((32, WIDE), F32)
     for h in range(2):
@@ -587,36 +591,28 @@
         return remote(table_part.at[pl.ds((1 - c) * 3, 3)], table_core, t_send.at[0], t_recv.at[0], other_core)
 
     def tp_copy(n):
-        return remote(table_p.at[plane], table_p.at[plane], tp_send.at[n], tp_recv.at[plane], plane_peer(n))
+        return remote(table_p.at[plane], table_p.at[plane], tp_send, tp_recv, plane_peer(n))
 
     def tz_copy(n):
-        return remote(table_z.at[z], table_z.at[z], tz_send.at[n], tz_recv.at[z], device(y, n, xh, xl, c))
+        return remote(table_z.at[z], table_z.at[z], tz_send, tz_recv, device(y, n, xh, xl, c))
 
     def half(at_c):
         return table_all.at[pl.ds(at_c * 3, 3)]
 
     def t_last():
         return remote(table_half, half(c), t_send.at[1], t_recv.at[1], other_core)
-
-    def arrive(count, ref, sem, own):
-        def step(n):
-            @pl.when(n != own)
-            def _():
-                wait(ref.at[n], ref.at[n], sem.at[n])
-
-        repeat(count, step)
 
     t_copy().start()
     wait(table_core, table_core, t_recv.at[0])
     table_p[plane] = table_part[pl.ds(c * 3, 3)] + table_core[...]
     start_all(16, tp_copy, plane)
 
-    repeat(8, lambda n: wait(weight_far.at[n], weight_far.at[n], wb_recv.at[n]))
+    wait(weight_far, weight_far, wb_recv)
     weight_total[...] = total(weight_far, 8).astype(BF16)
     start_all(16, wc_copy, plane)
-    local(weight_total, wc_slot(plane), wc_recv.at[plane]).start()
-
-    repeat(4, lambda n: wait(pair_part(n), pair_in.at[n], pair_recv.at[n]))
+    local(weight_total, wc_slot(plane), wc_recv).start()
+
+    wait(pair_in, pair_in, pair_recv)
     for at_z in range(8):
         run = [
             pair_in[at_x * 2 + at_z % 2, :, (at_z // 2) * 8 : (at_z // 2 + 1) * 8, :].astype(F32) for at_x in range(2)
@@ -624,7 +620,7 @@
         pair_out[:, at_z * 16 : (at_z + 1) * 16, :] = jnp.concatenate(run, axis=1).astype(BF16)
     local(pair_out, pair_h, out_sem.at[0]).start()
 
-    arrive(16, table_p, tp_recv, plane)
+    drain(tp_recv, gauge_t, 15)
     table_z[z] = total(table_p, 16)
     start_all(8, tz_copy, z)
 
@@ -633,27 +629,26 @@
             first = at_c * 16 + n % 4 * 4 + n // 4
             weight_out[pl.ds(first, 32, stride=32), :] = weight_all[at_c, n * 32 : (n + 1) * 32, :].astype(F32)
 
-    repeat(16, lambda n: wait(weight_total, wc_slot(n), wc_recv.at[n]))
+    wait(weight_all.at[c], weight_all.at[c], wc_recv)
     wd_copy().start()
 
-    sent_all(16, rm_copy, own_row)
-    sent_all(16, cm_copy, own_column)
-    sent_all(4, cot_copy, own_cot)
-    sent_all(16, l_copy, own_row)
-    sent_all(2, r3_copy, -1)
-    sent_all(2, gx_copy, -1)
-    sent_all(4, gz_copy, own_gz)
-    sent_all(16, gl_copy, own_gl)
-    sent_all(16, wa_copy, plane)
-    sent_all(8, wb_copy, z)
-    sent_all(4, pair_copy, own_pair)
+    sent(rm_send, gauge_m, 16, own_row)
+    sent(cm_send, gauge_m, 16, own_column)
+    sent(cot_send, gauge, 8, own_cot, 2)
+    sent(l_send, gauge, 16, own_row)
+    drain(r3_send, gauge, 8)
+    drain(gx_send, gauge, 8)
+    sent(gz_send, gauge, 8, own_gz, 2)
+    sent(gl_send, gauge, 16, own_gl)
+    drain(wa_send, gauge_w, 15)
+    drain(wb_send, gauge_w, 7)
+    sent(pair_send, gauge, 8, own_pair, 2)
     wh_copy().wait_send()
     t_copy().wait_send()
 
     @pl.when(active)
     def _():
-        sent_all(8, r2_copy, z)
-        sent_all(8, r2_forward, z)
+        drain(r2_send, gauge, 14)
         gf_copy().wait_send()
 
     @pl.when(jnp.logical_not(active))
@@ -664,16 +659,16 @@
     for at_c in range(2):
         lay_out(at_c)
     local(weight_out, weight_grad_h, out_sem.at[1]).start()
-    sent_all(16, wc_copy, plane)
-    sent_all(16, tp_copy, plane)
+    drain(wc_send, gauge_w, 15)
+    drain(tp_send, gauge_t, 15)
     wd_copy().wait_send()
 
-    arrive(8, table_z, tz_recv, z)
+    drain(tz_recv, gauge_t, 7)
     summed = total(table_z, 8)
     table_half[...] = summed
     t_last().start()
     table_all[pl.ds(c * 3, 3)] = summed
-    sent_all(8, tz_copy, z)
+    drain(tz_send, gauge_t, 7)
     wait(table_half, half(1 - c), t_recv.at[1])
     for n in range(TILES):
         high = min(8, table_out.shape[0] - (n // 2) * 8)
@@ -734,15 +729,19 @@
         vmem((16, 3, 8, 128), F32), vmem((8, 3, 8, 128), F32),
         vmem((3, 8, 128), F32), vmem((TILES, 8, 128), F32),
         vmem((8, 128, 128), BF16), vmem((1024, 128), F32),
+        vmem((16, ROWS, WIDE), BF16), vmem((16, 8, 128), F32),
+        vmem((16, 32, 128), BF16), vmem((16, 3, 8, 128), F32),
     ]
-    sizes = [len(inputs) + 1, 2, 16, 16, 16, 16, 4, 4, 1, 1, 16, 8, 2, 2, 16, 16]
-    sizes += [2, 2, 4, 8, 1, 1, 16, 16, 4, 4, 2, 2, 16, 16, 8, 8, 16, 16, 2, 2, 16, 16, 8, 8]
+    sizes = [
+        len(inputs) + 1, 2, 0, 0, 0, 0, 0, 0, 0, 0, 0, 0, 0, 0, 0, 0, 0, 0, 0, 0, 0, 0, 0, 0, 0, 0, 2, 2, 0,
+        0, 0, 0, 0, 0, 2, 2, 0, 0, 0, 0,
+    ]
     results = pl.pallas_call(
         kernel,
         out_shape=[shape((8, 128, 128)), shape((1024, 128), F32), shape((kinds, 256), F32)],
         in_specs=[pl.BlockSpec(memory_space=pl.ANY)] * (len(inputs) + 1),
         out_specs=[pl.BlockSpec(memory_space=pl.ANY)] * 2 + [pl.BlockSpec(memory_space=pltpu.VMEM)],
-        scratch_shapes=scratch + [pltpu.SemaphoreType.DMA((size,)) for size in sizes],
+        scratch_shapes=scratch + [pltpu.SemaphoreType.DMA((size,)) if size else pltpu.SemaphoreType.DMA for size in sizes],
         compiler_params=pltpu.CompilerParams(
             collective_id=0, has_side_effects=True, vmem_limit_bytes=60 * 1024 * 1024
         ),

time: 62.7 us -> 59.9 us (0.955)
  Pallas kernels: 62 us -> 59.1 us
    pallas_call x1, Pallas kernels: 60 us -> 57.2 us  [body(): pl.pallas_call(kernel, out_shape=[shape((8, 128, 128)), shape((1024, 128)...]
where the time goes in v6:
time: 59.9 us; the launch traced here: 59.8 us
  Pallas kernels  59.1 us (99%)
  between operations  0.64 us (1%)
    pallas_call x1, Pallas kernels, body(): pl.pallas_call(kernel, out_shape=[shape((8, 128, 128)), shape((1024, 128)...  57.2 us
    pallas_call x1, Pallas kernels, body(): pl.pallas_call(hand_over, out_shape=[shape(value.shape, value.dtype) for...  1.94 us

profile of v6, /device:TPU:1, one launch (start us, length us, event | category | flops | bytes accessed | tf_op | source)
XLA Modules:
  0.0 59.8 jit_solution(11893694153049638244)
XLA Ops:
  0.6 57.2 %outer_product_mean.1 = (bf16[8,128,128]{2,1,0:T(8,128)(2,1)}, f32[1024,128]{1,0:T(8,128)}, f32[23,256]{1,0:T(8,128)}) custom-call(s32[8,64]{1,0:T(8,128)} %bitcast.13, s32[8,64]{1,0:T(8,128)} %bitcast.14, s32[8,64]{1,0:T(8,128)} %bitcast.15, bf16[64,8,256]{2,1,0:T(8,128)(2,1)} %stack_h.1, f32[23,256]{1,0:T(8,128)} %letters_h.1, f32[2,256]{1,0:T(2,128)} %gaps_h.1, ...), custom_call_target="tpu_custom_call" | custom-call | tf_op jit(solution)/shard_map/outer_product_mean/pallas_call | solution.py:739
  57.8 1.9 %hand_over.1 = (bf16[8,128,128]{2,1,0:T(8,128)(2,1)}, f32[1024,128]{1,0:T(8,128)}, f32[23,256]{1,0:T(8,128)}) custom-call(bf16[8,128,128]{2,1,0:T(8,128)(2,1)} %get-tuple-element.6.pair, f32[1024,128]{1,0:T(8,128)} %get-tuple-element.7.weight, f32[23,256]{1,0:T(8,128)} %get-tuple-element.8.table), custom_call_target="tpu_custom_call" | custom-call | tf_op jit(solution)/shard_map/hand_over/pallas_call | solution.py:750

commit v7 on v6

--- a/solution.py
+++ b/solution.py
@@ -33,12 +33,11 @@
 
 
 def start_all(count, copy, own):
-    def step(n):
-        @pl.when(n != own)
-        def _():
+    for n in range(count):
+
+        @pl.when(own != n)
+        def _(n=n):
             copy(n).start()
-
-    repeat(count, step)
 
 
 def local(src, dst, sem):
@@ -175,7 +174,8 @@
         def _():
             signal((lax.div(n, 8) * 16 + z * 2 + lax.rem(lax.div(n, 4), 2), lax.rem(n, 4)))
 
-    repeat(32, greet)
+    for n in range(32):
+        greet(n)
 
     def line_user(n):
         return device(y, lax.div(n, 2), xh, parity, lax.rem(n, 2))
@@ -291,40 +291,39 @@
             left_value = jnp.where(lax.div(lane, 32) == i, part[:, :128], left_value)
             right_value = jnp.where(lax.rem(wide_lane, 8) == h * 4 + i, part[:, 128:], right_value)
         left_own[:, h * 128 : (h + 1) * 128] = left_value.astype(BF16)
-        if h == 0:
-            pl.semaphore_wait(barrier, 62)
-            start_all(4, cot_copy, own_cot)
-            start_all(16, rm_copy, own_row)
-            start_all(16, cm_copy, own_column)
-
-            @pl.when(inside)
-            def _():
-                local(mask_rows, row_masks.at[band, q], rm_recv).start()
-
-            @pl.when(jnp.logical_and(inside, xh == c))
-            def _():
-                local(cot_stage.at[y], cot_all.at[band], cot_recv).start()
-
-            @pl.when(active)
-            def _():
-                local(mask_rows, column_masks.at[zi, q], cm_recv).start()
-
     right_own[...] = right_value.astype(BF16)
-
+    pl.semaphore_wait(barrier, 62)
     @pl.when(jnp.logical_not(active))
     def _():
         r1_copy().start()
+
+    start_all(16, rm_copy, own_row)
+    start_all(16, cm_copy, own_column)
+
+    @pl.when(inside)
+    def _():
+        local(mask_rows, row_masks.at[band, q], rm_recv).start()
+
+    @pl.when(active)
+    def _():
+        local(mask_rows, column_masks.at[zi, q], cm_recv).start()
+
+    start_all(4, cot_copy, own_cot)
+
+    @pl.when(jnp.logical_and(inside, xh == c))
+    def _():
+        local(cot_stage.at[y], cot_all.at[band], cot_recv).start()
+
+    start_all(16, l_copy, own_row)
+
+    @pl.when(inside)
+    def _():
+        local(left_own, left_slot(band, q), l_recv).start()
 
     @pl.when(active)
     def _():
         start_all(8, r2_copy, z)
         local(right_own, right_all.at[zi, q], r2_recv).start()
-
-    start_all(16, l_copy, own_row)
-
-    @pl.when(inside)
-    def _():
-        local(left_own, left_slot(band, q), l_recv).start()
 
     @pl.when(active)
     def _():

time: 59.9 us -> 58.5 us (0.977)
  Pallas kernels: 59.1 us -> 57.7 us
    pallas_call x1, Pallas kernels: 57.2 us -> 55.8 us  [body(): pl.pallas_call(kernel, out_shape=[shape((8, 128, 128)), shape((1024, 128)...]
where the time goes in v7:
time: 58.5 us; the launch traced here: 58.4 us
  Pallas kernels  57.7 us (99%)
  between operations  0.64 us (1%)
    pallas_call x1, Pallas kernels, body(): pl.pallas_call(kernel, out_shape=[shape((8, 128, 128)), shape((1024, 128)...  55.8 us
    pallas_call x1, Pallas kernels, body(): pl.pallas_call(hand_over, out_shape=[shape(value.shape, value.dtype) for...  1.94 us

profile of v7, /device:TPU:1, one launch (start us, length us, event | category | flops | bytes accessed | tf_op | source)
XLA Modules:
  0.0 58.4 jit_solution(4040458254333185741)
XLA Ops:
  0.6 55.8 %outer_product_mean.1 = (bf16[8,128,128]{2,1,0:T(8,128)(2,1)}, f32[1024,128]{1,0:T(8,128)}, f32[23,256]{1,0:T(8,128)}) custom-call(s32[8,64]{1,0:T(8,128)} %bitcast.13, s32[8,64]{1,0:T(8,128)} %bitcast.14, s32[8,64]{1,0:T(8,128)} %bitcast.15, bf16[64,8,256]{2,1,0:T(8,128)(2,1)} %stack_h.1, f32[23,256]{1,0:T(8,128)} %letters_h.1, f32[2,256]{1,0:T(2,128)} %gaps_h.1, ...), custom_call_target="tpu_custom_call" | custom-call | tf_op jit(solution)/shard_map/outer_product_mean/pallas_call | solution.py:738
  56.4 1.9 %hand_over.1 = (bf16[8,128,128]{2,1,0:T(8,128)(2,1)}, f32[1024,128]{1,0:T(8,128)}, f32[23,256]{1,0:T(8,128)}) custom-call(bf16[8,128,128]{2,1,0:T(8,128)(2,1)} %get-tuple-element.6.pair, f32[1024,128]{1,0:T(8,128)} %get-tuple-element.7.weight, f32[23,256]{1,0:T(8,128)} %get-tuple-element.8.table), custom_call_target="tpu_custom_call" | custom-call | tf_op jit(solution)/shard_map/hand_over/pallas_call | solution.py:749

commit v8 on v7

--- a/solution.py
+++ b/solution.py
@@ -231,7 +231,7 @@
     square[16:24, 0:ROWS] = mask_value
     turned[...] = square[...].T[:ROWS]
     for n in range(2):
-        stack[n] = stack_raw[:, :, n * 128 : (n + 1) * 128].astype(F32).reshape(512, 128)
+        stack[n] = stack_raw[:, n * 128 : (n + 1) * 128].astype(F32)
     table[...] = jnp.zeros((128, WIDE), F32)
     table[: letters.shape[0], :] = letters[...]
     table[32:64, :] = steps[:, 0:1] * gaps[0:1, :] + steps[:, 1:2] * gaps[1:2, :]
@@ -614,7 +614,7 @@
     wait(pair_in, pair_in, pair_recv)
     for at_z in range(8):
         run = [
-            pair_in[at_x * 2 + at_z % 2, :, (at_z // 2) * 8 : (at_z // 2 + 1) * 8, :].astype(F32) for at_x in range(2)
+            pair_in[at_x * 2 + at_z % 2].astype(F32)[:, (at_z // 2) * 8 : (at_z // 2 + 1) * 8, :] for at_x in range(2)
         ]
         pair_out[:, at_z * 16 : (at_z + 1) * 16, :] = jnp.concatenate(run, axis=1).astype(BF16)
     local(pair_out, pair_h, out_sem.at[0]).start()
@@ -693,7 +693,7 @@
         np.stack([(grades > 0).astype(np.float32), (2.0 / math.pi * np.arctan(grades / 3.0)).astype(np.float32)], 1)
     )
     inputs = [
-        alignment_token_classes.T, deletions.T, alignment_mask.T, homolog_stack_values,
+        alignment_token_classes.T, deletions.T, alignment_mask.T, homolog_stack_values.reshape(512, 256),
         letter_lookup_coefficients, gap_lookup_coefficients, steps,
         standardize_gain.reshape(1, 256), standardize_offset.reshape(1, 256),
         first_factor_map.T, left_bias_vector.reshape(1, 32), second_factor_map.T, right_bias_vector.reshape(1, 32),

time: 58.5 us -> 58.5 us (level)
  no operation moved by 1% of the time
where the time goes in v8:
time: 58.5 us; the launch traced here: 58.4 us
  Pallas kernels  57.7 us (99%)
  between operations  0.64 us (1%)
    pallas_call x1, Pallas kernels, body(): pl.pallas_call(kernel, out_shape=[shape((8, 128, 128)), shape((1024, 128)...  55.8 us
    pallas_call x1, Pallas kernels, body(): pl.pallas_call(hand_over, out_shape=[shape(value.shape, value.dtype) for...  1.94 us

profile of v8, /device:TPU:1, one launch (start us, length us, event | category | flops | bytes accessed | tf_op | source)
XLA Modules:
  0.0 58.4 jit_solution(5212415391008867614)
XLA Ops:
  0.6 55.8 %outer_product_mean.1 = (bf16[8,128,128]{2,1,0:T(8,128)(2,1)}, f32[1024,128]{1,0:T(8,128)}, f32[23,256]{1,0:T(8,128)}) custom-call(s32[8,64]{1,0:T(8,128)} %bitcast.15, s32[8,64]{1,0:T(8,128)} %bitcast.16, s32[8,64]{1,0:T(8,128)} %bitcast.17, bf16[512,256]{1,0:T(8,128)(2,1)} %bitcast.12, f32[23,256]{1,0:T(8,128)} %letters_h.1, f32[2,256]{1,0:T(2,128)} %gaps_h.1, ...), custom_call_target="tpu_custom_call" | custom-call | tf_op jit(solution)/shard_map/outer_product_mean/pallas_call | solution.py:738
  56.4 1.9 %hand_over.1 = (bf16[8,128,128]{2,1,0:T(8,128)(2,1)}, f32[1024,128]{1,0:T(8,128)}, f32[23,256]{1,0:T(8,128)}) custom-call(bf16[8,128,128]{2,1,0:T(8,128)(2,1)} %get-tuple-element.6.pair, f32[1024,128]{1,0:T(8,128)} %get-tuple-element.7.weight, f32[23,256]{1,0:T(8,128)} %get-tuple-element.8.table), custom_call_target="tpu_custom_call" | custom-call | tf_op jit(solution)/shard_map/hand_over/pallas_call | solution.py:749

commit v9 on v8

--- a/solution.py
+++ b/solution.py
@@ -369,7 +369,7 @@
         wide_grad[...] = dot_nt(weight[...], scaled[span, :])
         for t in range(8):
             for half in range(2):
-                lane_part = wide_grad[t * 128 : (t + 1) * 128, half * 128 : (half + 1) * 128]
+                lane_part = wide_grad[t * 128 : (t + 1) * 128, half * 128 : (half + 1) * 128].astype(BF16)
                 parts = swap([lane_part[a * 32 : (a + 1) * 32, :] for a in range(4)], 32)
                 for i, part in enumerate(parts):
                     at = pl.ds(pl.multiple_of(g * 256 + half * 128 + i * 32, 32), 32)
@@ -378,13 +378,9 @@
     repeat(4, backward)
 
     def right_step(t):
-        for b in range(2):
-            right_part[:, b * 256 : (b + 1) * 256] = dot(
-                left_all[...].reshape(256, 1024), grad_outer[:, t * 512 + b * 256 : t * 512 + (b + 1) * 256]
-            )
         for at_q in range(4):
             rows = slice(at_q * ROWS, (at_q + 1) * ROWS)
-            parts = swap([right_part[rows, b * 128 : (b + 1) * 128] for b in range(4)], 8)
+            parts = swap([right_part[rows, (t * 4 + b) * 128 : (t * 4 + b + 1) * 128] for b in range(4)], 8)
             for b, part in enumerate(parts):
                 right_grad[b, at_q, :, t * 128 : (t + 1) * 128] = part.astype(BF16)
 
@@ -392,6 +388,7 @@
         return remote(right_grad.at[:, n * 2 + 1 - c], right_core.at[n], gx_send, gx_recv, other_core)
 
     wait(left_all, left_all, l_recv)
+    right_part[...] = dot(left_all[...].reshape(256, 1024), grad_outer[...])
     right_step(0)
     right_step(1)
     start_all(2, gx_copy, -1)
@@ -465,7 +462,7 @@
         for half in range(2):
             span = pl.ds(pl.multiple_of(g * 256 + half * 128, 128), 128)
             for t in range(8):
-                tile = wide_outer[half * 128 : (half + 1) * 128, t * 128 : (t + 1) * 128]
+                tile = wide_outer[half * 128 : (half + 1) * 128, t * 128 : (t + 1) * 128].astype(BF16)
                 parts = swap([tile[i * 32 : (i + 1) * 32, :] for i in range(4)], 32)
                 for a, part in enumerate(parts):
                     folded[(t * 4 + a) * 32 : (t * 4 + a + 1) * 32, span] = part.astype(BF16)
@@ -717,7 +714,7 @@
         vmem((1024, 128), F32), vmem((1024, 128), BF16),
         vmem((1024, 1024), BF16), vmem((1024, 1024), BF16),
         vmem((32, 32, 128), BF16), vmem((4, 8, 32, 128), BF16),
-        vmem((4, 4, ROWS, WIDE), BF16), vmem((256, 512), F32), vmem((2, 4, ROWS, WIDE), BF16),
+        vmem((4, 4, ROWS, WIDE), BF16), vmem((256, 1024), F32), vmem((2, 4, ROWS, WIDE), BF16),
         vmem((4, 2, ROWS, WIDE), BF16), vmem((8, 2, ROWS, WIDE), BF16),
         vmem((ROWS, WIDE), BF16), vmem((ROWS, WIDE), BF16),
         vmem((4, ROWS, 1024), BF16), vmem((16, ROWS, WIDE), BF16),

time: 58.5 us -> 58.4 us (level)
  no operation moved by 1% of the time
where the time goes in v9:
time: 58.4 us; the launch traced here: 58.3 us
  Pallas kernels  57.7 us (99%)
  between operations  0.64 us (1%)
    pallas_call x1, Pallas kernels, body(): pl.pallas_call(kernel, out_shape=[shape((8, 128, 128)), shape((1024, 128)...  55.7 us
    pallas_call x1, Pallas kernels, body(): pl.pallas_call(hand_over, out_shape=[shape(value.shape, value.dtype) for...  1.94 us

profile of v9, /device:TPU:1, one launch (start us, length us, event | category | flops | bytes accessed | tf_op | source)
XLA Modules:
  0.0 58.3 jit_solution(16388745177486930585)
XLA Ops:
  0.6 55.7 %outer_product_mean.1 = (bf16[8,128,128]{2,1,0:T(8,128)(2,1)}, f32[1024,128]{1,0:T(8,128)}, f32[23,256]{1,0:T(8,128)}) custom-call(s32[8,64]{1,0:T(8,128)} %bitcast.15, s32[8,64]{1,0:T(8,128)} %bitcast.16, s32[8,64]{1,0:T(8,128)} %bitcast.17, bf16[512,256]{1,0:T(8,128)(2,1)} %bitcast.12, f32[23,256]{1,0:T(8,128)} %letters_h.1, f32[2,256]{1,0:T(2,128)} %gaps_h.1, ...), custom_call_target="tpu_custom_call" | custom-call | tf_op jit(solution)/shard_map/outer_product_mean/pallas_call | solution.py:735
  56.4 1.9 %hand_over.1 = (bf16[8,128,128]{2,1,0:T(8,128)(2,1)}, f32[1024,128]{1,0:T(8,128)}, f32[23,256]{1,0:T(8,128)}) custom-call(bf16[8,128,128]{2,1,0:T(8,128)(2,1)} %get-tuple-element.6.pair, f32[1024,128]{1,0:T(8,128)} %get-tuple-element.7.weight, f32[23,256]{1,0:T(8,128)} %get-tuple-element.8.table), custom_call_target="tpu_custom_call" | custom-call | tf_op jit(solution)/shard_map/hand_over/pallas_call | solution.py:746
